TPU v7x, 32 devices: a whole 2x2x4 slice. The times are simulated.
32 devices in a mesh: tm: 4 (over x, core), dom: 8 (over z, y).
Axes of the slice: x: 2, y: 2, z: 4, core: 2. Of those that a mesh axis runs over, the one named last changes fastest.
Arguments:
- features: bfloat16 [8, 4096, 128], P('tm', 'dom'), may hold values from -6 to 6
- tile_values: bfloat16 [8, 32, 8, 4, 128, 128], P('tm', 'dom'), may hold values from -0.125 to 0.125
- tile_cols: int32 [8, 32, 8, 4], P('tm', 'dom'), may hold values from 0 to 3
- tile_count: int32 [8, 32, 8], P('tm', 'dom'), may hold values from 0 to 4, as said below
- hidden_start: float32 [4096, 512], P('dom'), may hold values from -4 to 4
- w_graph: bfloat16 [128, 512], replicated, may hold values from -0.5 to 0.5
- w_input: bfloat16 [512, 1536], replicated, may hold values from -0.25 to 0.25
- w_hidden: bfloat16 [512, 1536], replicated, may hold values from -0.25 to 0.25
- update_bias: float32 [512], replicated, may hold values from -1 to 4
Outputs:
- hidden_seq: bfloat16 [8, 4096, 512], P('tm', 'dom')
Inputs may be any that keep to these rules, and one draw needn't show every extreme that they name: `tile_count`: number of live slots; for each row block the entry of its own partition is 4.
All inputs are finite; a program needn't handle non-finite values.
Results may differ from a plain program's by a relative error of at most 0.0052.
Values may be sent and summed in bfloat16 or wider, within the bound.
No kernel may reach another device: no remote copies, remote signals or barrier semaphores. Data moves between devices by JAX's collectives and lax.ppermute only.
A program may use at most 128 MiB of HBM per device.

v0:
```python
import jax
import jax.numpy as jnp
from jax import lax
from jax.sharding import PartitionSpec as P


def gru_cell(state, gx, w_hidden, update_bias, hid):
    gh = jnp.dot(state.astype(jnp.bfloat16), w_hidden, preferred_element_type=jnp.float32)
    reset = jax.nn.sigmoid(gx[:, :hid] + gh[:, :hid])
    update = jax.nn.sigmoid(gx[:, hid : 2 * hid] + gh[:, hid : 2 * hid] + update_bias)
    cand = jnp.tanh(gx[:, 2 * hid :] + reset * gh[:, 2 * hid :])
    return update * state + (1.0 - update) * cand


def per_device(
    features,
    tile_values,
    tile_cols,
    tile_count,
    hidden_start,
    w_graph,
    w_input,
    w_hidden,
    update_bias,
):
    snaps, nodes, feats = features.shape
    hid = w_graph.shape[1]
    blk = tile_values.shape[-1]
    slot_count = tile_cols.shape[-1]
    nblocks = nodes // blk
    parts = lax.axis_size("dom")
    projected = jnp.einsum(
        "snf,fh->snh", features, w_graph, preferred_element_type=jnp.float32
    ).astype(jnp.bfloat16)
    live = jnp.arange(slot_count, dtype=jnp.int32)[None, None, None, :] < tile_count[..., None]
    masked = tile_values * live[..., None, None].astype(jnp.bfloat16)
    whole = lax.all_gather(projected, "dom", axis=1, tiled=True)
    all_blocks = whole.reshape(snaps, parts * nblocks, blk, hid)
    offsets = (jnp.arange(parts, dtype=jnp.int32) * nblocks)[None, None, :, None]
    global_cols = tile_cols + offsets

    def one_snapshot(args):
        block_set, col_set, tile_set = args
        picked = block_set[col_set]
        return jnp.einsum("npkij,npkjh->nih", tile_set, picked, preferred_element_type=jnp.float32)

    propagated = lax.map(one_snapshot, (all_blocks, global_cols, masked)).reshape(snaps, nodes, hid)
    graph_out = jax.nn.relu(propagated).astype(jnp.bfloat16)
    sections = lax.axis_size("tm")
    me_time = lax.axis_index("tm")
    mine = lax.all_to_all(graph_out, "tm", split_axis=1, concat_axis=0, tiled=True)
    share = nodes // sections
    start_rows = lax.dynamic_slice_in_dim(hidden_start, me_time * share, share, 0)

    def scan_cell(state, graph_row):
        gx = jnp.dot(graph_row, w_input, preferred_element_type=jnp.float32)
        state = gru_cell(state, gx, w_hidden, update_bias, hid)
        return (state, state.astype(jnp.bfloat16))

    last_state, own_seq = lax.scan(scan_cell, start_rows, mine)
    hidden_seq = lax.all_to_all(own_seq, "tm", split_axis=0, concat_axis=1, tiled=True)
    return hidden_seq


def solution(mesh):
    placed = (
        P("tm", "dom", None),
        P("tm", "dom", None, None, None, None),
        P("tm", "dom", None, None),
        P("tm", "dom", None),
        P("dom", None),
        P(),
        P(),
        P(),
        P(),
    )
    return jax.shard_map(
        per_device, mesh=mesh, in_specs=placed, out_specs=P("tm", "dom", None), check_vma=False
    )
```

profile of v0, /device:TPU:0, one launch (start us, length us, event | category | flops | bytes accessed | tf_op | source)
XLA Modules:
  0.0 264.1 jit_solution(17324912294171437866)
XLA Ops:
  6.5 2.5 convolution_convert_fusion
  10.5 7.2 %copy_multiply_fusion = bf16[2,4,8,4,128,128]{5,4,2,1,3,0:T(8,128)(2,1)} fusion(bf16[2,4,8,4,128,128]{5,4,3,2,1,0:T(8,128)(2,1)} %param.14, bf16[2,4,8,4]{2,1,3,0:T(4,128)(2,1)S(1)} %fusion.35), kind=kLoop, calls=%fused_computation.34 | loop fusion | flops 4194304 | bytes 16777728 | tf_op jit(solution)/shard_map/mul | solution.py:36
  17.7 119.5 %all-gather.2.cloned.1.call-done = bf16[2,4096,512]{2,1,0:T(8,128)(2,1)} async-done(((bf16[2,512,512]{2,1,0:T(8,128)(2,1)}), bf16[2,4096,512]{2,1,0:T(8,128)(2,1)}) %all-gather.2.cloned.1.call-update) | async-done | bytes 8388624 | tf_op jit(solution)/shard_map/all_gather | solution.py:37
  137.2 50.9 %while.24 = (s32[]{:T(128)}, bf16[2,4,128,512]{3,2,1,0:T(8,128)(2,1)}, bf16[2,4,8,4,128,128]{5,4,2,1,3,0:T(8,128)(2,1)}, bf16[2,32,128,512]{3,2,1,0:T(8,128)(2,1)}, s32[2,4,8,4]{2,3,1,0:T(4,128)S(1)}) while((s32[]{:T(128)}, bf16[2,4,128,512]{3,2,1,0:T(8,128)(2,1)}, bf16[2,4,8,4,128,128]{5,4,2,1,3,0:T(8,128)(2,1)}, ...), condition=%wide.region_1.2_spmd.clone, body=%wide.region_0.1_spmd.sunk.clone | while | flops 2147485184 | bytes 63972420 | solution.py:47
  137.2 4.7 %dynamic-slice_bitcast_fusion.3 = bf16[32,128,512]{2,1,0:T(8,128)(2,1)} fusion(bf16[2,32,128,512]{3,2,1,0:T(8,128)(2,1)} %get-tuple-element.218, s32[]{:T(128)} %get-tuple-element.210), kind=kLoop, calls=%fused_computation.27.clone.1.clone | loop fusion | bytes 8388612 | tf_op jit(solution)/shard_map/while/body/jit(dynamic_index_in_dim)/squeeze | solution.py:47
  142.1 10.4 %gather_fusion = bf16[128,128,512]{2,1,0:T(8,128)(2,1)} fusion(bf16[32,128,512]{2,1,0:T(8,128)(2,1)} %dynamic-slice_bitcast_fusion.3, s32[1024]{0:T(1024)S(1)} %pad_clamp_fusion.3), kind=kCustom, calls=%fused_computation.clone.1.clone | custom fusion | bytes 33554944 | tf_op jit(solution)/shard_map/while/body/eval_jaxpr/gather | solution.py:44
  152.5 10.2 %fusion.60 = bf16[2,4,128,512]{3,2,1,0:T(8,128)(2,1)} fusion(bf16[2,4,128,512]{3,2,1,0:T(8,128)(2,1)} %get-tuple-element.211, s32[]{:T(128)} %get-tuple-element.210, bf16[4,8,4,128,512]{4,3,2,1,0:T(8,128)(2,1)} %bitcast.72, bf16[2,4,8,4,128,128]{5,4,2,1,3,0:T(8,128)(2,1)} %get-tuple-element.217), kind=kOutput, calls=%fused_computation.30.clone.1.clone | convolution fusion | flops 2147483648 | bytes 22021120 | tf_op jit(solution)/shard_map/while/body/eval_jaxpr/npkij,npkjh->nih/dot_general | solution.py:45
  162.7 4.7 %dynamic-slice_bitcast_fusion.3 = bf16[32,128,512]{2,1,0:T(8,128)(2,1)} fusion(bf16[2,32,128,512]{3,2,1,0:T(8,128)(2,1)} %get-tuple-element.218, s32[]{:T(128)} %get-tuple-element.210), kind=kLoop, calls=%fused_computation.27.clone.1.clone | loop fusion | bytes 8388612 | tf_op jit(solution)/shard_map/while/body/jit(dynamic_index_in_dim)/squeeze | solution.py:47
  167.6 10.4 %gather_fusion = bf16[128,128,512]{2,1,0:T(8,128)(2,1)} fusion(bf16[32,128,512]{2,1,0:T(8,128)(2,1)} %dynamic-slice_bitcast_fusion.3, s32[1024]{0:T(1024)S(1)} %pad_clamp_fusion.3), kind=kCustom, calls=%fused_computation.clone.1.clone | custom fusion | bytes 33554944 | tf_op jit(solution)/shard_map/while/body/eval_jaxpr/gather | solution.py:44
  177.9 10.2 %fusion.60 = bf16[2,4,128,512]{3,2,1,0:T(8,128)(2,1)} fusion(bf16[2,4,128,512]{3,2,1,0:T(8,128)(2,1)} %get-tuple-element.211, s32[]{:T(128)} %get-tuple-element.210, bf16[4,8,4,128,512]{4,3,2,1,0:T(8,128)(2,1)} %bitcast.72, bf16[2,4,8,4,128,128]{5,4,2,1,3,0:T(8,128)(2,1)} %get-tuple-element.217), kind=kOutput, calls=%fused_computation.30.clone.1.clone | convolution fusion | flops 2147483648 | bytes 22021120 | tf_op jit(solution)/shard_map/while/body/eval_jaxpr/npkij,npkjh->nih/dot_general | solution.py:45
  188.1 1.5 maximum_convert_fusion
  189.7 2.1 copy.25
  191.8 4.3 %all-to-all-start = ((bf16[2,512,512]{2,0,1:T(2,128)(2,1)}), bf16[2,512,512]{2,0,1:T(2,128)(2,1)}, u32[]{:S(2)}, u32[]{:S(2)}) async-start(bf16[2,512,512]{2,0,1:T(2,128)(2,1)} %bitcast.74), calls=%async_computation | async-start | bytes 2097152 | tf_op jit(solution)/shard_map/all_to_all | solution.py:51
  196.1 14.5 %all-to-all-done = bf16[2,512,512]{2,0,1:T(2,128)(2,1)} async-done(((bf16[2,512,512]{2,0,1:T(2,128)(2,1)}), bf16[2,512,512]{2,0,1:T(2,128)(2,1)}, u32[]{:S(2)}, u32[]{:S(2)}) %all-to-all-start) | async-done | bytes 1048608 | tf_op jit(solution)/shard_map/all_to_all | solution.py:51
  210.6 1.4 copy.26
  211.9 1.1 copy.27
  213.0 25.2 %while.25 = (s32[]{:T(128)}, f32[128,512]{1,0:T(8,128)S(1)}, bf16[8,128,512]{2,1,0:T(8,128)(2,1)}, bf16[8,128,512]{2,1,0:T(8,128)(2,1)}, bf16[512,1536]{1,0:T(8,...) while((s32[]{:T(128)}, f32[128,512]{1,0:T(8,128)S(1)}, ...), condition=%wide.region_3.4_spmd.clone, body=%wide.region_2.3_spmd.sunk.clone | while | flops 403767296 | bytes 7343181 | solution.py:60
  213.0 1.9 fusion.66
  215.3 0.9 bitcast_dynamic-update-slice_fusion.3
  216.2 1.9 fusion.66
  218.4 0.9 bitcast_dynamic-update-slice_fusion.3
  219.3 1.9 fusion.66
  221.6 0.9 bitcast_dynamic-update-slice_fusion.3
  222.5 1.9 fusion.66
  224.7 0.9 bitcast_dynamic-update-slice_fusion.3
  225.6 1.9 fusion.66
  227.9 0.9 bitcast_dynamic-update-slice_fusion.3
  228.8 1.9 fusion.66
  231.9 1.9 fusion.66
  235.1 1.9 fusion.66
  238.2 17.9 %all_to_all.36 = bf16[8,128,512]{2,1,0:T(8,128)(2,1)S(1)} all-to-all(bf16[8,128,512]{2,1,0:T(8,128)(2,1)} %get-tuple-element.70), channel_id=1, replica_groups=mesh['tm'=4,'dom'=8] {'tm'}, dimensions={0} | all-to-all | bytes 2097152 | tf_op jit(solution)/shard_map/all_to_all | solution.py:61
  256.2 1.1 copy.28
  (33 shorter events, 7.6 us)
Async XLA Ops:
  6.5 189.5 %copy-start = (f32[512,512]{1,0:T(8,128)S(1)}, f32[512,512]{1,0:T(8,128)}, u32[]{:S(2)}) copy-start(f32[512,512]{1,0:T(8,128)} %param.17) | copy-start | bytes 3145732
  6.5 130.7 %all-gather.2.cloned.1.call-start = ((), (), s32[]{:S(2)}) async-start(), calls=%async_computation.2 | async-start | bytes 9437184 | tf_op jit(solution)/shard_map/all_gather | solution.py:37
  188.1 24.9 %copy-start.1 = (bf16[512,1536]{1,0:T(8,128)(2,1)S(1)}, bf16[512,1536]{1,0:T(8,128)(2,1)}, u32[]{:S(2)}) copy-start(bf16[512,1536]{1,0:T(8,128)(2,1)} %param.20) | copy-start | bytes 4718596
  188.1 24.9 %copy-start.2 = (f32[512]{0:T(512)S(1)}, f32[512]{0:T(512)}, u32[]{:S(2)}) copy-start(f32[512]{0:T(512)} %param.21) | copy-start | bytes 6148
  191.8 18.8 %all-to-all-start = ((bf16[2,512,512]{2,0,1:T(2,128)(2,1)}), bf16[2,512,512]{2,0,1:T(2,128)(2,1)}, u32[]{:S(2)}, u32[]{:S(2)}) async-start(bf16[2,512,512]{2,0,1:T(2,128)(2,1)} %bitcast.74), calls=%async_computation | async-start | bytes 2097152 | tf_op jit(solution)/shard_map/all_to_all | solution.py:51
Sparse Core Ops, SparseCore 0:
  9.5 127.6 all-gather.1
where the time goes:
time: 265 us; the launch traced here: 264 us
  waiting for transfers between devices  134 us (51%)
  matrix products  40.6 us (15%)
  local copies, waits for them, and re-layouts  36.2 us (14%)
  blocking collectives  17.9 us (7%)
  other arithmetic  17.5 us (7%)
  between operations  13.5 us (5%)
  starting transfers between devices  4.26 us (2%)
    all_gather x1, waiting for transfers between devices, per_device(): whole = lax.all_gather(projected, 'dom', axis=1, tiled=True)  120 us
    gather x2, local copies, waits for them, and re-layouts, one_snapshot(): picked = block_set[col_set]  20.7 us
    dot_general x2, matrix products, one_snapshot(): jnp.einsum('npkij,npkjh->nih', tile_set, picked, preferred_element_type=j...  20.4 us
    all_to_all x1, blocking collectives, per_device(): lax.all_to_all(own_seq, 'tm', split_axis=0, concat_axis=1, tiled=True)  17.9 us
    dot_general x8, matrix products, scan_cell(): gx = jnp.dot(graph_row, w_input, preferred_element_type=jnp.float32)  14.8 us
    all_to_all x1, waiting for transfers between devices, per_device(): lax.all_to_all(graph_out, 'tm', split_axis=1, concat_axis=0, tiled=True)  14.5 us
    squeeze x2, local copies, waits for them, and re-layouts, per_device(): lax.map(one_snapshot, (all_blocks, global_cols, masked))  9.38 us
    dynamic_update_slice x8, other arithmetic, per_device(): last_state, own_seq = lax.scan(scan_cell, start_rows, mine)  7.27 us
  transfers between devices with their start and end apart: 2, of which 2 were waited for; matrix products, arithmetic and copies ran while one was open for 3% of the time, Pallas kernels for 0%

commit v1 on v0

v1 whole, which is shorter than its diff:
```python
import functools

import jax
import jax.numpy as jnp
from jax import lax
from jax.experimental import pallas as pl
from jax.experimental.pallas import tpu as pltpu
from jax.sharding import PartitionSpec as P

BF16 = jnp.bfloat16
F32 = jnp.float32
CORES = 2
CHUNKS = 2
VMEM = pltpu.MemorySpace.VMEM
SMEM = pltpu.MemorySpace.SMEM


def ring_order(size):
    width = 1
    while width * width * 4 <= size:
        width *= 2
    depth = size // width
    walk = [(z, 0) for z in range(depth)]
    for step, z in enumerate(reversed(range(depth))):
        row = range(1, width) if step % 2 == 0 else reversed(range(1, width))
        walk += [(z, y) for y in row]
    return [z * width + y for z, y in walk]


def sigmoid(x):
    return 0.5 * jnp.tanh(0.5 * x) + 0.5


def params():
    return pltpu.CompilerParams(vmem_limit_bytes=24 * 2**20)


def cost(flops, bytes_accessed):
    return pl.CostEstimate(flops=int(flops), bytes_accessed=int(bytes_accessed), transcendentals=0)


def add_partition(tiles, cols, counts, x_ref, snap, row, part, lhs, rhs):
    parts, slots = tiles.shape[2:4]
    blk = tiles.shape[-1]
    rows = tiles.shape[1]
    base = (snap * rows + row) * parts + part
    for k in range(slots):
        col = cols[base * slots + k]
        block = x_ref[pl.ds(pl.multiple_of(col * blk, blk), blk), :]
        rhs.append(jnp.where(k < counts[base], block, jnp.zeros_like(block)))
        lhs.append(tiles[snap, row, part, k])


def spmm_kernel(info, cols, counts, tiles, *refs, pieces, first, last):
    x_refs = refs[: len(pieces)]
    acc_in = None if first else refs[len(pieces)]
    outs = refs[len(pieces) + (0 if first else 1) :]
    snaps, rows = tiles.shape[:2]
    half = rows // CORES
    core = info[0]
    for snap in range(snaps):
        for rel in range(rows):
            row = lax.rem(rel + core * half, rows)
            lhs, rhs = [], []
            for x_ref, (piece_snap, where) in zip(x_refs, pieces):
                if piece_snap == snap:
                    add_partition(tiles, cols, counts, x_ref, snap, row, info[where], lhs, rhs)
            total = jnp.dot(
                jnp.concatenate(lhs, axis=1), jnp.concatenate(rhs, axis=0), preferred_element_type=F32
            )
            if not first:
                total = total + acc_in[snap, rel]
            if last:
                keep, send = outs
                blk = total.shape[0]
                target = keep if rel < half else send
                at = (rel % half) * blk
                target[snap, at : at + blk, :] = total.astype(BF16)
            else:
                outs[0][snap, rel] = total


def spmm(info, cols, counts, tiles, xs, pieces, acc, last):
    snaps, rows, parts, slots, blk, _ = tiles.shape
    feats = xs[0].shape[-1]
    first = acc is None
    operands = [info, cols, counts, tiles, *xs] + ([] if first else [acc])
    specs = [pl.BlockSpec(memory_space=SMEM)] * 3 + [pl.BlockSpec(memory_space=VMEM)] * (len(operands) - 3)
    if last:
        out = jax.ShapeDtypeStruct((snaps, rows // CORES * blk, feats), BF16)
        out_shape = (out, out)
        aliases = {}
    else:
        out_shape = jax.ShapeDtypeStruct((snaps, rows, blk, feats), F32)
        aliases = {} if first else {len(operands) - 1: 0}
    flops = 2 * len(xs) * rows * slots * blk * blk * feats
    return pl.pallas_call(
        functools.partial(spmm_kernel, pieces=pieces, first=first, last=last),
        out_shape=out_shape,
        in_specs=specs,
        out_specs=jax.tree.map(lambda _: pl.BlockSpec(memory_space=VMEM), out_shape),
        input_output_aliases=aliases,
        compiler_params=params(),
        cost_estimate=cost(flops * 4, 2**20),
        name="spmm",
    )(*operands)


def gates(ax, w_graph, w_input):
    snaps, rows, feats = ax.shape
    hid, width = w_input.shape

    def kernel(ax, w_graph, w_input, out):
        graph = jnp.dot(ax[...].reshape(snaps * rows, feats), w_graph[...], preferred_element_type=F32)
        graph = jnp.maximum(graph, 0.0).astype(BF16)
        for j in range(0, width, hid):
            part = jnp.dot(graph, w_input[:, j : j + hid], preferred_element_type=F32)
            out[:, :, j : j + hid] = part.reshape(snaps, rows, hid)

    return pl.pallas_call(
        kernel,
        out_shape=jax.ShapeDtypeStruct((snaps, rows, width), F32),
        in_specs=[pl.BlockSpec(memory_space=VMEM)] * 3,
        out_specs=pl.BlockSpec(memory_space=VMEM),
        compiler_params=params(),
        cost_estimate=cost(2 * snaps * rows * hid * width * 2, 2**20),
        name="gates",
    )(ax, w_graph, w_input)


def recurrence_kernel(info, state_in, gx_own, gx_other, w_hidden, bias, *refs, phase, chunk):
    state_out, keep, send = refs[-3:]
    core, place = info[0], info[1]
    snaps, rows, hid = keep.shape
    at = slice(chunk * rows, (chunk + 1) * rows)
    block = min(256, hid)

    def run(own_first):
        state = state_in[...].astype(F32)
        for step in range(CORES * snaps):
            own = (step < snaps) == own_first
            gx, out, s = (gx_own if own else gx_other), (keep if own else send), step % snaps
            low = state.astype(BF16)
            parts = []
            for j in range(0, hid, block):
                def gate(g):
                    return jnp.dot(low, w_hidden[:, g * hid + j : g * hid + j + block], preferred_element_type=F32)

                def given(g):
                    return gx[s, at, g * hid + j : g * hid + j + block]

                gh_r, gh_c, gh_u = gate(0), gate(2), gate(1)
                reset = sigmoid(given(0) + gh_r)
                cand = jnp.tanh(given(2) + reset * gh_c)
                update = sigmoid(given(1) + gh_u + bias[:, j : j + block])
                parts.append(update * state[:, j : j + block] + (1.0 - update) * cand)
            state = jnp.concatenate(parts, axis=1)
            out[s] = state.astype(BF16)
        state_out[...] = state.astype(BF16)

    @pl.when((place == phase) & (core == 0))
    def _():
        run(True)

    @pl.when((place == phase) & (core != 0))
    def _():
        run(False)


def recurrence(info, state, gx_own, gx_other, w_hidden, bias, hidden, phase, chunk):
    hid = w_hidden.shape[0]
    snaps = gx_own.shape[0]
    rows = gx_own.shape[1] // CHUNKS
    operands = [info, state, gx_own, gx_other, w_hidden, bias] + list(hidden)
    part = jax.ShapeDtypeStruct((snaps, rows, hid), BF16)
    specs = [pl.BlockSpec(memory_space=SMEM)] + [pl.BlockSpec(memory_space=VMEM)] * (len(operands) - 1)
    return pl.pallas_call(
        functools.partial(recurrence_kernel, phase=phase, chunk=chunk),
        out_shape=(jax.ShapeDtypeStruct((rows, hid), BF16), part, part),
        in_specs=specs,
        out_specs=(pl.BlockSpec(memory_space=VMEM),) * 3,
        input_output_aliases={6: 1, 7: 2} if hidden else {},
        compiler_params=params(),
        cost_estimate=cost(2 * CORES * snaps * rows * hid * 3 * hid * 4, 2**20),
        name="recurrence",
    )(*operands)


def per_device(
    features, tile_values, tile_cols, tile_count, hidden_start, w_graph, w_input, w_hidden, update_bias
):
    snaps, nodes, feats = features.shape
    parts = lax.axis_size("dom")
    sections = lax.axis_size("tm")
    places = sections // CORES
    me_time, me_dom = lax.axis_index("tm"), lax.axis_index("dom")
    core, place = me_time % CORES, me_time // CORES

    order = ring_order(parts)
    spot = [0] * parts
    for i, d in enumerate(order):
        spot[d] = i
    ahead = [(order[i], order[(i + 1) % parts]) for i in range(parts)]
    back = [(b, a) for a, b in ahead]
    my_spot = jnp.array(spot, jnp.int32)[me_dom]
    ring = jnp.array(order, jnp.int32)
    shifted = ring[(my_spot + jnp.arange(parts, dtype=jnp.int32)) % parts]
    info = jnp.concatenate([jnp.stack([core, place]).astype(jnp.int32), shifted])
    cols = tile_cols.reshape(-1)
    counts = tile_count.reshape(-1)

    own = [features[s] for s in range(snaps)]
    forward = [[x] for x in own]
    reverse = [[x] for x in own]
    far = parts // 2
    acc = spmm(info, cols, counts, tile_values, own, [(s, 2) for s in range(snaps)], None, False)
    for hop in range(1, far + 1):
        xs, pieces = [], []
        for s in range(snaps):
            if hop < far or s % 2 == 0:
                forward[s].append(lax.ppermute(forward[s][-1], "dom", ahead))
                xs.append(forward[s][-1])
                pieces.append((s, 2 + (parts - hop) % parts))
            if hop < far or s % 2 == 1:
                reverse[s].append(lax.ppermute(reverse[s][-1], "dom", back))
                xs.append(reverse[s][-1])
                pieces.append((s, 2 + hop))
        acc = spmm(info, cols, counts, tile_values, xs, pieces, acc, hop == far)
    keep_ax, send_ax = acc

    swap = [(t, t ^ 1) for t in range(sections)]
    other_ax = lax.ppermute(send_ax, "tm", swap)
    gx_own = gates(keep_ax, w_graph, w_input)
    gx_other = gates(other_ax, w_graph, w_input)

    bias = update_bias.reshape(1, -1)
    mine = nodes // CORES
    rows = mine // CHUNKS
    onward = [(t, t + CORES) for t in range(sections - CORES)]
    states = [
        lax.dynamic_slice_in_dim(hidden_start, core * mine + chunk * rows, rows, 0) for chunk in range(CHUNKS)
    ]
    hidden = [()] * CHUNKS
    for phase in range(places):
        for chunk in range(CHUNKS):
            state, keep, send = recurrence(
                info, states[chunk], gx_own, gx_other, w_hidden, bias, hidden[chunk], phase, chunk
            )
            hidden[chunk] = (keep, send)
            if phase < places - 1:
                states[chunk] = lax.ppermute(state, "tm", onward)
    swapped = [lax.ppermute(send, "tm", swap) for _, send in hidden]
    kept = jnp.concatenate([keep for keep, _ in hidden], axis=1)
    got = jnp.concatenate(swapped, axis=1)
    return jnp.where(
        core == 0, jnp.concatenate([kept, got], axis=1), jnp.concatenate([got, kept], axis=1)
    )


def solution(mesh):
    placed = (
        P("tm", "dom", None),
        P("tm", "dom", None, None, None, None),
        P("tm", "dom", None, None),
        P("tm", "dom", None),
        P("dom", None),
        P(),
        P(),
        P(),
        P(),
    )
    return jax.shard_map(
        per_device, mesh=mesh, in_specs=placed, out_specs=P("tm", "dom", None), check_vma=False
    )
```

time: 265 us -> 52.8 us (0.20)
  the two profiles are of different devices: /device:TPU:0 before, /device:TPU:23 now
where the time goes in v1:
time: 52.8 us; the launch traced here: 52.4 us
  starting transfers between devices  18.7 us (35%)
  Pallas kernels  14.9 us (28%)
  local copies, waits for them, and re-layouts  9.33 us (18%)
  waiting for transfers between devices  7.13 us (14%)
  other arithmetic  2.14 us (4%)
    ppermute x7, starting transfers between devices, per_device(): reverse[s].append(lax.ppermute(reverse[s][-1], 'dom', back))  9.19 us
    pallas_call x4, Pallas kernels, recurrence(): pl.pallas_call(functools.partial(recurrence_kernel, phase=phase, chunk=ch...  6.64 us
    pallas_call x5, Pallas kernels, spmm(): pl.pallas_call(functools.partial(spmm_kernel, pieces=pieces, first=first,...  6.04 us
    unnamed x13, local copies, waits for them, and re-layouts  4.51 us
    ppermute x1, starting transfers between devices, per_device(): other_ax = lax.ppermute(send_ax, 'tm', swap)  4.36 us
    ppermute x2, waiting for transfers between devices, per_device(): states[chunk] = lax.ppermute(state, 'tm', onward)  3.83 us
    ppermute x2, starting transfers between devices, per_device(): states[chunk] = lax.ppermute(state, 'tm', onward)  2.58 us
    pallas_call x2, Pallas kernels, gates(): pl.pallas_call(kernel, out_shape=jax.ShapeDtypeStruct((snaps, rows, width...  2.21 us
  transfers between devices with their start and end apart: 19, of which 3 were waited for; matrix products, arithmetic and copies ran while one was open for 10% of the time, Pallas kernels for 23%

profile of v1, /device:TPU:23, one launch (start us, length us, event | category | flops | bytes accessed | tf_op | source)
XLA Modules:
  0.0 52.4 jit_solution(4153593564431992797)
XLA Ops:
  0.0 1.0 %slice_bitcast_fusion = (bf16[512,128]{1,0:T(8,128)(2,1)S(1)}, bf16[512,128]{1,0:T(8,128)(2,1)S(1)}) fusion(bf16[2,512,128]{2,1,0:T(8,128)(2,1)} %param.11), kind=kLoop, calls=%fused_computation.2 | loop fusion | bytes 524288 | tf_op jit(solution)/shard_map/squeeze | solution.py:212
  1.2 1.3 %collective-permute-start.4 = (bf16[512,128]{1,0:T(8,128)(2,1)S(1)}, bf16[512,128]{1,0:T(8,128)(2,1)S(1)}, u32[]{:S(2)}, u32[]{:S(2)}) collective-permute-start(bf16[512,128]{1,0:T(8,128)(2,1)S(1)} %get-tuple-element.31.refs_1_), channel_id=1, source_target_pairs={{2,0},{4,2},{6,4},{7,6},{5,7},{3,5},{1,3},{0,1},{10,8},{12,10},{14... | collective-permute-start | bytes 393224 | tf_op jit(solution)/shard_map/ppermute | solution.py:225
  2.5 1.3 %collective-permute-start.8 = (bf16[512,128]{1,0:T(8,128)(2,1)S(1)}, bf16[512,128]{1,0:T(8,128)(2,1)S(1)}, u32[]{:S(2)}, u32[]{:S(2)}) collective-permute-start(bf16[512,128]{1,0:T(8,128)(2,1)S(1)} %get-tuple-element.32.refs_0_), channel_id=1, source_target_pairs={{2,0},{4,2},{6,4},{7,6},{5,7},{3,5},{1,3},{0,1},{10,8},{12,10},{14... | collective-permute-start | bytes 393224 | tf_op jit(solution)/shard_map/ppermute | solution.py:225
  4.0 1.1 %constant_dynamic-slice_fusion.1 = (f32[128,512]{1,0:T(8,128)S(1)}, f32[128,512]{1,0:T(8,128)S(1)}) fusion(f32[512,512]{1,0:T(8,128)} %param.15, s32[]{:T(128)S(6)} %select_n.57, s32[]{:T(128)S(6)} %select_n.58), kind=kLoop, calls=%fused_computation.13 | loop fusion | bytes 1048584 | tf_op jit(solution)/shard_map/dynamic_slice | solution.py:241
  5.1 1.2 %dynamic_slice.9 = s32[1]{0:T(128)} dynamic-slice(s32[8]{0:T(128)} %constant.61.clone, s32[]{:T(128)S(6)} %select_n.54), dynamic_slice_sizes={1} | dynamic-slice | bytes 12 | tf_op jit(solution)/shard_map/dynamic_slice | solution.py:205
  6.3 0.7 %fusion.1 = s32[8]{0:T(128)S(1)} fusion(s32[]{:T(128)} %bitcast.2), kind=kLoop, calls=%fused_computation.10 | loop fusion | flops 120 | bytes 36 | tf_op jit(solution)/shard_map/select_n | solution.py:207
  7.0 1.3 %collective-permute-start.5 = (bf16[512,128]{1,0:T(8,128)(2,1)S(1)}, bf16[512,128]{1,0:T(8,128)(2,1)S(1)}, u32[]{:S(2)}, u32[]{:S(2)}) collective-permute-start(bf16[512,128]{1,0:T(8,128)(2,1)S(1)} %collective-permute-done.4.refs_3_), channel_id=1, source_target_pairs={{2,0},{4,2},{6,4},{7,6},{5,7},{3,5},{1,3},{0,1},{10,8},{12,10},{14... | collective-permute-start | bytes 393224 | tf_op jit(solution)/shard_map/ppermute | solution.py:225
  8.5 0.8 %reshape.59.counts = s32[64]{0:T(128)S(1)} reshape(s32[2,4,8]{2,1,0:T(4,128)} %param.14) | data formatting | bytes 512 | tf_op jit(solution)/shard_map/reshape | solution.py:210
  9.3 0.8 %copy.19 = s32[2,4,8,4]{3,2,1,0:T(8,128)S(1)} copy(s32[2,4,8,4]{2,3,1,0:T(4,128)} %param.13) | data formatting | bytes 2048 | tf_op args[2]
  10.2 0.6 %gather_fusion = s32[8]{0:T(128)S(1)} fusion(s32[8]{0:T(128)S(1)} %copy-done.5, s32[1024]{0:T(1024)S(1)} %pad_clamp_fusion), kind=kCustom, calls=%fused_computation | custom fusion | bytes 96 | tf_op jit(solution)/shard_map/gather | solution.py:207
  11.1 1.3 %collective-permute-start.9 = (bf16[512,128]{1,0:T(8,128)(2,1)S(1)}, bf16[512,128]{1,0:T(8,128)(2,1)S(1)}, u32[]{:S(2)}, u32[]{:S(2)}) collective-permute-start(bf16[512,128]{1,0:T(8,128)(2,1)S(1)} %collective-permute-done.8.refs_1_), channel_id=1, source_target_pairs={{2,0},{4,2},{6,4},{7,6},{5,7},{3,5},{1,3},{0,1},{10,8},{12,10},{14... | collective-permute-start | bytes 393224 | tf_op jit(solution)/shard_map/ppermute | solution.py:225
  12.5 1.3 %collective-permute-start.6 = (bf16[512,128]{1,0:T(8,128)(2,1)S(1)}, bf16[512,128]{1,0:T(8,128)(2,1)S(1)}, u32[]{:S(2)}, u32[]{:S(2)}) collective-permute-start(bf16[512,128]{1,0:T(8,128)(2,1)S(1)} %collective-permute-done.5.refs_3_), channel_id=1, source_target_pairs={{2,0},{4,2},{6,4},{7,6},{5,7},{3,5},{1,3},{0,1},{10,8},{12,10},{14... | collective-permute-start | bytes 393224 | tf_op jit(solution)/shard_map/ppermute | solution.py:225
  14.0 3.4 %copy-done = bf16[2,4,8,4,128,128]{5,4,3,2,1,0:T(8,128)(2,1)S(1)} copy-done((bf16[2,4,8,4,128,128]{5,4,3,2,1,0:T(8,128)(2,1)S(1)}, bf16[2,4,8,4,128,128]{5,4,3,2,1,0:T(8,128)(2,1)}, u32[]{:S(2)}) %copy-start) | copy-done | bytes 8388632
  17.3 1.0 %spmm.5.refs_4_ = f32[2,4,128,128]{3,2,1,0:T(8,128)S(1)} custom-call(s32[10]{0:T(128)S(1)} %pad_add_fusion.info, s32[256]{0:T(256)S(1)} %reshape.58.cols, s32[64]{0:T(128)S(1)} %reshape.59.counts, bf16[2,4,8,4,128,128]{5,4,3,2,1,0:T(8,128)(2,1)S(1)} %copy-done, bf16[512,128]{1,0:T(8,128)(2,1)S(1)} %get-tuple-element.32.refs_0_, ...), custom_call_target="tpu_custom_call" | custom-call | flops 536870912 | bytes 1048576 | tf_op jit(solution)/shard_map/spmm/pallas_call | solution.py:97
  18.6 1.3 %collective-permute-start.10 = (bf16[512,128]{1,0:T(8,128)(2,1)S(1)}, bf16[512,128]{1,0:T(8,128)(2,1)S(1)}, u32[]{:S(2)}, u32[]{:S(2)}) collective-permute-start(bf16[512,128]{1,0:T(8,128)(2,1)S(1)} %collective-permute-done.9.refs_1_), channel_id=1, source_target_pairs={{2,0},{4,2},{6,4},{7,6},{5,7},{3,5},{1,3},{0,1},{10,8},{12,10},{14... | collective-permute-start | bytes 393224 | tf_op jit(solution)/shard_map/ppermute | solution.py:225
  19.9 1.4 %spmm.6.refs_4_ = f32[2,4,128,128]{3,2,1,0:T(8,128)S(1)} custom-call(s32[10]{0:T(128)S(1)} %pad_add_fusion.info, s32[256]{0:T(256)S(1)} %reshape.58.cols, s32[64]{0:T(128)S(1)} %reshape.59.counts, bf16[2,4,8,4,128,128]{5,4,3,2,1,0:T(8,128)(2,1)S(1)} %copy-done, bf16[512,128]{1,0:T(8,128)(2,1)S(1)} %collective-permute-done.refs_0_, ...), custom_call_target="tpu_custom_call", output_to_operand_aliasing={{}: (8, {})} | custom-call | flops 1073741824 | bytes 1048576 | tf_op jit(solution)/shard_map/spmm/pallas_call | solution.py:97
  21.3 1.3 %collective-permute-start.7 = (bf16[512,128]{1,0:T(8,128)(2,1)S(1)}, bf16[512,128]{1,0:T(8,128)(2,1)S(1)}, u32[]{:S(2)}, u32[]{:S(2)}) collective-permute-start(bf16[512,128]{1,0:T(8,128)(2,1)S(1)} %collective-permute-done.6.refs_3_), channel_id=1, source_target_pairs={{2,0},{4,2},{6,4},{7,6},{5,7},{3,5},{1,3},{0,1},{10,8},{12,10},{14... | collective-permute-start | bytes 393224 | tf_op jit(solution)/shard_map/ppermute | solution.py:225
  22.8 1.3 %spmm.7.refs_4_ = f32[2,4,128,128]{3,2,1,0:T(8,128)S(1)} custom-call(s32[10]{0:T(128)S(1)} %pad_add_fusion.info, s32[256]{0:T(256)S(1)} %reshape.58.cols, s32[64]{0:T(128)S(1)} %reshape.59.counts, bf16[2,4,8,4,128,128]{5,4,3,2,1,0:T(8,128)(2,1)S(1)} %copy-done, bf16[512,128]{1,0:T(8,128)(2,1)S(1)} %collective-permute-done.1.refs_0_, ...), custom_call_target="tpu_custom_call", output_to_operand_aliasing={{}: (8, {})} | custom-call | flops 1073741824 | bytes 1048576 | tf_op jit(solution)/shard_map/spmm/pallas_call | solution.py:97
  24.2 1.3 %spmm.8.refs_2_ = f32[2,4,128,128]{3,2,1,0:T(8,128)S(1)} custom-call(s32[10]{0:T(128)S(1)} %pad_add_fusion.info, s32[256]{0:T(256)S(1)} %reshape.58.cols, s32[64]{0:T(128)S(1)} %reshape.59.counts, bf16[2,4,8,4,128,128]{5,4,3,2,1,0:T(8,128)(2,1)S(1)} %copy-done, bf16[512,128]{1,0:T(8,128)(2,1)S(1)} %collective-permute-done.2.refs_0_, ...), custom_call_target="tpu_custom_call", output_to_operand_aliasing={{}: (8, {})} | custom-call | flops 1073741824 | bytes 1048576 | tf_op jit(solution)/shard_map/spmm/pallas_call | solution.py:97
  25.5 2.1 %collective-permute-done.3.refs_0_ = bf16[512,128]{1,0:T(8,128)(2,1)S(1)} collective-permute-done((bf16[512,128]{1,0:T(8,128)(2,1)S(1)}, bf16[512,128]{1,0:T(8,128)(2,1)S(1)}, u32[]{:S(2)}, u32[]{:S(2)}) %collective-permute-start.3) | collective-permute-done | bytes 131104 | tf_op jit(solution)/shard_map/ppermute | solution.py:221
  27.6 1.0 %spmm.9 = (bf16[2,256,128]{2,1,0:T(8,128)(2,1)S(1)}, bf16[2,256,128]{2,1,0:T(8,128)(2,1)S(1)}) custom-call(s32[10]{0:T(128)S(1)} %pad_add_fusion.info, s32[256]{0:T(256)S(1)} %reshape.58.cols, s32[64]{0:T(128)S(1)} %reshape.59.counts, bf16[2,4,8,4,128,128]{5,4,3,2,1,0:T(8,128)(2,1)S(1)} %copy-done, bf16[512,128]{1,0:T(8,128)(2,1)S(1)} %collective-permute-done.3.refs_0_, ...), custom_call_target="tpu_custom_call" | custom-call | flops 536870912 | bytes 1048576 | tf_op jit(solution)/shard_map/spmm/pallas_call | solution.py:97
  28.6 4.4 %collective-permute-start.14 = (bf16[2,256,128]{2,1,0:T(8,128)(2,1)S(1)}, bf16[2,256,128]{2,1,0:T(8,128)(2,1)S(1)}, u32[]{:S(2)}, u32[]{:S(2)}) collective-permute-start(bf16[2,256,128]{2,1,0:T(8,128)(2,1)S(1)} %get-tuple-element.18), channel_id=1, source_target_pairs={{0,8},{8,0},{16,24},{24,16},{1,9},{9,1},{17,25},{25,17},{2,10},{10... | collective-permute-start | bytes 393224 | tf_op jit(solution)/shard_map/ppermute | solution.py:232
  33.0 1.1 %gates.2.gx_own = f32[2,256,1536]{2,1,0:T(8,128)S(1)} custom-call(bf16[2,256,128]{2,1,0:T(8,128)(2,1)S(1)} %get-tuple-element.17.ax, bf16[128,512]{1,0:T(8,128)(2,1)S(1)} %copy-done.3, bf16[512,1536]{1,0:T(8,128)(2,1)S(1)} %copy-done.1), custom_call_target="tpu_custom_call" | custom-call | flops 1610612736 | bytes 1048576 | tf_op jit(solution)/shard_map/gates/pallas_call | solution.py:120
  34.1 1.1 %gates.3.gx_other = f32[2,256,1536]{2,1,0:T(8,128)S(1)} custom-call(bf16[2,256,128]{2,1,0:T(8,128)(2,1)S(1)} %collective-permute-done.14.ax, bf16[128,512]{1,0:T(8,128)(2,1)S(1)} %copy-done.3, bf16[512,1536]{1,0:T(8,128)(2,1)S(1)} %copy-done.1), custom_call_target="tpu_custom_call" | custom-call | flops 1610612736 | bytes 1048576 | tf_op jit(solution)/shard_map/gates/pallas_call | solution.py:120
  36.1 1.3 %collective-permute-start.16 = (bf16[128,512]{1,0:T(8,128)(2,1)S(1)}, bf16[128,512]{1,0:T(8,128)(2,1)S(1)}, u32[]{:S(2)}, u32[]{:S(2)}) collective-permute-start(bf16[128,512]{1,0:T(8,128)(2,1)S(1)} %get-tuple-element.23), channel_id=1, source_target_pairs={{0,16},{8,24},{1,17},{9,25},{2,18},{10,26},{3,19},{11,27},{4,20},{... | collective-permute-start | bytes 393224 | tf_op jit(solution)/shard_map/ppermute | solution.py:251
  38.0 1.3 %collective-permute-start.15 = (bf16[128,512]{1,0:T(8,128)(2,1)S(1)}, bf16[128,512]{1,0:T(8,128)(2,1)S(1)}, u32[]{:S(2)}, u32[]{:S(2)}) collective-permute-start(bf16[128,512]{1,0:T(8,128)(2,1)S(1)} %get-tuple-element.19), channel_id=1, source_target_pairs={{0,16},{8,24},{1,17},{9,25},{2,18},{10,26},{3,19},{11,27},{4,20},{... | collective-permute-start | bytes 393224 | tf_op jit(solution)/shard_map/ppermute | solution.py:251
  39.3 3.8 %collective-permute-done.16.state_in = bf16[128,512]{1,0:T(8,128)(2,1)S(1)} collective-permute-done((bf16[128,512]{1,0:T(8,128)(2,1)S(1)}, bf16[128,512]{1,0:T(8,128)(2,1)S(1)}, u32[]{:S(2)}, u32[]{:S(2)}) %collective-permute-start.16) | collective-permute-done | bytes 131104 | tf_op jit(solution)/shard_map/ppermute | solution.py:251
  43.1 2.9 %recurrence.7 = (bf16[128,512]{1,0:T(8,128)(2,1)}, bf16[2,128,512]{2,1,0:T(8,128)(2,1)S(1)}, bf16[2,128,512]{2,1,0:T(8,128)(2,1)S(1)}) custom-call(s32[10]{0:T(128)S(1)} %pad_add_fusion.info, bf16[128,512]{1,0:T(8,128)(2,1)S(1)} %collective-permute-done.16.state_in, f32[2,256,1536]{2,1,0:T(8,128)S(1)} %gates.2.gx_own, ...), custom_call_target="tpu_custom_call", output_to_operand_aliasing={{1}: (6, {}), {2}: (7, {})} | custom-call | flops 3221225472 | bytes 1048576 | tf_op jit(solution)/shard_map/recurrence/pallas_call | solution.py:177
  45.9 0.8 %collective-permute-start.18 = (bf16[2,128,512]{2,1,0:T(8,128)(2,1)S(1)}, bf16[2,128,512]{2,1,0:T(8,128)(2,1)S(1)}, u32[]{:S(2)}, u32[]{:S(2)}) collective-permute-start(bf16[2,128,512]{2,1,0:T(8,128)(2,1)S(1)} %get-tuple-element.28), channel_id=1, source_target_pairs={{0,8},{8,0},{16,24},{24,16},{1,9},{9,1},{17,25},{25,17},{2,10},{10... | collective-permute-start | bytes 786440 | tf_op jit(solution)/shard_map/ppermute | solution.py:252
  46.7 2.7 %recurrence.5 = (bf16[128,512]{1,0:T(8,128)(2,1)}, bf16[2,128,512]{2,1,0:T(8,128)(2,1)S(1)}, bf16[2,128,512]{2,1,0:T(8,128)(2,1)S(1)}) custom-call(s32[10]{0:T(128)S(1)} %pad_add_fusion.info, bf16[128,512]{1,0:T(8,128)(2,1)S(1)} %collective-permute-done.15.state_in, f32[2,256,1536]{2,1,0:T(8,128)S(1)} %gates.2.gx_own, ...), custom_call_target="tpu_custom_call", output_to_operand_aliasing={{1}: (6, {}), {2}: (7, {})} | custom-call | flops 3221225472 | bytes 1048576 | tf_op jit(solution)/shard_map/recurrence/pallas_call | solution.py:177
  49.9 1.2 %collective-permute-done.17 = bf16[2,128,512]{2,1,0:T(8,128)(2,1)S(1)} collective-permute-done((bf16[2,128,512]{2,1,0:T(8,128)(2,1)S(1)}, bf16[2,128,512]{2,1,0:T(8,128)(2,1)S(1)}, u32[]{:S(2)}, u32[]{:S(2)}) %collective-permute-start.17) | collective-permute-done | bytes 262176 | tf_op jit(solution)/shard_map/ppermute | solution.py:252
  51.0 1.4 %maximum_select_fusion = bf16[2,512,512]{2,1,0:T(8,128)(2,1)} fusion(bf16[2,128,512]{2,1,0:T(8,128)(2,1)S(1)} %collective-permute-done.18, bf16[2,128,512]{2,1,0:T(8,128)(2,1)S(1)} %collective-permute-done.17, bf16[2,128,512]{2,1,0:T(8,128)(2,1)S(1)} %get-tuple-element.26, bf16[2,128,512]{2,1,0:T(8,128)(2,1)S(1)} %get-tuple-element.22, pred[]{:T(512)S(6)} %eq.7), kind=kLoop, calls=%fused_computation.1 | loop fusion | flops 8912896 | bytes 2097153 | tf_op jit(solution)/shard_map/jit(_where)/select_n | solution.py:255
  (40 shorter events, 3.4 us)
Async XLA Ops:
  0.0 10.2 %copy-start.5 = (s32[8]{0:T(128)S(1)}, s32[8]{0:T(128)}, u32[]{:S(2)}) copy-start(s32[8]{0:T(128)} %constant.62.clone) | copy-start | bytes 100
  1.0 9.9 %collective-permute-start.11 = (bf16[512,128]{1,0:T(8,128)(2,1)S(1)}, bf16[512,128]{1,0:T(8,128)(2,1)S(1)}, u32[]{:S(2)}, u32[]{:S(2)}) collective-permute-start(bf16[512,128]{1,0:T(8,128)(2,1)S(1)} %get-tuple-element.31.refs_1_), channel_id=1, source_target_pairs={{0,2},{2,4},{4,6},{6,7},{7,5},{5,3},{3,1},{1,0},{8,10},{10,12},{12... | collective-permute-start | bytes 393224 | tf_op jit(solution)/shard_map/ppermute | solution.py:221
  1.2 5.7 %collective-permute-start.4 = (bf16[512,128]{1,0:T(8,128)(2,1)S(1)}, bf16[512,128]{1,0:T(8,128)(2,1)S(1)}, u32[]{:S(2)}, u32[]{:S(2)}) collective-permute-start(bf16[512,128]{1,0:T(8,128)(2,1)S(1)} %get-tuple-element.31.refs_1_), channel_id=1, source_target_pairs={{2,0},{4,2},{6,4},{7,6},{5,7},{3,5},{1,3},{0,1},{10,8},{12,10},{14... | collective-permute-start | bytes 393224 | tf_op jit(solution)/shard_map/ppermute | solution.py:225
  2.5 8.6 %collective-permute-start.8 = (bf16[512,128]{1,0:T(8,128)(2,1)S(1)}, bf16[512,128]{1,0:T(8,128)(2,1)S(1)}, u32[]{:S(2)}, u32[]{:S(2)}) collective-permute-start(bf16[512,128]{1,0:T(8,128)(2,1)S(1)} %get-tuple-element.32.refs_0_), channel_id=1, source_target_pairs={{2,0},{4,2},{6,4},{7,6},{5,7},{3,5},{1,3},{0,1},{10,8},{12,10},{14... | collective-permute-start | bytes 393224 | tf_op jit(solution)/shard_map/ppermute | solution.py:225
  3.8 4.5 %collective-permute-start = (bf16[512,128]{1,0:T(8,128)(2,1)S(1)}, bf16[512,128]{1,0:T(8,128)(2,1)S(1)}, u32[]{:S(2)}, u32[]{:S(2)}) collective-permute-start(bf16[512,128]{1,0:T(8,128)(2,1)S(1)} %get-tuple-element.32.refs_0_), channel_id=1, source_target_pairs={{0,2},{2,4},{4,6},{6,7},{7,5},{5,3},{3,1},{1,0},{8,10},{10,12},{12... | collective-permute-start | bytes 393224 | tf_op jit(solution)/shard_map/ppermute | solution.py:221
  7.0 5.5 %collective-permute-start.5 = (bf16[512,128]{1,0:T(8,128)(2,1)S(1)}, bf16[512,128]{1,0:T(8,128)(2,1)S(1)}, u32[]{:S(2)}, u32[]{:S(2)}) collective-permute-start(bf16[512,128]{1,0:T(8,128)(2,1)S(1)} %collective-permute-done.4.refs_3_), channel_id=1, source_target_pairs={{2,0},{4,2},{6,4},{7,6},{5,7},{3,5},{1,3},{0,1},{10,8},{12,10},{14... | collective-permute-start | bytes 393224 | tf_op jit(solution)/shard_map/ppermute | solution.py:225
  8.3 5.5 %collective-permute-start.1 = (bf16[512,128]{1,0:T(8,128)(2,1)S(1)}, bf16[512,128]{1,0:T(8,128)(2,1)S(1)}, u32[]{:S(2)}, u32[]{:S(2)}) collective-permute-start(bf16[512,128]{1,0:T(8,128)(2,1)S(1)} %collective-permute-done.refs_0_), channel_id=1, source_target_pairs={{0,2},{2,4},{4,6},{6,7},{7,5},{5,3},{3,1},{1,0},{8,10},{10,12},{12... | collective-permute-start | bytes 393224 | tf_op jit(solution)/shard_map/ppermute | solution.py:221
  10.9 7.5 %collective-permute-start.12 = (bf16[512,128]{1,0:T(8,128)(2,1)S(1)}, bf16[512,128]{1,0:T(8,128)(2,1)S(1)}, u32[]{:S(2)}, u32[]{:S(2)}) collective-permute-start(bf16[512,128]{1,0:T(8,128)(2,1)S(1)} %collective-permute-done.11.refs_2_), channel_id=1, source_target_pairs={{0,2},{2,4},{4,6},{6,7},{7,5},{5,3},{3,1},{1,0},{8,10},{10,12},{12... | collective-permute-start | bytes 393224 | tf_op jit(solution)/shard_map/ppermute | solution.py:221
  11.1 7.5 %collective-permute-start.9 = (bf16[512,128]{1,0:T(8,128)(2,1)S(1)}, bf16[512,128]{1,0:T(8,128)(2,1)S(1)}, u32[]{:S(2)}, u32[]{:S(2)}) collective-permute-start(bf16[512,128]{1,0:T(8,128)(2,1)S(1)} %collective-permute-done.8.refs_1_), channel_id=1, source_target_pairs={{2,0},{4,2},{6,4},{7,6},{5,7},{3,5},{1,3},{0,1},{10,8},{12,10},{14... | collective-permute-start | bytes 393224 | tf_op jit(solution)/shard_map/ppermute | solution.py:225
  12.5 8.8 %collective-permute-start.6 = (bf16[512,128]{1,0:T(8,128)(2,1)S(1)}, bf16[512,128]{1,0:T(8,128)(2,1)S(1)}, u32[]{:S(2)}, u32[]{:S(2)}) collective-permute-start(bf16[512,128]{1,0:T(8,128)(2,1)S(1)} %collective-permute-done.5.refs_3_), channel_id=1, source_target_pairs={{2,0},{4,2},{6,4},{7,6},{5,7},{3,5},{1,3},{0,1},{10,8},{12,10},{14... | collective-permute-start | bytes 393224 | tf_op jit(solution)/shard_map/ppermute | solution.py:225
  13.8 8.8 %collective-permute-start.2 = (bf16[512,128]{1,0:T(8,128)(2,1)S(1)}, bf16[512,128]{1,0:T(8,128)(2,1)S(1)}, u32[]{:S(2)}, u32[]{:S(2)}) collective-permute-start(bf16[512,128]{1,0:T(8,128)(2,1)S(1)} %collective-permute-done.1.refs_0_), channel_id=1, source_target_pairs={{0,2},{2,4},{4,6},{6,7},{7,5},{5,3},{3,1},{1,0},{8,10},{10,12},{12... | collective-permute-start | bytes 393224 | tf_op jit(solution)/shard_map/ppermute | solution.py:221
  14.0 3.4 %copy-start = (bf16[2,4,8,4,128,128]{5,4,3,2,1,0:T(8,128)(2,1)S(1)}, bf16[2,4,8,4,128,128]{5,4,3,2,1,0:T(8,128)(2,1)}, u32[]{:S(2)}) copy-start(bf16[2,4,8,4,128,128]{5,4,3,2,1,0:T(8,128)(2,1)} %tiles.9) | copy-start | bytes 25165828
  18.4 5.8 %collective-permute-start.13 = (bf16[512,128]{1,0:T(8,128)(2,1)S(1)}, bf16[512,128]{1,0:T(8,128)(2,1)S(1)}, u32[]{:S(2)}, u32[]{:S(2)}) collective-permute-start(bf16[512,128]{1,0:T(8,128)(2,1)S(1)} %collective-permute-done.12.refs_2_), channel_id=1, source_target_pairs={{0,2},{2,4},{4,6},{6,7},{7,5},{5,3},{3,1},{1,0},{8,10},{10,12},{12... | collective-permute-start | bytes 393224 | tf_op jit(solution)/shard_map/ppermute | solution.py:221
  18.6 5.5 %collective-permute-start.10 = (bf16[512,128]{1,0:T(8,128)(2,1)S(1)}, bf16[512,128]{1,0:T(8,128)(2,1)S(1)}, u32[]{:S(2)}, u32[]{:S(2)}) collective-permute-start(bf16[512,128]{1,0:T(8,128)(2,1)S(1)} %collective-permute-done.9.refs_1_), channel_id=1, source_target_pairs={{2,0},{4,2},{6,4},{7,6},{5,7},{3,5},{1,3},{0,1},{10,8},{12,10},{14... | collective-permute-start | bytes 393224 | tf_op jit(solution)/shard_map/ppermute | solution.py:225
  21.3 4.2 %collective-permute-start.7 = (bf16[512,128]{1,0:T(8,128)(2,1)S(1)}, bf16[512,128]{1,0:T(8,128)(2,1)S(1)}, u32[]{:S(2)}, u32[]{:S(2)}) collective-permute-start(bf16[512,128]{1,0:T(8,128)(2,1)S(1)} %collective-permute-done.6.refs_3_), channel_id=1, source_target_pairs={{2,0},{4,2},{6,4},{7,6},{5,7},{3,5},{1,3},{0,1},{10,8},{12,10},{14... | collective-permute-start | bytes 393224 | tf_op jit(solution)/shard_map/ppermute | solution.py:225
  22.6 5.0 %collective-permute-start.3 = (bf16[512,128]{1,0:T(8,128)(2,1)S(1)}, bf16[512,128]{1,0:T(8,128)(2,1)S(1)}, u32[]{:S(2)}, u32[]{:S(2)}) collective-permute-start(bf16[512,128]{1,0:T(8,128)(2,1)S(1)} %collective-permute-done.2.refs_0_), channel_id=1, source_target_pairs={{0,2},{2,4},{4,6},{6,7},{7,5},{5,3},{3,1},{1,0},{8,10},{10,12},{12... | collective-permute-start | bytes 393224 | tf_op jit(solution)/shard_map/ppermute | solution.py:221
  25.5 7.5 %copy-start.1 = (bf16[512,1536]{1,0:T(8,128)(2,1)S(1)}, bf16[512,1536]{1,0:T(8,128)(2,1)}, u32[]{:S(2)}) copy-start(bf16[512,1536]{1,0:T(8,128)(2,1)} %w_input.3) | copy-start | bytes 4718596
  25.5 7.5 %copy-start.3 = (bf16[128,512]{1,0:T(8,128)(2,1)S(1)}, bf16[128,512]{1,0:T(8,128)(2,1)}, u32[]{:S(2)}) copy-start(bf16[128,512]{1,0:T(8,128)(2,1)} %w_graph.3) | copy-start | bytes 393220
  28.6 5.5 %collective-permute-start.14 = (bf16[2,256,128]{2,1,0:T(8,128)(2,1)S(1)}, bf16[2,256,128]{2,1,0:T(8,128)(2,1)S(1)}, u32[]{:S(2)}, u32[]{:S(2)}) collective-permute-start(bf16[2,256,128]{2,1,0:T(8,128)(2,1)S(1)} %get-tuple-element.18), channel_id=1, source_target_pairs={{0,8},{8,0},{16,24},{24,16},{1,9},{9,1},{17,25},{25,17},{2,10},{10... | collective-permute-start | bytes 393224 | tf_op jit(solution)/shard_map/ppermute | solution.py:232
  34.1 1.4 %copy-start.2 = (bf16[512,1536]{1,0:T(8,128)(2,1)S(1)}, bf16[512,1536]{1,0:T(8,128)(2,1)}, u32[]{:S(2)}) copy-start(bf16[512,1536]{1,0:T(8,128)(2,1)} %w_hidden.7) | copy-start | bytes 4718596
  34.1 1.4 %copy-start.4 = (f32[512]{0:T(512)S(1)}, f32[512]{0:T(512)}, u32[]{:S(2)}) copy-start(f32[512]{0:T(512)} %param.19) | copy-start | bytes 6148
  36.1 7.0 %collective-permute-start.16 = (bf16[128,512]{1,0:T(8,128)(2,1)S(1)}, bf16[128,512]{1,0:T(8,128)(2,1)S(1)}, u32[]{:S(2)}, u32[]{:S(2)}) collective-permute-start(bf16[128,512]{1,0:T(8,128)(2,1)S(1)} %get-tuple-element.23), channel_id=1, source_target_pairs={{0,16},{8,24},{1,17},{9,25},{2,18},{10,26},{3,19},{11,27},{4,20},{... | collective-permute-start | bytes 393224 | tf_op jit(solution)/shard_map/ppermute | solution.py:251
  38.0 8.8 %collective-permute-start.15 = (bf16[128,512]{1,0:T(8,128)(2,1)S(1)}, bf16[128,512]{1,0:T(8,128)(2,1)S(1)}, u32[]{:S(2)}, u32[]{:S(2)}) collective-permute-start(bf16[128,512]{1,0:T(8,128)(2,1)S(1)} %get-tuple-element.19), channel_id=1, source_target_pairs={{0,16},{8,24},{1,17},{9,25},{2,18},{10,26},{3,19},{11,27},{4,20},{... | collective-permute-start | bytes 393224 | tf_op jit(solution)/shard_map/ppermute | solution.py:251
  45.9 3.9 %collective-permute-start.18 = (bf16[2,128,512]{2,1,0:T(8,128)(2,1)S(1)}, bf16[2,128,512]{2,1,0:T(8,128)(2,1)S(1)}, u32[]{:S(2)}, u32[]{:S(2)}) collective-permute-start(bf16[2,128,512]{2,1,0:T(8,128)(2,1)S(1)} %get-tuple-element.28), channel_id=1, source_target_pairs={{0,8},{8,0},{16,24},{24,16},{1,9},{9,1},{17,25},{25,17},{2,10},{10... | collective-permute-start | bytes 786440 | tf_op jit(solution)/shard_map/ppermute | solution.py:252
  49.4 1.6 %collective-permute-start.17 = (bf16[2,128,512]{2,1,0:T(8,128)(2,1)S(1)}, bf16[2,128,512]{2,1,0:T(8,128)(2,1)S(1)}, u32[]{:S(2)}, u32[]{:S(2)}) collective-permute-start(bf16[2,128,512]{2,1,0:T(8,128)(2,1)S(1)} %get-tuple-element.27), channel_id=1, source_target_pairs={{0,8},{8,0},{16,24},{24,16},{1,9},{9,1},{17,25},{25,17},{2,10},{10... | collective-permute-start | bytes 786440 | tf_op jit(solution)/shard_map/ppermute | solution.py:252

commit v2 on v0

v2 whole, which is shorter than its diff:
```python
import functools

import jax
import jax.numpy as jnp
from jax import lax
from jax.experimental import pallas as pl
from jax.experimental.pallas import tpu as pltpu
from jax.sharding import PartitionSpec as P

BF16 = jnp.bfloat16
F32 = jnp.float32
CORES = 2
CHUNKS = 2
VMEM = pltpu.MemorySpace.VMEM
SMEM = pltpu.MemorySpace.SMEM


def ring_order(size):
    width = 1
    while width * width * 4 <= size:
        width *= 2
    depth = size // width
    walk = [(z, 0) for z in range(depth)]
    for step, z in enumerate(reversed(range(depth))):
        row = range(1, width) if step % 2 == 0 else reversed(range(1, width))
        walk += [(z, y) for y in row]
    return [z * width + y for z, y in walk]


def sigmoid(x):
    return 0.5 * jnp.tanh(0.5 * x) + 0.5


def params(mib=32):
    return pltpu.CompilerParams(vmem_limit_bytes=mib * 2**20)


def cost(flops, bytes_accessed):
    return pl.CostEstimate(flops=int(flops), bytes_accessed=int(bytes_accessed), transcendentals=0)


def where_am_i():
    me = lax.axis_index("tm")
    return lax.rem(me, CORES), lax.div(me, CORES)


def lookup(table, index):
    found = jnp.int32(table[0])
    for i, entry in enumerate(table[1:], 1):
        found = jnp.where(index == i, jnp.int32(entry), found)
    return found


def whole(memory=VMEM):
    return pl.BlockSpec(memory_space=memory)


def load_tiles(tiles, cols, counts, order):
    snaps, rows, parts, slots, blk, _ = tiles.shape
    half = rows // CORES
    spot = [0] * parts
    for i, d in enumerate(order):
        spot[d] = i

    def kernel(tiles, cols, counts, out, table, sems):
        core, _ = where_am_i()
        here = lookup(spot, lax.axis_index("dom"))
        parts_at = [lookup(order, lax.rem(here + step, parts)) for step in range(parts)]
        copies = []
        for snap in range(snaps):
            for step in range(parts):
                for h in range(CORES):
                    row = lax.rem(core + h, CORES) * half
                    copies.append(
                        pltpu.make_async_copy(
                            tiles.at[snap, pl.ds(row, half), parts_at[step]],
                            out.at[snap, pl.ds(h * half, half), step],
                            sems.at[snap, step, h],
                        )
                    )
                    copies[-1].start()

        def fill(at, carry):
            snap, rel = at // rows, at % rows
            row = lax.rem(rel + core * half, rows)
            for step in range(parts):
                count = counts[snap, row, parts_at[step]]
                for k in range(slots):
                    col = cols[snap, row, k, parts_at[step]]
                    table[(at * parts + step) * slots + k] = jnp.where(k < count, col, -1)
            return carry

        lax.fori_loop(0, snaps * rows, fill, 0)
        for copy in copies:
            copy.wait()

    return pl.pallas_call(
        kernel,
        out_shape=(
            jax.ShapeDtypeStruct(tiles.shape, tiles.dtype),
            jax.ShapeDtypeStruct((snaps * rows * parts * slots,), jnp.int32),
        ),
        in_specs=[whole(pltpu.MemorySpace.HBM), whole(SMEM), whole(SMEM)],
        out_specs=(whole(), whole(SMEM)),
        scratch_shapes=[pltpu.SemaphoreType.DMA((snaps, parts, CORES))],
        compiler_params=params(44),
        cost_estimate=cost(0, 2**20),
        name="load_tiles",
    )(tiles, jnp.swapaxes(cols, 2, 3), counts)


def picked(table, tiles, x_block, snap, rel, step, lhs, rhs):
    rows, parts, slots, blk = tiles.shape[1:5]
    for k in range(slots):
        col = table[((snap * rows + rel) * parts + step) * slots + k]
        block = x_block(pl.ds(pl.multiple_of(jnp.maximum(col, 0) * blk, blk), blk))
        rhs.append(jnp.where(col >= 0, block, jnp.zeros_like(block)))
        lhs.append(tiles[snap, rel, step, k])


def product(lhs, rhs):
    return jnp.dot(jnp.concatenate(lhs, axis=1), jnp.concatenate(rhs, axis=0), preferred_element_type=F32)


def spmm(table, tiles, xs, steps, acc, beside=()):
    snaps, rows, parts, slots, blk, _ = tiles.shape
    feats = xs[0].shape[-1]
    first = acc is None
    joint = xs[0].ndim == 3

    def kernel(table, tiles, *refs):
        x_refs, rest = refs[: len(xs)], refs[len(xs) :]
        out = rest[-1]
        for snap in range(snaps):
            for rel in range(rows):
                lhs, rhs = [], []
                for i, step in enumerate(steps):
                    x = x_refs[i].at[snap] if joint else x_refs[i * snaps + snap]
                    picked(table, tiles, lambda at: x[at, :], snap, rel, step, lhs, rhs)
                total = product(lhs, rhs)
                out[snap, rel] = total if first else total + rest[0][snap, rel]

    operands = [table, tiles, *xs] + ([] if first else [acc]) + list(beside)
    return pl.pallas_call(
        kernel,
        out_shape=jax.ShapeDtypeStruct((snaps, rows, blk, feats), F32),
        in_specs=[whole(SMEM)] + [whole()] * (len(operands) - 1),
        out_specs=whole(),
        compiler_params=params(),
        cost_estimate=cost(2 * len(steps) * snaps * rows * slots * blk * blk * feats * 4, 2**20),
        name="spmm",
    )(*operands)


def spmm_last(table, tiles, x, snap, step, acc):
    snaps, rows, parts, slots, blk, _ = tiles.shape
    feats = x.shape[-1]
    half = rows // CORES

    def kernel(table, tiles, x_ref, acc_in, *outs):
        for rel in range(rows):
            lhs, rhs = [], []
            picked(table, tiles, lambda at: x_ref[at, :], snap, rel, step, lhs, rhs)
            total = product(lhs, rhs) + acc_in[snap, rel]
            outs[rel // half][(rel % half) * blk : (rel % half + 1) * blk, :] = total.astype(BF16)

    part = jax.ShapeDtypeStruct((half * blk, feats), BF16)
    return pl.pallas_call(
        kernel,
        out_shape=(part, part),
        in_specs=[whole(SMEM)] + [whole()] * 3,
        out_specs=(whole(), whole()),
        compiler_params=params(),
        cost_estimate=cost(2 * rows * slots * blk * blk * feats * 4, 2**20),
        name="spmm_last",
    )(table, tiles, x, acc)


def write_gates(axs, w_graph, w_input, out):
    snaps, rows = len(axs), axs[0].shape[0]
    hid, width = w_input.shape
    graph = jnp.dot(jnp.concatenate(axs, axis=0), w_graph[...], preferred_element_type=F32)
    graph = jnp.maximum(graph, 0.0).astype(BF16)
    for j in range(0, width, hid):
        part = jnp.dot(graph, w_input[:, j : j + hid], preferred_element_type=F32)
        out[:, :, j : j + hid] = part.reshape(snaps, rows, hid)


def gates(axs, w_graph, w_input):
    snaps, rows = len(axs), axs[0].shape[0]
    hid, width = w_input.shape

    def kernel(*refs):
        write_gates([ref[...] for ref in refs[:snaps]], *refs[snaps:])

    return pl.pallas_call(
        kernel,
        out_shape=jax.ShapeDtypeStruct((snaps, rows, width), F32),
        in_specs=[whole()] * (snaps + 2),
        out_specs=whole(),
        compiler_params=params(),
        cost_estimate=cost(2 * snaps * rows * hid * width * 2, 2**20),
        name="gates",
    )(*axs, w_graph, w_input)


def run_steps(state, given_first, given_second, outs_first, outs_second, w_hidden, bias, state_out):
    hid = w_hidden.shape[0]
    block = min(256, hid)
    snaps = outs_first.shape[0]
    for step in range(CORES * snaps):
        s = step % snaps
        given, out = (given_first, outs_first) if step < snaps else (given_second, outs_second)
        low = state.astype(BF16)
        parts = []
        for j in range(0, hid, block):
            gh_r, gh_c, gh_u = (
                jnp.dot(low, w_hidden[:, g * hid + j : g * hid + j + block], preferred_element_type=F32)
                for g in (0, 2, 1)
            )
            gx_r, gx_u, gx_c = (given(s, slice(g * hid + j, g * hid + j + block)) for g in (0, 1, 2))
            reset = sigmoid(gx_r + gh_r)
            cand = jnp.tanh(gx_c + reset * gh_c)
            update = sigmoid(gx_u + gh_u + bias[:, j : j + block])
            parts.append(update * state[:, j : j + block] + (1.0 - update) * cand)
        state = jnp.concatenate(parts, axis=1)
        out[s] = state.astype(BF16)
    if state_out is not None:
        state_out[...] = state.astype(BF16)


def recurrence_first(hidden_start, gx_own, axs_other, w_graph, w_input, w_hidden, bias, chunk):
    snaps, mine, width = gx_own.shape
    feats, hid = w_graph.shape
    rows = mine // CHUNKS

    def kernel(hidden_start, gx_own, w_graph, w_input, w_hidden, bias, *refs):
        axs, (state_out, keep, send, gx_other) = refs[:snaps], refs[snaps:]
        core, place = where_am_i()
        at = slice(chunk * rows, (chunk + 1) * rows)
        write_gates([ref[at, :] for ref in axs], w_graph, w_input, gx_other)
        own = lambda s, columns: gx_own[s, at, columns]
        other = lambda s, columns: gx_other[s, :, columns]

        @pl.when((place == 0) & (core == 0))
        def _():
            state = hidden_start[chunk * rows : (chunk + 1) * rows, :]
            run_steps(state, own, other, keep, send, w_hidden, bias, state_out)

        @pl.when((place == 0) & (core != 0))
        def _():
            state = hidden_start[mine + chunk * rows : mine + (chunk + 1) * rows, :]
            run_steps(state, other, own, send, keep, w_hidden, bias, state_out)

    part = jax.ShapeDtypeStruct((snaps, rows, hid), BF16)
    return pl.pallas_call(
        kernel,
        out_shape=(
            jax.ShapeDtypeStruct((rows, hid), BF16),
            part,
            part,
            jax.ShapeDtypeStruct((snaps, rows, width), F32),
        ),
        in_specs=[whole()] * (6 + snaps),
        out_specs=(whole(),) * 4,
        compiler_params=params(),
        cost_estimate=cost(2 * CORES * snaps * rows * hid * 3 * hid * 4, 2**20),
        name="recurrence_first",
    )(hidden_start, gx_own, w_graph, w_input, w_hidden, bias, *axs_other)


def recurrence_later(state, gx_own, gx_other, w_hidden, bias, before, phase, chunk, last):
    snaps, rows, width = gx_other.shape
    hid = w_hidden.shape[0]

    def kernel(state_in, gx_own, gx_other, w_hidden, bias, keep_in, send_in, keep, send, state_out=None):
        core, place = where_am_i()
        at = slice(chunk * rows, (chunk + 1) * rows)
        own = lambda s, columns: gx_own[s, at, columns]
        other = lambda s, columns: gx_other[s, :, columns]

        @pl.when((place == phase) & (core == 0))
        def _():
            run_steps(state_in[...].astype(F32), own, other, keep, send, w_hidden, bias, state_out)

        @pl.when((place == phase) & (core != 0))
        def _():
            run_steps(state_in[...].astype(F32), other, own, send, keep, w_hidden, bias, state_out)

        @pl.when(place != phase)
        def _():
            keep[...] = keep_in[...]
            send[...] = send_in[...]

    part = jax.ShapeDtypeStruct((snaps, rows, hid), BF16)
    return pl.pallas_call(
        kernel,
        out_shape=(part, part) + (() if last else (jax.ShapeDtypeStruct((rows, hid), BF16),)),
        in_specs=[whole()] * 7,
        out_specs=(whole(),) * (2 if last else 3),
        compiler_params=params(),
        cost_estimate=cost(2 * CORES * snaps * rows * hid * 3 * hid * 4, 2**20),
        name="recurrence_later",
    )(state, gx_own, gx_other, w_hidden, bias, *before)


def write_out(out, pieces, nodes):
    snaps, rows, hid = pieces[0][0].shape
    shape = jax.ShapeDtypeStruct((snaps, nodes, hid), BF16)
    count = len(pieces)

    def kernel(*refs):
        sources, target, sems = refs[:count], refs[-2], refs[-1]
        core, _ = where_am_i()
        copies = []
        for i, (_, own, chunk) in enumerate(pieces):
            half = core if own else 1 - core
            start = pl.multiple_of(half * (nodes // CORES) + chunk * rows, rows)
            copies.append(pltpu.make_async_copy(sources[i], target.at[:, pl.ds(start, rows), :], sems.at[i]))
            copies[-1].start()
        for copy in copies:
            copy.wait()

    operands = [array for array, _, _ in pieces] + ([] if out is None else [out])
    return pl.pallas_call(
        kernel,
        out_shape=shape,
        in_specs=[whole()] * count + ([] if out is None else [whole(pl.ANY)]),
        out_specs=whole(pl.ANY),
        scratch_shapes=[pltpu.SemaphoreType.DMA((count,))],
        input_output_aliases={} if out is None else {count: 0},
        compiler_params=params(),
        cost_estimate=cost(0, 2**20),
        name="write_out",
    )(*operands)


def per_device(
    features, tile_values, tile_cols, tile_count, hidden_start, w_graph, w_input, w_hidden, update_bias
):
    snaps, nodes, feats = features.shape
    parts = lax.axis_size("dom")
    sections = lax.axis_size("tm")
    places = sections // CORES
    order = ring_order(parts)
    ahead = [(order[i], order[(i + 1) % parts]) for i in range(parts)]
    back = [(b, a) for a, b in ahead]

    far = parts // 2
    tiles, table = load_tiles(tile_values, tile_cols, tile_count, order)
    forward = lax.ppermute(features, "dom", ahead)
    reverse = lax.ppermute(features, "dom", back)
    forward, tiles, table = lax.optimization_barrier((forward, tiles, table))
    waiting = [([features, forward, reverse], [0, parts - 1, 1])]
    forward = [forward[s] for s in range(snaps)]
    reverse = [reverse[s] for s in range(snaps)]
    acc = None
    beside = [w_graph, w_input, w_hidden, hidden_start]
    for hop in range(2, far):
        for turn in range(2):
            for s in range(snaps):
                if s % 2 == turn:
                    forward[s] = lax.ppermute(forward[s], "dom", ahead)
                else:
                    reverse[s] = lax.ppermute(reverse[s], "dom", back)
        waiting.append((forward + reverse, [parts - hop, hop]))
        if hop > 2:
            acc = spmm(table, tiles, *waiting.pop(0), acc)
            first = [forward[s] if s % 2 == 0 else reverse[s] for s in range(snaps)]
            first, acc = lax.optimization_barrier((first, acc))
            forward = [first[s] if s % 2 == 0 else forward[s] for s in range(snaps)]
            reverse = [first[s] if s % 2 == 1 else reverse[s] for s in range(snaps)]
    arriving = [
        lax.ppermute(forward[s], "dom", ahead) if s % 2 == 0 else lax.ppermute(reverse[s], "dom", back)
        for s in range(snaps)
    ]
    while waiting:
        xs, steps = waiting.pop(0)
        acc = spmm(table, tiles, xs, steps, acc, [] if waiting else beside)
    swap = [(t, t ^ 1) for t in range(sections)]
    keep_ax, other_ax = [], []
    for s in range(snaps):
        keep, send = spmm_last(table, tiles, arriving[s], s, far, acc)
        keep_ax.append(keep)
        other_ax.append(lax.ppermute(send, "tm", swap))
    gx_own = gates(keep_ax, w_graph, w_input)

    bias = update_bias.reshape(1, -1)
    onward = [(t, t + CORES) for t in range(sections - CORES)]
    hidden, states, gx_other = [], [], []
    for chunk in range(CHUNKS):
        state, keep, send, gx = recurrence_first(
            hidden_start, gx_own, other_ax, w_graph, w_input, w_hidden, bias, chunk
        )
        hidden.append((keep, send))
        states.append(state)
        gx_other.append(gx)
    for phase in range(1, places):
        states = [lax.ppermute(state, "tm", onward) for state in states]
        for chunk in range(CHUNKS):
            last = phase == places - 1
            hidden[chunk] = recurrence_later(
                states[chunk], gx_own, gx_other[chunk], w_hidden, bias, hidden[chunk], phase, chunk, last
            )
            if not last:
                *hidden[chunk], states[chunk] = hidden[chunk]
    pieces = [(keep, True, chunk) for chunk, (keep, _) in enumerate(hidden)]
    pieces += [(lax.ppermute(send, "tm", swap), False, chunk) for chunk, (_, send) in enumerate(hidden)]
    out = write_out(None, pieces[:-1], nodes)
    return write_out(out, pieces[-1:], nodes)


def solution(mesh):
    placed = (
        P("tm", "dom", None),
        P("tm", "dom", None, None, None, None),
        P("tm", "dom", None, None),
        P("tm", "dom", None),
        P("dom", None),
        P(),
        P(),
        P(),
        P(),
    )
    return jax.shard_map(
        per_device, mesh=mesh, in_specs=placed, out_specs=P("tm", "dom", None), check_vma=False
    )
```

time: 265 us -> 46.8 us (0.18)
  the two profiles are of different devices: /device:TPU:0 before, /device:TPU:15 now
where the time goes in v2:
time: 46.8 us; the launch traced here: 46.5 us
  starting transfers between devices  18.9 us (40%)
  Pallas kernels  18.1 us (39%)
  waiting for transfers between devices  7.55 us (16%)
  local copies, waits for them, and re-layouts  1.47 us (3%)
    ppermute x2, starting transfers between devices, per_device(): other_ax.append(lax.ppermute(send, 'tm', swap))  5.46 us
    ppermute x4, starting transfers between devices, per_device(): reverse[s] = lax.ppermute(reverse[s], 'dom', back)  5.24 us
    pallas_call x1, Pallas kernels, load_tiles(): pl.pallas_call(kernel, out_shape=(jax.ShapeDtypeStruct(tiles.shape, tiles...  5.14 us
    ppermute x2, waiting for transfers between devices, per_device(): states = [lax.ppermute(state, 'tm', onward) for state in states]  4.65 us
    pallas_call x3, Pallas kernels, spmm(): pl.pallas_call(kernel, out_shape=jax.ShapeDtypeStruct((snaps, rows, blk,...  4.2 us
    pallas_call x2, Pallas kernels, recurrence_later(): pl.pallas_call(kernel, out_shape=(part, part) + (() if last else (jax.Sha...  2.93 us
    ppermute x2, starting transfers between devices, per_device(): states = [lax.ppermute(state, 'tm', onward) for state in states]  2.58 us
    ppermute x4, waiting for transfers between devices, per_device(): forward[s] = lax.ppermute(forward[s], 'dom', ahead)  2.36 us
  transfers between devices with their start and end apart: 18, of which 7 were waited for; matrix products, arithmetic and copies ran while one was open for 0% of the time, Pallas kernels for 36%

profile of v2, /device:TPU:15, one launch (start us, length us, event | category | flops | bytes accessed | tf_op | source)
XLA Modules:
  0.0 46.5 jit_solution(15166022223937681182)
XLA Ops:
  0.2 1.3 %collective-permute-start.3 = (bf16[2,512,128]{2,1,0:T(8,128)(2,1)}, bf16[2,512,128]{2,1,0:T(8,128)(2,1)S(1)}, u32[]{:S(2)}, u32[]{:S(2)}) collective-permute-start(bf16[2,512,128]{2,1,0:T(8,128)(2,1)} %refs_0_.1), channel_id=1, source_target_pairs={{2,0},{4,2},{6,4},{7,6},{5,7},{3,5},{1,3},{0,1},{10,8},{12,10},{14... | collective-permute-start | bytes 786440 | tf_op jit(solution)/shard_map/ppermute | solution.py:352
  1.5 0.7 %copy-done.5 = s32[2,4,8,4]{2,3,1,0:T(4,128)S(1)} copy-done((s32[2,4,8,4]{2,3,1,0:T(4,128)S(1)}, s32[2,4,8,4]{2,3,1,0:T(4,128)}, u32[]{:S(2)}) %copy-start.5) | copy-done | bytes 1048
  2.2 0.7 %copy-done.6 = s32[2,4,8]{2,1,0:T(4,128)S(1)} copy-done((s32[2,4,8]{2,1,0:T(4,128)S(1)}, s32[2,4,8]{2,1,0:T(4,128)}, u32[]{:S(2)}) %copy-start.6) | copy-done | bytes 280
  2.9 5.1 %load_tiles.1 = (bf16[2,4,8,4,128,128]{5,4,3,2,1,0:T(8,128)(2,1)S(1)}, s32[256]{0:T(256)S(1)}) custom-call(bf16[2,4,8,4,128,128]{5,4,3,2,1,0:T(8,128)(2,1)} %tiles.1, s32[2,4,4,8]{3,2,1,0:T(4,128)S(1)} %bitcast.10, s32[2,4,8]{2,1,0:T(4,128)S(1)} %copy-done.6), custom_call_target="tpu_custom_call" | custom-call | bytes 1048576 | tf_op jit(solution)/shard_map/load_tiles/pallas_call | solution.py:97
  8.3 1.3 %collective-permute-start.4 = (bf16[512,128]{1,0:T(8,128)(2,1)S(1)}, bf16[512,128]{1,0:T(8,128)(2,1)S(1)}, u32[]{:S(2)}, u32[]{:S(2)}) collective-permute-start(bf16[512,128]{1,0:T(8,128)(2,1)S(1)} %get-tuple-element.54), channel_id=1, source_target_pairs={{2,0},{4,2},{6,4},{7,6},{5,7},{3,5},{1,3},{0,1},{10,8},{12,10},{14... | collective-permute-start | bytes 393224 | tf_op jit(solution)/shard_map/ppermute | solution.py:365
  9.8 1.3 %collective-permute-start.9 = (bf16[512,128]{1,0:T(8,128)(2,1)S(1)}, bf16[512,128]{1,0:T(8,128)(2,1)S(1)}, u32[]{:S(2)}, u32[]{:S(2)}) collective-permute-start(bf16[512,128]{1,0:T(8,128)(2,1)S(1)} %get-tuple-element.53), channel_id=1, source_target_pairs={{2,0},{4,2},{6,4},{7,6},{5,7},{3,5},{1,3},{0,1},{10,8},{12,10},{14... | collective-permute-start | bytes 393224 | tf_op jit(solution)/shard_map/ppermute | solution.py:365
  11.1 0.8 %collective-permute-done.1.refs_0_ = bf16[512,128]{1,0:T(8,128)(2,1)S(1)} collective-permute-done((bf16[512,128]{1,0:T(8,128)(2,1)S(1)}, bf16[512,128]{1,0:T(8,128)(2,1)S(1)}, u32[]{:S(2)}, u32[]{:S(2)}) %collective-permute-start.1) | collective-permute-done | bytes 131104 | tf_op jit(solution)/shard_map/ppermute | solution.py:363
  12.2 1.3 %collective-permute-start.5 = (bf16[512,128]{1,0:T(8,128)(2,1)S(1)}, bf16[512,128]{1,0:T(8,128)(2,1)S(1)}, u32[]{:S(2)}, u32[]{:S(2)}) collective-permute-start(bf16[512,128]{1,0:T(8,128)(2,1)S(1)} %collective-permute-done.4.refs_3_), channel_id=1, source_target_pairs={{2,0},{4,2},{6,4},{7,6},{5,7},{3,5},{1,3},{0,1},{10,8},{12,10},{14... | collective-permute-start | bytes 393224 | tf_op jit(solution)/shard_map/ppermute | solution.py:365
  13.5 1.5 %collective-permute-done.7.refs_1_ = bf16[512,128]{1,0:T(8,128)(2,1)S(1)} collective-permute-done((bf16[512,128]{1,0:T(8,128)(2,1)S(1)}, bf16[512,128]{1,0:T(8,128)(2,1)S(1)}, u32[]{:S(2)}, u32[]{:S(2)}) %collective-permute-start.7) | collective-permute-done | bytes 131104 | tf_op jit(solution)/shard_map/ppermute | solution.py:363
  15.2 1.3 %collective-permute-start.10 = (bf16[512,128]{1,0:T(8,128)(2,1)S(1)}, bf16[512,128]{1,0:T(8,128)(2,1)S(1)}, u32[]{:S(2)}, u32[]{:S(2)}) collective-permute-start(bf16[512,128]{1,0:T(8,128)(2,1)S(1)} %collective-permute-done.9.refs_2_), channel_id=1, source_target_pairs={{2,0},{4,2},{6,4},{7,6},{5,7},{3,5},{1,3},{0,1},{10,8},{12,10},{14... | collective-permute-start | bytes 393224 | tf_op jit(solution)/shard_map/ppermute | solution.py:365
  16.5 1.6 %spmm.3.refs_4_ = f32[2,4,128,128]{3,2,1,0:T(8,128)S(1)} custom-call(s32[256]{0:T(256)S(1)} %get-tuple-element.31.table, bf16[2,4,8,4,128,128]{5,4,3,2,1,0:T(8,128)(2,1)S(1)} %get-tuple-element.32.tiles, bf16[2,512,128]{2,1,0:T(8,128)(2,1)S(1)} %copy-done.3, bf16[2,512,128]{2,1,0:T(8,128)(2,1)S(1)} %collective-permute-done.refs_1_, ...), custom_call_target="tpu_custom_call" | custom-call | flops 1610612736 | bytes 1048576 | tf_op jit(solution)/shard_map/spmm/pallas_call | solution.py:144
  18.2 1.4 %collective-permute-start.11 = (bf16[512,128]{1,0:T(8,128)(2,1)S(1)}, bf16[512,128]{1,0:T(8,128)(2,1)S(1)}, u32[]{:S(2)}, u32[]{:S(2)}) collective-permute-start(bf16[512,128]{1,0:T(8,128)(2,1)S(1)} %collective-permute-done.5.refs_3_), channel_id=1, source_target_pairs={{2,0},{4,2},{6,4},{7,6},{5,7},{3,5},{1,3},{0,1},{10,8},{12,10},{14... | collective-permute-start | bytes 393224 | tf_op jit(solution)/shard_map/ppermute | solution.py:374
  19.7 1.3 %spmm.4.refs_4_ = f32[2,4,128,128]{3,2,1,0:T(8,128)S(1)} custom-call(s32[256]{0:T(256)S(1)} %get-tuple-element.31.table, bf16[2,4,8,4,128,128]{5,4,3,2,1,0:T(8,128)(2,1)S(1)} %get-tuple-element.32.tiles, bf16[512,128]{1,0:T(8,128)(2,1)S(1)} %collective-permute-done.1.refs_0_, bf16[512,128]{1,0:T(8,128)(2,1)S(1)} %collective-permute-done.7.refs_1_, ...), custom_call_target="tpu_custom_call" | custom-call | flops 1073741824 | bytes 1048576 | tf_op jit(solution)/shard_map/spmm/pallas_call | solution.py:144
  21.1 1.3 %spmm.5.acc_in = f32[2,4,128,128]{3,2,1,0:T(8,128)S(1)} custom-call(s32[256]{0:T(256)S(1)} %get-tuple-element.31.table, bf16[2,4,8,4,128,128]{5,4,3,2,1,0:T(8,128)(2,1)S(1)} %get-tuple-element.32.tiles, bf16[512,128]{1,0:T(8,128)(2,1)S(1)} %collective-permute-done.2.refs_0_, bf16[512,128]{1,0:T(8,128)(2,1)S(1)} %collective-permute-done.8.refs_1_, ...), custom_call_target="tpu_custom_call" | custom-call | flops 1073741824 | bytes 1048576 | tf_op jit(solution)/shard_map/spmm/pallas_call | solution.py:144
  22.6 0.9 %spmm_last.3 = (bf16[256,128]{1,0:T(8,128)(2,1)S(1)}, bf16[256,128]{1,0:T(8,128)(2,1)S(1)}) custom-call(s32[256]{0:T(256)S(1)} %get-tuple-element.31.table, bf16[2,4,8,4,128,128]{5,4,3,2,1,0:T(8,128)(2,1)S(1)} %get-tuple-element.32.tiles, bf16[512,128]{1,0:T(8,128)(2,1)S(1)} %collective-permute-done.11.x_ref, f32[2,4,128,128]{3,2,1,0:T(8,128)S(1)} %spmm.5.acc_in), custom_call_target="tpu_custom_call" | custom-call | flops 268435456 | bytes 1048576 | tf_op jit(solution)/shard_map/spmm_last/pallas_call | solution.py:168
  23.4 4.8 %collective-permute-start.13 = (bf16[256,128]{1,0:T(8,128)(2,1)S(1)}, bf16[256,128]{1,0:T(8,128)(2,1)S(1)}, u32[]{:S(2)}, u32[]{:S(2)}) collective-permute-start(bf16[256,128]{1,0:T(8,128)(2,1)S(1)} %get-tuple-element.40), channel_id=1, source_target_pairs={{0,8},{8,0},{16,24},{24,16},{1,9},{9,1},{17,25},{25,17},{2,10},{10... | collective-permute-start | bytes 196616 | tf_op jit(solution)/shard_map/ppermute | solution.py:385
  28.2 0.9 %spmm_last.2 = (bf16[256,128]{1,0:T(8,128)(2,1)S(1)}, bf16[256,128]{1,0:T(8,128)(2,1)S(1)}) custom-call(s32[256]{0:T(256)S(1)} %get-tuple-element.31.table, bf16[2,4,8,4,128,128]{5,4,3,2,1,0:T(8,128)(2,1)S(1)} %get-tuple-element.32.tiles, bf16[512,128]{1,0:T(8,128)(2,1)S(1)} %collective-permute-done.6.x_ref, f32[2,4,128,128]{3,2,1,0:T(8,128)S(1)} %spmm.5.acc_in), custom_call_target="tpu_custom_call" | custom-call | flops 268435456 | bytes 1048576 | tf_op jit(solution)/shard_map/spmm_last/pallas_call | solution.py:168
  29.1 0.7 %collective-permute-start.12 = (bf16[256,128]{1,0:T(8,128)(2,1)S(1)}, bf16[256,128]{1,0:T(8,128)(2,1)S(1)}, u32[]{:S(2)}, u32[]{:S(2)}) collective-permute-start(bf16[256,128]{1,0:T(8,128)(2,1)S(1)} %get-tuple-element.39), channel_id=1, source_target_pairs={{0,8},{8,0},{16,24},{24,16},{1,9},{9,1},{17,25},{25,17},{2,10},{10... | collective-permute-start | bytes 196616 | tf_op jit(solution)/shard_map/ppermute | solution.py:385
  29.8 1.1 %gates.1.gx_own = f32[2,256,1536]{2,1,0:T(8,128)S(1)} custom-call(bf16[256,128]{1,0:T(8,128)(2,1)S(1)} %get-tuple-element.36.refs_0_, bf16[256,128]{1,0:T(8,128)(2,1)S(1)} %get-tuple-element.38.refs_1_, bf16[128,512]{1,0:T(8,128)(2,1)S(1)} %copy-done.4, bf16[512,1536]{1,0:T(8,128)(2,1)S(1)} %copy-done), custom_call_target="tpu_custom_call" | custom-call | flops 1610612736 | bytes 1048576 | tf_op jit(solution)/shard_map/gates/pallas_call | solution.py:196
  30.9 0.7 %recurrence_first.3 = (bf16[128,512]{1,0:T(8,128)(2,1)S(1)}, bf16[2,128,512]{2,1,0:T(8,128)(2,1)S(1)}, bf16[2,128,512]{2,1,0:T(8,128)(2,1)S(1)}, f32[2,128,1536]{2,1,0:T(8,128)S(1)}) custom-call(f32[512,512]{1,0:T(8,128)S(1)} %copy-done.2, f32[2,256,1536]{2,1,0:T(8,128)S(1)} %gates.1.gx_own, bf16[128,512]{1,0:T(8,128)(2,1)S(1)} %copy-done.4, ...), custom_call_target="tpu_custom_call" | custom-call | flops 3221225472 | bytes 1048576 | tf_op jit(solution)/shard_map/recurrence_first/pallas_call | solution.py:256
  31.6 1.3 %collective-permute-start.16 = (bf16[128,512]{1,0:T(8,128)(2,1)S(1)}, bf16[128,512]{1,0:T(8,128)(2,1)S(1)}, u32[]{:S(2)}, u32[]{:S(2)}) collective-permute-start(bf16[128,512]{1,0:T(8,128)(2,1)S(1)} %get-tuple-element.46), channel_id=1, source_target_pairs={{0,16},{8,24},{1,17},{9,25},{2,18},{10,26},{3,19},{11,27},{4,20},{... | collective-permute-start | bytes 393224 | tf_op jit(solution)/shard_map/ppermute | solution.py:399
  32.9 0.7 %recurrence_first.2 = (bf16[128,512]{1,0:T(8,128)(2,1)S(1)}, bf16[2,128,512]{2,1,0:T(8,128)(2,1)S(1)}, bf16[2,128,512]{2,1,0:T(8,128)(2,1)S(1)}, f32[2,128,1536]{2,1,0:T(8,128)S(1)}) custom-call(f32[512,512]{1,0:T(8,128)S(1)} %copy-done.2, f32[2,256,1536]{2,1,0:T(8,128)S(1)} %gates.1.gx_own, bf16[128,512]{1,0:T(8,128)(2,1)S(1)} %copy-done.4, ...), custom_call_target="tpu_custom_call" | custom-call | flops 3221225472 | bytes 1048576 | tf_op jit(solution)/shard_map/recurrence_first/pallas_call | solution.py:256
  33.6 1.3 %collective-permute-start.14 = (bf16[128,512]{1,0:T(8,128)(2,1)S(1)}, bf16[128,512]{1,0:T(8,128)(2,1)S(1)}, u32[]{:S(2)}, u32[]{:S(2)}) collective-permute-start(bf16[128,512]{1,0:T(8,128)(2,1)S(1)} %get-tuple-element.41), channel_id=1, source_target_pairs={{0,16},{8,24},{1,17},{9,25},{2,18},{10,26},{3,19},{11,27},{4,20},{... | collective-permute-start | bytes 393224 | tf_op jit(solution)/shard_map/ppermute | solution.py:399
  34.9 3.7 %collective-permute-done.16.state_in = bf16[128,512]{1,0:T(8,128)(2,1)S(1)} collective-permute-done((bf16[128,512]{1,0:T(8,128)(2,1)S(1)}, bf16[128,512]{1,0:T(8,128)(2,1)S(1)}, u32[]{:S(2)}, u32[]{:S(2)}) %collective-permute-start.16) | collective-permute-done | bytes 131104 | tf_op jit(solution)/shard_map/ppermute | solution.py:399
  38.6 1.5 %recurrence_later.3 = (bf16[2,128,512]{2,1,0:T(8,128)(2,1)S(1)}, bf16[2,128,512]{2,1,0:T(8,128)(2,1)S(1)}) custom-call(bf16[128,512]{1,0:T(8,128)(2,1)S(1)} %collective-permute-done.16.state_in, f32[2,256,1536]{2,1,0:T(8,128)S(1)} %gates.1.gx_own, f32[2,128,1536]{2,1,0:T(8,128)S(1)} %get-tuple-element.47.gx_other, bf16[512,1536]{1,0:T(8,128)(2,1)S(1)} %copy-done.1, ...), custom_call_target="tpu_custom_call" | custom-call | flops 3221225472 | bytes 1048576 | tf_op jit(solution)/shard_map/recurrence_later/pallas_call | solution.py:296
  40.1 0.9 %collective-permute-start.17 = (bf16[2,128,512]{2,1,0:T(8,128)(2,1)S(1)}, bf16[2,128,512]{2,1,0:T(8,128)(2,1)S(1)}, u32[]{:S(2)}, u32[]{:S(2)}) collective-permute-start(bf16[2,128,512]{2,1,0:T(8,128)(2,1)S(1)} %get-tuple-element.52), channel_id=1, source_target_pairs={{0,8},{8,0},{16,24},{24,16},{1,9},{9,1},{17,25},{25,17},{2,10},{10... | collective-permute-start | bytes 786440 | tf_op jit(solution)/shard_map/ppermute | solution.py:408
  41.0 1.0 %collective-permute-done.14.state_in = bf16[128,512]{1,0:T(8,128)(2,1)S(1)} collective-permute-done((bf16[128,512]{1,0:T(8,128)(2,1)S(1)}, bf16[128,512]{1,0:T(8,128)(2,1)S(1)}, u32[]{:S(2)}, u32[]{:S(2)}) %collective-permute-start.14) | collective-permute-done | bytes 131104 | tf_op jit(solution)/shard_map/ppermute | solution.py:399
  42.0 1.5 %recurrence_later.2 = (bf16[2,128,512]{2,1,0:T(8,128)(2,1)S(1)}, bf16[2,128,512]{2,1,0:T(8,128)(2,1)S(1)}) custom-call(bf16[128,512]{1,0:T(8,128)(2,1)S(1)} %collective-permute-done.14.state_in, f32[2,256,1536]{2,1,0:T(8,128)S(1)} %gates.1.gx_own, f32[2,128,1536]{2,1,0:T(8,128)S(1)} %get-tuple-element.42.gx_other, bf16[512,1536]{1,0:T(8,128)(2,1)S(1)} %copy-done.1, ...), custom_call_target="tpu_custom_call" | custom-call | flops 3221225472 | bytes 1048576 | tf_op jit(solution)/shard_map/recurrence_later/pallas_call | solution.py:296
  43.5 1.0 %collective-permute-start.15 = (bf16[2,128,512]{2,1,0:T(8,128)(2,1)S(1)}, bf16[2,128,512]{2,1,0:T(8,128)(2,1)S(1)}, u32[]{:S(2)}, u32[]{:S(2)}) collective-permute-start(bf16[2,128,512]{2,1,0:T(8,128)(2,1)S(1)} %get-tuple-element.45), channel_id=1, source_target_pairs={{0,8},{8,0},{16,24},{24,16},{1,9},{9,1},{17,25},{25,17},{2,10},{10... | collective-permute-start | bytes 786440 | tf_op jit(solution)/shard_map/ppermute | solution.py:408
  44.5 0.9 %write_out.2.refs_1_ = bf16[2,512,512]{2,1,0:T(8,128)(2,1)} custom-call(bf16[2,128,512]{2,1,0:T(8,128)(2,1)S(1)} %get-tuple-element.50.refs_0_, bf16[2,128,512]{2,1,0:T(8,128)(2,1)S(1)} %get-tuple-element.51.refs_1_, bf16[2,128,512]{2,1,0:T(8,128)(2,1)S(1)} %collective-permute-done.17.refs_2_), custom_call_target="tpu_custom_call" | custom-call | bytes 1048576 | tf_op jit(solution)/shard_map/write_out/pallas_call | solution.py:325
  45.4 0.3 collective-permute-done.15.refs_0_
  45.6 0.7 %write_out.3 = bf16[2,512,512]{2,1,0:T(8,128)(2,1)} custom-call(bf16[2,128,512]{2,1,0:T(8,128)(2,1)S(1)} %collective-permute-done.15.refs_0_, bf16[2,512,512]{2,1,0:T(8,128)(2,1)} %write_out.2.refs_1_), custom_call_target="tpu_custom_call", output_to_operand_aliasing={{}: (1, {})} | custom-call | bytes 1048576 | tf_op jit(solution)/shard_map/write_out/pallas_call | solution.py:325
  (35 shorter events, 1.4 us)
Async XLA Ops:
  0.0 8.0 %collective-permute-start = (bf16[2,512,128]{2,1,0:T(8,128)(2,1)}, bf16[2,512,128]{2,1,0:T(8,128)(2,1)S(1)}, u32[]{:S(2)}, u32[]{:S(2)}) collective-permute-start(bf16[2,512,128]{2,1,0:T(8,128)(2,1)} %refs_0_.1), channel_id=1, source_target_pairs={{0,2},{2,4},{4,6},{6,7},{7,5},{5,3},{3,1},{1,0},{8,10},{10,12},{12... | collective-permute-start | bytes 786440 | tf_op jit(solution)/shard_map/ppermute | solution.py:351
  0.2 8.1 %collective-permute-start.3 = (bf16[2,512,128]{2,1,0:T(8,128)(2,1)}, bf16[2,512,128]{2,1,0:T(8,128)(2,1)S(1)}, u32[]{:S(2)}, u32[]{:S(2)}) collective-permute-start(bf16[2,512,128]{2,1,0:T(8,128)(2,1)} %refs_0_.1), channel_id=1, source_target_pairs={{2,0},{4,2},{6,4},{7,6},{5,7},{3,5},{1,3},{0,1},{10,8},{12,10},{14... | collective-permute-start | bytes 786440 | tf_op jit(solution)/shard_map/ppermute | solution.py:352
  1.5 0.7 %copy-start.5 = (s32[2,4,8,4]{2,3,1,0:T(4,128)S(1)}, s32[2,4,8,4]{2,3,1,0:T(4,128)}, u32[]{:S(2)}) copy-start(s32[2,4,8,4]{2,3,1,0:T(4,128)} %param.11) | copy-start | bytes 3076
  2.2 0.7 %copy-start.6 = (s32[2,4,8]{2,1,0:T(4,128)S(1)}, s32[2,4,8]{2,1,0:T(4,128)}, u32[]{:S(2)}) copy-start(s32[2,4,8]{2,1,0:T(4,128)} %counts.1) | copy-start | bytes 772
  2.9 13.6 %copy-start.3 = (bf16[2,512,128]{2,1,0:T(8,128)(2,1)S(1)}, bf16[2,512,128]{2,1,0:T(8,128)(2,1)}, u32[]{:S(2)}) copy-start(bf16[2,512,128]{2,1,0:T(8,128)(2,1)} %refs_0_.1) | copy-start | bytes 786436
  8.1 3.9 %collective-permute-start.1 = (bf16[512,128]{1,0:T(8,128)(2,1)S(1)}, bf16[512,128]{1,0:T(8,128)(2,1)S(1)}, u32[]{:S(2)}, u32[]{:S(2)}) collective-permute-start(bf16[512,128]{1,0:T(8,128)(2,1)S(1)} %get-tuple-element.56), channel_id=1, source_target_pairs={{0,2},{2,4},{4,6},{6,7},{7,5},{5,3},{3,1},{1,0},{8,10},{10,12},{12... | collective-permute-start | bytes 393224 | tf_op jit(solution)/shard_map/ppermute | solution.py:363
  8.3 3.9 %collective-permute-start.4 = (bf16[512,128]{1,0:T(8,128)(2,1)S(1)}, bf16[512,128]{1,0:T(8,128)(2,1)S(1)}, u32[]{:S(2)}, u32[]{:S(2)}) collective-permute-start(bf16[512,128]{1,0:T(8,128)(2,1)S(1)} %get-tuple-element.54), channel_id=1, source_target_pairs={{2,0},{4,2},{6,4},{7,6},{5,7},{3,5},{1,3},{0,1},{10,8},{12,10},{14... | collective-permute-start | bytes 393224 | tf_op jit(solution)/shard_map/ppermute | solution.py:365
  9.7 5.4 %collective-permute-start.7 = (bf16[512,128]{1,0:T(8,128)(2,1)S(1)}, bf16[512,128]{1,0:T(8,128)(2,1)S(1)}, u32[]{:S(2)}, u32[]{:S(2)}) collective-permute-start(bf16[512,128]{1,0:T(8,128)(2,1)S(1)} %get-tuple-element.55), channel_id=1, source_target_pairs={{0,2},{2,4},{4,6},{6,7},{7,5},{5,3},{3,1},{1,0},{8,10},{10,12},{12... | collective-permute-start | bytes 393224 | tf_op jit(solution)/shard_map/ppermute | solution.py:363
  9.8 5.4 %collective-permute-start.9 = (bf16[512,128]{1,0:T(8,128)(2,1)S(1)}, bf16[512,128]{1,0:T(8,128)(2,1)S(1)}, u32[]{:S(2)}, u32[]{:S(2)}) collective-permute-start(bf16[512,128]{1,0:T(8,128)(2,1)S(1)} %get-tuple-element.53), channel_id=1, source_target_pairs={{2,0},{4,2},{6,4},{7,6},{5,7},{3,5},{1,3},{0,1},{10,8},{12,10},{14... | collective-permute-start | bytes 393224 | tf_op jit(solution)/shard_map/ppermute | solution.py:365
  11.9 6.2 %collective-permute-start.2 = (bf16[512,128]{1,0:T(8,128)(2,1)S(1)}, bf16[512,128]{1,0:T(8,128)(2,1)S(1)}, u32[]{:S(2)}, u32[]{:S(2)}) collective-permute-start(bf16[512,128]{1,0:T(8,128)(2,1)S(1)} %collective-permute-done.1.refs_0_), channel_id=1, source_target_pairs={{0,2},{2,4},{4,6},{6,7},{7,5},{5,3},{3,1},{1,0},{8,10},{10,12},{12... | collective-permute-start | bytes 393224 | tf_op jit(solution)/shard_map/ppermute | solution.py:363
  12.2 6.0 %collective-permute-start.5 = (bf16[512,128]{1,0:T(8,128)(2,1)S(1)}, bf16[512,128]{1,0:T(8,128)(2,1)S(1)}, u32[]{:S(2)}, u32[]{:S(2)}) collective-permute-start(bf16[512,128]{1,0:T(8,128)(2,1)S(1)} %collective-permute-done.4.refs_3_), channel_id=1, source_target_pairs={{2,0},{4,2},{6,4},{7,6},{5,7},{3,5},{1,3},{0,1},{10,8},{12,10},{14... | collective-permute-start | bytes 393224 | tf_op jit(solution)/shard_map/ppermute | solution.py:365
  15.0 6.0 %collective-permute-start.8 = (bf16[512,128]{1,0:T(8,128)(2,1)S(1)}, bf16[512,128]{1,0:T(8,128)(2,1)S(1)}, u32[]{:S(2)}, u32[]{:S(2)}) collective-permute-start(bf16[512,128]{1,0:T(8,128)(2,1)S(1)} %collective-permute-done.7.refs_1_), channel_id=1, source_target_pairs={{0,2},{2,4},{4,6},{6,7},{7,5},{5,3},{3,1},{1,0},{8,10},{10,12},{12... | collective-permute-start | bytes 393224 | tf_op jit(solution)/shard_map/ppermute | solution.py:363
  15.2 5.8 %collective-permute-start.10 = (bf16[512,128]{1,0:T(8,128)(2,1)S(1)}, bf16[512,128]{1,0:T(8,128)(2,1)S(1)}, u32[]{:S(2)}, u32[]{:S(2)}) collective-permute-start(bf16[512,128]{1,0:T(8,128)(2,1)S(1)} %collective-permute-done.9.refs_2_), channel_id=1, source_target_pairs={{2,0},{4,2},{6,4},{7,6},{5,7},{3,5},{1,3},{0,1},{10,8},{12,10},{14... | collective-permute-start | bytes 393224 | tf_op jit(solution)/shard_map/ppermute | solution.py:365
  18.1 2.9 %copy-start = (bf16[512,1536]{1,0:T(8,128)(2,1)S(1)}, bf16[512,1536]{1,0:T(8,128)(2,1)}, u32[]{:S(2)}) copy-start(bf16[512,1536]{1,0:T(8,128)(2,1)} %w_input.3) | copy-start | bytes 4718596
  18.1 2.9 %copy-start.1 = (bf16[512,1536]{1,0:T(8,128)(2,1)S(1)}, bf16[512,1536]{1,0:T(8,128)(2,1)}, u32[]{:S(2)}) copy-start(bf16[512,1536]{1,0:T(8,128)(2,1)} %w_hidden.7) | copy-start | bytes 4718596
  18.1 2.9 %copy-start.2 = (f32[512,512]{1,0:T(8,128)S(1)}, f32[512,512]{1,0:T(8,128)}, u32[]{:S(2)}) copy-start(f32[512,512]{1,0:T(8,128)} %hidden_start.3) | copy-start | bytes 3145732
  18.1 2.9 %copy-start.4 = (bf16[128,512]{1,0:T(8,128)(2,1)S(1)}, bf16[128,512]{1,0:T(8,128)(2,1)}, u32[]{:S(2)}) copy-start(bf16[128,512]{1,0:T(8,128)(2,1)} %w_graph.3) | copy-start | bytes 393220
  18.2 4.4 %collective-permute-start.11 = (bf16[512,128]{1,0:T(8,128)(2,1)S(1)}, bf16[512,128]{1,0:T(8,128)(2,1)S(1)}, u32[]{:S(2)}, u32[]{:S(2)}) collective-permute-start(bf16[512,128]{1,0:T(8,128)(2,1)S(1)} %collective-permute-done.5.refs_3_), channel_id=1, source_target_pairs={{2,0},{4,2},{6,4},{7,6},{5,7},{3,5},{1,3},{0,1},{10,8},{12,10},{14... | collective-permute-start | bytes 393224 | tf_op jit(solution)/shard_map/ppermute | solution.py:374
  19.5 8.7 %collective-permute-start.6 = (bf16[512,128]{1,0:T(8,128)(2,1)S(1)}, bf16[512,128]{1,0:T(8,128)(2,1)S(1)}, u32[]{:S(2)}, u32[]{:S(2)}) collective-permute-start(bf16[512,128]{1,0:T(8,128)(2,1)S(1)} %collective-permute-done.2.refs_0_), channel_id=1, source_target_pairs={{0,2},{2,4},{4,6},{6,7},{7,5},{5,3},{3,1},{1,0},{8,10},{10,12},{12... | collective-permute-start | bytes 393224 | tf_op jit(solution)/shard_map/ppermute | solution.py:374
  23.4 7.5 %collective-permute-start.13 = (bf16[256,128]{1,0:T(8,128)(2,1)S(1)}, bf16[256,128]{1,0:T(8,128)(2,1)S(1)}, u32[]{:S(2)}, u32[]{:S(2)}) collective-permute-start(bf16[256,128]{1,0:T(8,128)(2,1)S(1)} %get-tuple-element.40), channel_id=1, source_target_pairs={{0,8},{8,0},{16,24},{24,16},{1,9},{9,1},{17,25},{25,17},{2,10},{10... | collective-permute-start | bytes 196616 | tf_op jit(solution)/shard_map/ppermute | solution.py:385
  29.1 1.8 %collective-permute-start.12 = (bf16[256,128]{1,0:T(8,128)(2,1)S(1)}, bf16[256,128]{1,0:T(8,128)(2,1)S(1)}, u32[]{:S(2)}, u32[]{:S(2)}) collective-permute-start(bf16[256,128]{1,0:T(8,128)(2,1)S(1)} %get-tuple-element.39), channel_id=1, source_target_pairs={{0,8},{8,0},{16,24},{24,16},{1,9},{9,1},{17,25},{25,17},{2,10},{10... | collective-permute-start | bytes 196616 | tf_op jit(solution)/shard_map/ppermute | solution.py:385
  29.8 1.1 %copy-start.7 = (f32[512]{0:T(512)S(1)}, f32[512]{0:T(512)}, u32[]{:S(2)}) copy-start(f32[512]{0:T(512)} %param.17) | copy-start | bytes 6148
  31.6 7.0 %collective-permute-start.16 = (bf16[128,512]{1,0:T(8,128)(2,1)S(1)}, bf16[128,512]{1,0:T(8,128)(2,1)S(1)}, u32[]{:S(2)}, u32[]{:S(2)}) collective-permute-start(bf16[128,512]{1,0:T(8,128)(2,1)S(1)} %get-tuple-element.46), channel_id=1, source_target_pairs={{0,16},{8,24},{1,17},{9,25},{2,18},{10,26},{3,19},{11,27},{4,20},{... | collective-permute-start | bytes 393224 | tf_op jit(solution)/shard_map/ppermute | solution.py:399
  33.6 8.4 %collective-permute-start.14 = (bf16[128,512]{1,0:T(8,128)(2,1)S(1)}, bf16[128,512]{1,0:T(8,128)(2,1)S(1)}, u32[]{:S(2)}, u32[]{:S(2)}) collective-permute-start(bf16[128,512]{1,0:T(8,128)(2,1)S(1)} %get-tuple-element.41), channel_id=1, source_target_pairs={{0,16},{8,24},{1,17},{9,25},{2,18},{10,26},{3,19},{11,27},{4,20},{... | collective-permute-start | bytes 393224 | tf_op jit(solution)/shard_map/ppermute | solution.py:399
  40.1 4.4 %collective-permute-start.17 = (bf16[2,128,512]{2,1,0:T(8,128)(2,1)S(1)}, bf16[2,128,512]{2,1,0:T(8,128)(2,1)S(1)}, u32[]{:S(2)}, u32[]{:S(2)}) collective-permute-start(bf16[2,128,512]{2,1,0:T(8,128)(2,1)S(1)} %get-tuple-element.52), channel_id=1, source_target_pairs={{0,8},{8,0},{16,24},{24,16},{1,9},{9,1},{17,25},{25,17},{2,10},{10... | collective-permute-start | bytes 786440 | tf_op jit(solution)/shard_map/ppermute | solution.py:408
  43.5 2.1 %collective-permute-start.15 = (bf16[2,128,512]{2,1,0:T(8,128)(2,1)S(1)}, bf16[2,128,512]{2,1,0:T(8,128)(2,1)S(1)}, u32[]{:S(2)}, u32[]{:S(2)}) collective-permute-start(bf16[2,128,512]{2,1,0:T(8,128)(2,1)S(1)} %get-tuple-element.45), channel_id=1, source_target_pairs={{0,8},{8,0},{16,24},{24,16},{1,9},{9,1},{17,25},{25,17},{2,10},{10... | collective-permute-start | bytes 786440 | tf_op jit(solution)/shard_map/ppermute | solution.py:408

commit v3 on v2

--- a/solution.py
+++ b/solution.py
@@ -386,7 +386,7 @@
     gx_own = gates(keep_ax, w_graph, w_input)
 
     bias = update_bias.reshape(1, -1)
-    onward = [(t, t + CORES) for t in range(sections - CORES)]
+    onward = [(t, (t + CORES) % sections) for t in range(sections)]
     hidden, states, gx_other = [], [], []
     for chunk in range(CHUNKS):
         state, keep, send, gx = recurrence_first(

time: 46.8 us -> 45.4 us (0.970)
  the two profiles are of different devices: /device:TPU:15 before, /device:TPU:0 now
where the time goes in v3:
time: 45.4 us; the launch traced here: 45.1 us
  Pallas kernels  18.2 us (40%)
  starting transfers between devices  15 us (33%)
  waiting for transfers between devices  9.95 us (22%)
  local copies, waits for them, and re-layouts  1.47 us (3%)
    ppermute x4, starting transfers between devices, per_device(): forward[s] = lax.ppermute(forward[s], 'dom', ahead)  8.51 us
    ppermute x2, waiting for transfers between devices, per_device(): states = [lax.ppermute(state, 'tm', onward) for state in states]  5.5 us
    pallas_call x1, Pallas kernels, load_tiles(): pl.pallas_call(kernel, out_shape=(jax.ShapeDtypeStruct(tiles.shape, tiles...  5.14 us
    pallas_call x2, Pallas kernels, recurrence_first(): pl.pallas_call(kernel, out_shape=(jax.ShapeDtypeStruct((rows, hid), BF16)...  4.31 us
    pallas_call x3, Pallas kernels, spmm(): pl.pallas_call(kernel, out_shape=jax.ShapeDtypeStruct((snaps, rows, blk,...  4.2 us
    ppermute x1, starting transfers between devices, per_device(): forward = lax.ppermute(features, 'dom', ahead)  3.02 us
    ppermute x4, waiting for transfers between devices, per_device(): forward[s] = lax.ppermute(forward[s], 'dom', ahead)  2.51 us
    pallas_call x2, Pallas kernels, spmm_last(): pl.pallas_call(kernel, out_shape=(part, part), in_specs=[whole(SMEM)] + [...  1.74 us
  transfers between devices with their start and end apart: 18, of which 8 were waited for; matrix products, arithmetic and copies ran while one was open for 0% of the time, Pallas kernels for 34%

profile of v3, /device:TPU:0, one launch (start us, length us, event | category | flops | bytes accessed | tf_op | source)
XLA Modules:
  0.0 45.1 jit_solution(9910024763903615036)
XLA Ops:
  0.0 3.0 %collective-permute-start = (bf16[2,512,128]{2,1,0:T(8,128)(2,1)}, bf16[2,512,128]{2,1,0:T(8,128)(2,1)S(1)}, u32[]{:S(2)}, u32[]{:S(2)}) collective-permute-start(bf16[2,512,128]{2,1,0:T(8,128)(2,1)} %refs_0_.1), channel_id=1, source_target_pairs={{0,2},{2,4},{4,6},{6,7},{7,5},{5,3},{3,1},{1,0},{8,10},{10,12},{12... | collective-permute-start | bytes 786440 | tf_op jit(solution)/shard_map/ppermute | solution.py:351
  3.0 0.7 %copy-done.5 = s32[2,4,8,4]{2,3,1,0:T(4,128)S(1)} copy-done((s32[2,4,8,4]{2,3,1,0:T(4,128)S(1)}, s32[2,4,8,4]{2,3,1,0:T(4,128)}, u32[]{:S(2)}) %copy-start.5) | copy-done | bytes 1048
  3.7 0.7 %copy-done.6 = s32[2,4,8]{2,1,0:T(4,128)S(1)} copy-done((s32[2,4,8]{2,1,0:T(4,128)S(1)}, s32[2,4,8]{2,1,0:T(4,128)}, u32[]{:S(2)}) %copy-start.6) | copy-done | bytes 280
  4.4 5.1 %load_tiles.1 = (bf16[2,4,8,4,128,128]{5,4,3,2,1,0:T(8,128)(2,1)S(1)}, s32[256]{0:T(256)S(1)}) custom-call(bf16[2,4,8,4,128,128]{5,4,3,2,1,0:T(8,128)(2,1)} %tiles.1, s32[2,4,4,8]{3,2,1,0:T(4,128)S(1)} %bitcast.10, s32[2,4,8]{2,1,0:T(4,128)S(1)} %copy-done.6), custom_call_target="tpu_custom_call" | custom-call | bytes 1048576 | tf_op jit(solution)/shard_map/load_tiles/pallas_call | solution.py:97
  9.6 2.1 %collective-permute-start.1 = (bf16[512,128]{1,0:T(8,128)(2,1)S(1)}, bf16[512,128]{1,0:T(8,128)(2,1)S(1)}, u32[]{:S(2)}, u32[]{:S(2)}) collective-permute-start(bf16[512,128]{1,0:T(8,128)(2,1)S(1)} %get-tuple-element.56), channel_id=1, source_target_pairs={{0,2},{2,4},{4,6},{6,7},{7,5},{5,3},{3,1},{1,0},{8,10},{10,12},{12... | collective-permute-start | bytes 393224 | tf_op jit(solution)/shard_map/ppermute | solution.py:363
  11.8 2.0 %collective-permute-start.7 = (bf16[512,128]{1,0:T(8,128)(2,1)S(1)}, bf16[512,128]{1,0:T(8,128)(2,1)S(1)}, u32[]{:S(2)}, u32[]{:S(2)}) collective-permute-start(bf16[512,128]{1,0:T(8,128)(2,1)S(1)} %get-tuple-element.55), channel_id=1, source_target_pairs={{0,2},{2,4},{4,6},{6,7},{7,5},{5,3},{3,1},{1,0},{8,10},{10,12},{12... | collective-permute-start | bytes 393224 | tf_op jit(solution)/shard_map/ppermute | solution.py:363
  13.9 2.0 %collective-permute-done.1.refs_0_ = bf16[512,128]{1,0:T(8,128)(2,1)S(1)} collective-permute-done((bf16[512,128]{1,0:T(8,128)(2,1)S(1)}, bf16[512,128]{1,0:T(8,128)(2,1)S(1)}, u32[]{:S(2)}, u32[]{:S(2)}) %collective-permute-start.1) | collective-permute-done | bytes 131104 | tf_op jit(solution)/shard_map/ppermute | solution.py:363
  15.9 2.2 %collective-permute-start.2 = (bf16[512,128]{1,0:T(8,128)(2,1)S(1)}, bf16[512,128]{1,0:T(8,128)(2,1)S(1)}, u32[]{:S(2)}, u32[]{:S(2)}) collective-permute-start(bf16[512,128]{1,0:T(8,128)(2,1)S(1)} %collective-permute-done.1.refs_0_), channel_id=1, source_target_pairs={{0,2},{2,4},{4,6},{6,7},{7,5},{5,3},{3,1},{1,0},{8,10},{10,12},{12... | collective-permute-start | bytes 393224 | tf_op jit(solution)/shard_map/ppermute | solution.py:363
  18.1 0.1 collective-permute-start.5
  18.1 0.5 %collective-permute-done.7.refs_1_ = bf16[512,128]{1,0:T(8,128)(2,1)S(1)} collective-permute-done((bf16[512,128]{1,0:T(8,128)(2,1)S(1)}, bf16[512,128]{1,0:T(8,128)(2,1)S(1)}, u32[]{:S(2)}, u32[]{:S(2)}) %collective-permute-start.7) | collective-permute-done | bytes 131104 | tf_op jit(solution)/shard_map/ppermute | solution.py:363
  18.7 2.2 %collective-permute-start.8 = (bf16[512,128]{1,0:T(8,128)(2,1)S(1)}, bf16[512,128]{1,0:T(8,128)(2,1)S(1)}, u32[]{:S(2)}, u32[]{:S(2)}) collective-permute-start(bf16[512,128]{1,0:T(8,128)(2,1)S(1)} %collective-permute-done.7.refs_1_), channel_id=1, source_target_pairs={{0,2},{2,4},{4,6},{6,7},{7,5},{5,3},{3,1},{1,0},{8,10},{10,12},{12... | collective-permute-start | bytes 393224 | tf_op jit(solution)/shard_map/ppermute | solution.py:363
  20.9 1.6 %spmm.3.refs_4_ = f32[2,4,128,128]{3,2,1,0:T(8,128)S(1)} custom-call(s32[256]{0:T(256)S(1)} %get-tuple-element.31.table, bf16[2,4,8,4,128,128]{5,4,3,2,1,0:T(8,128)(2,1)S(1)} %get-tuple-element.32.tiles, bf16[2,512,128]{2,1,0:T(8,128)(2,1)S(1)} %copy-done.3, bf16[2,512,128]{2,1,0:T(8,128)(2,1)S(1)} %collective-permute-done.refs_1_, ...), custom_call_target="tpu_custom_call" | custom-call | flops 1610612736 | bytes 1048576 | tf_op jit(solution)/shard_map/spmm/pallas_call | solution.py:144
  22.5 0.8 %collective-permute-done.5.refs_3_ = bf16[512,128]{1,0:T(8,128)(2,1)S(1)} collective-permute-done((bf16[512,128]{1,0:T(8,128)(2,1)S(1)}, bf16[512,128]{1,0:T(8,128)(2,1)S(1)}, u32[]{:S(2)}, u32[]{:S(2)}) %collective-permute-start.5) | collective-permute-done | bytes 131104 | tf_op jit(solution)/shard_map/ppermute | solution.py:365
  23.4 1.2 %collective-permute-start.11 = (bf16[512,128]{1,0:T(8,128)(2,1)S(1)}, bf16[512,128]{1,0:T(8,128)(2,1)S(1)}, u32[]{:S(2)}, u32[]{:S(2)}) collective-permute-start(bf16[512,128]{1,0:T(8,128)(2,1)S(1)} %collective-permute-done.5.refs_3_), channel_id=1, source_target_pairs={{2,0},{4,2},{6,4},{7,6},{5,7},{3,5},{1,3},{0,1},{10,8},{12,10},{14... | collective-permute-start | bytes 393224 | tf_op jit(solution)/shard_map/ppermute | solution.py:374
  24.6 0.9 %collective-permute-start.6 = (bf16[512,128]{1,0:T(8,128)(2,1)S(1)}, bf16[512,128]{1,0:T(8,128)(2,1)S(1)}, u32[]{:S(2)}, u32[]{:S(2)}) collective-permute-start(bf16[512,128]{1,0:T(8,128)(2,1)S(1)} %collective-permute-done.2.refs_0_), channel_id=1, source_target_pairs={{0,2},{2,4},{4,6},{6,7},{7,5},{5,3},{3,1},{1,0},{8,10},{10,12},{12... | collective-permute-start | bytes 393224 | tf_op jit(solution)/shard_map/ppermute | solution.py:374
  25.4 1.3 %spmm.4.refs_4_ = f32[2,4,128,128]{3,2,1,0:T(8,128)S(1)} custom-call(s32[256]{0:T(256)S(1)} %get-tuple-element.31.table, bf16[2,4,8,4,128,128]{5,4,3,2,1,0:T(8,128)(2,1)S(1)} %get-tuple-element.32.tiles, bf16[512,128]{1,0:T(8,128)(2,1)S(1)} %collective-permute-done.1.refs_0_, bf16[512,128]{1,0:T(8,128)(2,1)S(1)} %collective-permute-done.7.refs_1_, ...), custom_call_target="tpu_custom_call" | custom-call | flops 1073741824 | bytes 1048576 | tf_op jit(solution)/shard_map/spmm/pallas_call | solution.py:144
  26.8 1.3 %spmm.5.acc_in = f32[2,4,128,128]{3,2,1,0:T(8,128)S(1)} custom-call(s32[256]{0:T(256)S(1)} %get-tuple-element.31.table, bf16[2,4,8,4,128,128]{5,4,3,2,1,0:T(8,128)(2,1)S(1)} %get-tuple-element.32.tiles, bf16[512,128]{1,0:T(8,128)(2,1)S(1)} %collective-permute-done.2.refs_0_, bf16[512,128]{1,0:T(8,128)(2,1)S(1)} %collective-permute-done.8.refs_1_, ...), custom_call_target="tpu_custom_call" | custom-call | flops 1073741824 | bytes 1048576 | tf_op jit(solution)/shard_map/spmm/pallas_call | solution.py:144
  28.1 0.3 collective-permute-done.11.x_ref
  28.4 0.9 %spmm_last.3 = (bf16[256,128]{1,0:T(8,128)(2,1)S(1)}, bf16[256,128]{1,0:T(8,128)(2,1)S(1)}) custom-call(s32[256]{0:T(256)S(1)} %get-tuple-element.31.table, bf16[2,4,8,4,128,128]{5,4,3,2,1,0:T(8,128)(2,1)S(1)} %get-tuple-element.32.tiles, bf16[512,128]{1,0:T(8,128)(2,1)S(1)} %collective-permute-done.11.x_ref, f32[2,4,128,128]{3,2,1,0:T(8,128)S(1)} %spmm.5.acc_in), custom_call_target="tpu_custom_call" | custom-call | flops 268435456 | bytes 1048576 | tf_op jit(solution)/shard_map/spmm_last/pallas_call | solution.py:168
  29.3 0.2 collective-permute-done.6.x_ref
  29.5 0.9 %spmm_last.2 = (bf16[256,128]{1,0:T(8,128)(2,1)S(1)}, bf16[256,128]{1,0:T(8,128)(2,1)S(1)}) custom-call(s32[256]{0:T(256)S(1)} %get-tuple-element.31.table, bf16[2,4,8,4,128,128]{5,4,3,2,1,0:T(8,128)(2,1)S(1)} %get-tuple-element.32.tiles, bf16[512,128]{1,0:T(8,128)(2,1)S(1)} %collective-permute-done.6.x_ref, f32[2,4,128,128]{3,2,1,0:T(8,128)S(1)} %spmm.5.acc_in), custom_call_target="tpu_custom_call" | custom-call | flops 268435456 | bytes 1048576 | tf_op jit(solution)/shard_map/spmm_last/pallas_call | solution.py:168
  30.4 0.3 collective-permute-start.12
  30.8 1.1 %gates.1.gx_own = f32[2,256,1536]{2,1,0:T(8,128)S(1)} custom-call(bf16[256,128]{1,0:T(8,128)(2,1)S(1)} %get-tuple-element.36.refs_0_, bf16[256,128]{1,0:T(8,128)(2,1)S(1)} %get-tuple-element.38.refs_1_, bf16[128,512]{1,0:T(8,128)(2,1)S(1)} %copy-done.4, bf16[512,1536]{1,0:T(8,128)(2,1)S(1)} %copy-done), custom_call_target="tpu_custom_call" | custom-call | flops 1610612736 | bytes 1048576 | tf_op jit(solution)/shard_map/gates/pallas_call | solution.py:196
  31.9 2.2 %recurrence_first.3 = (bf16[128,512]{1,0:T(8,128)(2,1)S(1)}, bf16[2,128,512]{2,1,0:T(8,128)(2,1)S(1)}, bf16[2,128,512]{2,1,0:T(8,128)(2,1)S(1)}, f32[2,128,1536]{2,1,0:T(8,128)S(1)}) custom-call(f32[512,512]{1,0:T(8,128)S(1)} %copy-done.2, f32[2,256,1536]{2,1,0:T(8,128)S(1)} %gates.1.gx_own, bf16[128,512]{1,0:T(8,128)(2,1)S(1)} %copy-done.4, ...), custom_call_target="tpu_custom_call" | custom-call | flops 3221225472 | bytes 1048576 | tf_op jit(solution)/shard_map/recurrence_first/pallas_call | solution.py:256
  34.1 0.1 collective-permute-start.16
  34.2 2.1 %recurrence_first.2 = (bf16[128,512]{1,0:T(8,128)(2,1)S(1)}, bf16[2,128,512]{2,1,0:T(8,128)(2,1)S(1)}, bf16[2,128,512]{2,1,0:T(8,128)(2,1)S(1)}, f32[2,128,1536]{2,1,0:T(8,128)S(1)}) custom-call(f32[512,512]{1,0:T(8,128)S(1)} %copy-done.2, f32[2,256,1536]{2,1,0:T(8,128)S(1)} %gates.1.gx_own, bf16[128,512]{1,0:T(8,128)(2,1)S(1)} %copy-done.4, ...), custom_call_target="tpu_custom_call" | custom-call | flops 3221225472 | bytes 1048576 | tf_op jit(solution)/shard_map/recurrence_first/pallas_call | solution.py:256
  36.3 0.6 %collective-permute-start.14 = (bf16[128,512]{1,0:T(8,128)(2,1)S(1)}, bf16[128,512]{1,0:T(8,128)(2,1)S(1)}, u32[]{:S(2)}, u32[]{:S(2)}) collective-permute-start(bf16[128,512]{1,0:T(8,128)(2,1)S(1)} %get-tuple-element.41), channel_id=1, source_target_pairs={{0,16},{8,24},{16,0},{24,8},{1,17},{9,25},{17,1},{25,9},{2,18},{10... | collective-permute-start | bytes 393224 | tf_op jit(solution)/shard_map/ppermute | solution.py:399
  36.9 3.3 %collective-permute-done.16.state_in = bf16[128,512]{1,0:T(8,128)(2,1)S(1)} collective-permute-done((bf16[128,512]{1,0:T(8,128)(2,1)S(1)}, bf16[128,512]{1,0:T(8,128)(2,1)S(1)}, u32[]{:S(2)}, u32[]{:S(2)}) %collective-permute-start.16) | collective-permute-done | bytes 131104 | tf_op jit(solution)/shard_map/ppermute | solution.py:399
  40.4 2.2 %collective-permute-done.14.state_in = bf16[128,512]{1,0:T(8,128)(2,1)S(1)} collective-permute-done((bf16[128,512]{1,0:T(8,128)(2,1)S(1)}, bf16[128,512]{1,0:T(8,128)(2,1)S(1)}, u32[]{:S(2)}, u32[]{:S(2)}) %collective-permute-start.14) | collective-permute-done | bytes 131104 | tf_op jit(solution)/shard_map/ppermute | solution.py:399
  42.7 0.9 %write_out.2.refs_1_ = bf16[2,512,512]{2,1,0:T(8,128)(2,1)} custom-call(bf16[2,128,512]{2,1,0:T(8,128)(2,1)S(1)} %get-tuple-element.50.refs_0_, bf16[2,128,512]{2,1,0:T(8,128)(2,1)S(1)} %get-tuple-element.51.refs_1_, bf16[2,128,512]{2,1,0:T(8,128)(2,1)S(1)} %collective-permute-done.17.refs_2_), custom_call_target="tpu_custom_call" | custom-call | bytes 1048576 | tf_op jit(solution)/shard_map/write_out/pallas_call | solution.py:325
  43.6 0.6 %collective-permute-done.15.refs_0_ = bf16[2,128,512]{2,1,0:T(8,128)(2,1)S(1)} collective-permute-done((bf16[2,128,512]{2,1,0:T(8,128)(2,1)S(1)}, bf16[2,128,512]{2,1,0:T(8,128)(2,1)S(1)}, u32[]{:S(2)}, u32[]{:S(2)}) %collective-permute-start.15) | collective-permute-done | bytes 262176 | tf_op jit(solution)/shard_map/ppermute | solution.py:408
  44.2 0.7 %write_out.3 = bf16[2,512,512]{2,1,0:T(8,128)(2,1)} custom-call(bf16[2,128,512]{2,1,0:T(8,128)(2,1)S(1)} %collective-permute-done.15.refs_0_, bf16[2,512,512]{2,1,0:T(8,128)(2,1)} %write_out.2.refs_1_), custom_call_target="tpu_custom_call", output_to_operand_aliasing={{}: (1, {})} | custom-call | bytes 1048576 | tf_op jit(solution)/shard_map/write_out/pallas_call | solution.py:325
  (35 shorter events, 0.5 us)
Async XLA Ops:
  0.0 9.6 %collective-permute-start = (bf16[2,512,128]{2,1,0:T(8,128)(2,1)}, bf16[2,512,128]{2,1,0:T(8,128)(2,1)S(1)}, u32[]{:S(2)}, u32[]{:S(2)}) collective-permute-start(bf16[2,512,128]{2,1,0:T(8,128)(2,1)} %refs_0_.1), channel_id=1, source_target_pairs={{0,2},{2,4},{4,6},{6,7},{7,5},{5,3},{3,1},{1,0},{8,10},{10,12},{12... | collective-permute-start | bytes 786440 | tf_op jit(solution)/shard_map/ppermute | solution.py:351
  3.0 8.7 %collective-permute-start.3 = (bf16[2,512,128]{2,1,0:T(8,128)(2,1)}, bf16[2,512,128]{2,1,0:T(8,128)(2,1)S(1)}, u32[]{:S(2)}, u32[]{:S(2)}) collective-permute-start(bf16[2,512,128]{2,1,0:T(8,128)(2,1)} %refs_0_.1), channel_id=1, source_target_pairs={{2,0},{4,2},{6,4},{7,6},{5,7},{3,5},{1,3},{0,1},{10,8},{12,10},{14... | collective-permute-start | bytes 786440 | tf_op jit(solution)/shard_map/ppermute | solution.py:352
  3.0 0.7 %copy-start.5 = (s32[2,4,8,4]{2,3,1,0:T(4,128)S(1)}, s32[2,4,8,4]{2,3,1,0:T(4,128)}, u32[]{:S(2)}) copy-start(s32[2,4,8,4]{2,3,1,0:T(4,128)} %param.11) | copy-start | bytes 3076
  3.7 0.7 %copy-start.6 = (s32[2,4,8]{2,1,0:T(4,128)S(1)}, s32[2,4,8]{2,1,0:T(4,128)}, u32[]{:S(2)}) copy-start(s32[2,4,8]{2,1,0:T(4,128)} %counts.1) | copy-start | bytes 772
  4.4 16.4 %copy-start.3 = (bf16[2,512,128]{2,1,0:T(8,128)(2,1)S(1)}, bf16[2,512,128]{2,1,0:T(8,128)(2,1)}, u32[]{:S(2)}) copy-start(bf16[2,512,128]{2,1,0:T(8,128)(2,1)} %refs_0_.1) | copy-start | bytes 786436
  9.6 6.2 %collective-permute-start.1 = (bf16[512,128]{1,0:T(8,128)(2,1)S(1)}, bf16[512,128]{1,0:T(8,128)(2,1)S(1)}, u32[]{:S(2)}, u32[]{:S(2)}) collective-permute-start(bf16[512,128]{1,0:T(8,128)(2,1)S(1)} %get-tuple-element.56), channel_id=1, source_target_pairs={{0,2},{2,4},{4,6},{6,7},{7,5},{5,3},{3,1},{1,0},{8,10},{10,12},{12... | collective-permute-start | bytes 393224 | tf_op jit(solution)/shard_map/ppermute | solution.py:363
  11.7 6.3 %collective-permute-start.4 = (bf16[512,128]{1,0:T(8,128)(2,1)S(1)}, bf16[512,128]{1,0:T(8,128)(2,1)S(1)}, u32[]{:S(2)}, u32[]{:S(2)}) collective-permute-start(bf16[512,128]{1,0:T(8,128)(2,1)S(1)} %get-tuple-element.54), channel_id=1, source_target_pairs={{2,0},{4,2},{6,4},{7,6},{5,7},{3,5},{1,3},{0,1},{10,8},{12,10},{14... | collective-permute-start | bytes 393224 | tf_op jit(solution)/shard_map/ppermute | solution.py:365
  11.8 6.9 %collective-permute-start.7 = (bf16[512,128]{1,0:T(8,128)(2,1)S(1)}, bf16[512,128]{1,0:T(8,128)(2,1)S(1)}, u32[]{:S(2)}, u32[]{:S(2)}) collective-permute-start(bf16[512,128]{1,0:T(8,128)(2,1)S(1)} %get-tuple-element.55), channel_id=1, source_target_pairs={{0,2},{2,4},{4,6},{6,7},{7,5},{5,3},{3,1},{1,0},{8,10},{10,12},{12... | collective-permute-start | bytes 393224 | tf_op jit(solution)/shard_map/ppermute | solution.py:363
  13.8 7.1 %collective-permute-start.9 = (bf16[512,128]{1,0:T(8,128)(2,1)S(1)}, bf16[512,128]{1,0:T(8,128)(2,1)S(1)}, u32[]{:S(2)}, u32[]{:S(2)}) collective-permute-start(bf16[512,128]{1,0:T(8,128)(2,1)S(1)} %get-tuple-element.53), channel_id=1, source_target_pairs={{2,0},{4,2},{6,4},{7,6},{5,7},{3,5},{1,3},{0,1},{10,8},{12,10},{14... | collective-permute-start | bytes 393224 | tf_op jit(solution)/shard_map/ppermute | solution.py:365
  15.9 6.7 %collective-permute-start.2 = (bf16[512,128]{1,0:T(8,128)(2,1)S(1)}, bf16[512,128]{1,0:T(8,128)(2,1)S(1)}, u32[]{:S(2)}, u32[]{:S(2)}) collective-permute-start(bf16[512,128]{1,0:T(8,128)(2,1)S(1)} %collective-permute-done.1.refs_0_), channel_id=1, source_target_pairs={{0,2},{2,4},{4,6},{6,7},{7,5},{5,3},{3,1},{1,0},{8,10},{10,12},{12... | collective-permute-start | bytes 393224 | tf_op jit(solution)/shard_map/ppermute | solution.py:363
  18.1 5.3 %collective-permute-start.5 = (bf16[512,128]{1,0:T(8,128)(2,1)S(1)}, bf16[512,128]{1,0:T(8,128)(2,1)S(1)}, u32[]{:S(2)}, u32[]{:S(2)}) collective-permute-start(bf16[512,128]{1,0:T(8,128)(2,1)S(1)} %collective-permute-done.4.refs_3_), channel_id=1, source_target_pairs={{2,0},{4,2},{6,4},{7,6},{5,7},{3,5},{1,3},{0,1},{10,8},{12,10},{14... | collective-permute-start | bytes 393224 | tf_op jit(solution)/shard_map/ppermute | solution.py:365
  18.7 8.1 %collective-permute-start.8 = (bf16[512,128]{1,0:T(8,128)(2,1)S(1)}, bf16[512,128]{1,0:T(8,128)(2,1)S(1)}, u32[]{:S(2)}, u32[]{:S(2)}) collective-permute-start(bf16[512,128]{1,0:T(8,128)(2,1)S(1)} %collective-permute-done.7.refs_1_), channel_id=1, source_target_pairs={{0,2},{2,4},{4,6},{6,7},{7,5},{5,3},{3,1},{1,0},{8,10},{10,12},{12... | collective-permute-start | bytes 393224 | tf_op jit(solution)/shard_map/ppermute | solution.py:363
  20.9 5.9 %collective-permute-start.10 = (bf16[512,128]{1,0:T(8,128)(2,1)S(1)}, bf16[512,128]{1,0:T(8,128)(2,1)S(1)}, u32[]{:S(2)}, u32[]{:S(2)}) collective-permute-start(bf16[512,128]{1,0:T(8,128)(2,1)S(1)} %collective-permute-done.9.refs_2_), channel_id=1, source_target_pairs={{2,0},{4,2},{6,4},{7,6},{5,7},{3,5},{1,3},{0,1},{10,8},{12,10},{14... | collective-permute-start | bytes 393224 | tf_op jit(solution)/shard_map/ppermute | solution.py:365
  22.5 4.3 %copy-start = (bf16[512,1536]{1,0:T(8,128)(2,1)S(1)}, bf16[512,1536]{1,0:T(8,128)(2,1)}, u32[]{:S(2)}) copy-start(bf16[512,1536]{1,0:T(8,128)(2,1)} %w_input.3) | copy-start | bytes 4718596
  22.5 4.3 %copy-start.1 = (bf16[512,1536]{1,0:T(8,128)(2,1)S(1)}, bf16[512,1536]{1,0:T(8,128)(2,1)}, u32[]{:S(2)}) copy-start(bf16[512,1536]{1,0:T(8,128)(2,1)} %w_hidden.7) | copy-start | bytes 4718596
  22.5 4.3 %copy-start.2 = (f32[512,512]{1,0:T(8,128)S(1)}, f32[512,512]{1,0:T(8,128)}, u32[]{:S(2)}) copy-start(f32[512,512]{1,0:T(8,128)} %hidden_start.3) | copy-start | bytes 3145732
  22.5 4.3 %copy-start.4 = (bf16[128,512]{1,0:T(8,128)(2,1)S(1)}, bf16[128,512]{1,0:T(8,128)(2,1)}, u32[]{:S(2)}) copy-start(bf16[128,512]{1,0:T(8,128)(2,1)} %w_graph.3) | copy-start | bytes 393220
  23.4 5.0 %collective-permute-start.11 = (bf16[512,128]{1,0:T(8,128)(2,1)S(1)}, bf16[512,128]{1,0:T(8,128)(2,1)S(1)}, u32[]{:S(2)}, u32[]{:S(2)}) collective-permute-start(bf16[512,128]{1,0:T(8,128)(2,1)S(1)} %collective-permute-done.5.refs_3_), channel_id=1, source_target_pairs={{2,0},{4,2},{6,4},{7,6},{5,7},{3,5},{1,3},{0,1},{10,8},{12,10},{14... | collective-permute-start | bytes 393224 | tf_op jit(solution)/shard_map/ppermute | solution.py:374
  24.6 5.0 %collective-permute-start.6 = (bf16[512,128]{1,0:T(8,128)(2,1)S(1)}, bf16[512,128]{1,0:T(8,128)(2,1)S(1)}, u32[]{:S(2)}, u32[]{:S(2)}) collective-permute-start(bf16[512,128]{1,0:T(8,128)(2,1)S(1)} %collective-permute-done.2.refs_0_), channel_id=1, source_target_pairs={{0,2},{2,4},{4,6},{6,7},{7,5},{5,3},{3,1},{1,0},{8,10},{10,12},{12... | collective-permute-start | bytes 393224 | tf_op jit(solution)/shard_map/ppermute | solution.py:374
  29.2 2.6 %collective-permute-start.13 = (bf16[256,128]{1,0:T(8,128)(2,1)S(1)}, bf16[256,128]{1,0:T(8,128)(2,1)S(1)}, u32[]{:S(2)}, u32[]{:S(2)}) collective-permute-start(bf16[256,128]{1,0:T(8,128)(2,1)S(1)} %get-tuple-element.40), channel_id=1, source_target_pairs={{0,8},{8,0},{16,24},{24,16},{1,9},{9,1},{17,25},{25,17},{2,10},{10... | collective-permute-start | bytes 196616 | tf_op jit(solution)/shard_map/ppermute | solution.py:385
  30.4 1.5 %collective-permute-start.12 = (bf16[256,128]{1,0:T(8,128)(2,1)S(1)}, bf16[256,128]{1,0:T(8,128)(2,1)S(1)}, u32[]{:S(2)}, u32[]{:S(2)}) collective-permute-start(bf16[256,128]{1,0:T(8,128)(2,1)S(1)} %get-tuple-element.39), channel_id=1, source_target_pairs={{0,8},{8,0},{16,24},{24,16},{1,9},{9,1},{17,25},{25,17},{2,10},{10... | collective-permute-start | bytes 196616 | tf_op jit(solution)/shard_map/ppermute | solution.py:385
  30.8 1.1 %copy-start.7 = (f32[512]{0:T(512)S(1)}, f32[512]{0:T(512)}, u32[]{:S(2)}) copy-start(f32[512]{0:T(512)} %param.17) | copy-start | bytes 6148
  34.1 6.2 %collective-permute-start.16 = (bf16[128,512]{1,0:T(8,128)(2,1)S(1)}, bf16[128,512]{1,0:T(8,128)(2,1)S(1)}, u32[]{:S(2)}, u32[]{:S(2)}) collective-permute-start(bf16[128,512]{1,0:T(8,128)(2,1)S(1)} %get-tuple-element.46), channel_id=1, source_target_pairs={{0,16},{8,24},{16,0},{24,8},{1,17},{9,25},{17,1},{25,9},{2,18},{10... | collective-permute-start | bytes 393224 | tf_op jit(solution)/shard_map/ppermute | solution.py:399
  36.3 6.2 %collective-permute-start.14 = (bf16[128,512]{1,0:T(8,128)(2,1)S(1)}, bf16[128,512]{1,0:T(8,128)(2,1)S(1)}, u32[]{:S(2)}, u32[]{:S(2)}) collective-permute-start(bf16[128,512]{1,0:T(8,128)(2,1)S(1)} %get-tuple-element.41), channel_id=1, source_target_pairs={{0,16},{8,24},{16,0},{24,8},{1,17},{9,25},{17,1},{25,9},{2,18},{10... | collective-permute-start | bytes 393224 | tf_op jit(solution)/shard_map/ppermute | solution.py:399
  40.3 2.4 %collective-permute-start.17 = (bf16[2,128,512]{2,1,0:T(8,128)(2,1)S(1)}, bf16[2,128,512]{2,1,0:T(8,128)(2,1)S(1)}, u32[]{:S(2)}, u32[]{:S(2)}) collective-permute-start(bf16[2,128,512]{2,1,0:T(8,128)(2,1)S(1)} %get-tuple-element.52), channel_id=1, source_target_pairs={{0,8},{8,0},{16,24},{24,16},{1,9},{9,1},{17,25},{25,17},{2,10},{10... | collective-permute-start | bytes 786440 | tf_op jit(solution)/shard_map/ppermute | solution.py:408
  42.6 1.6 %collective-permute-start.15 = (bf16[2,128,512]{2,1,0:T(8,128)(2,1)S(1)}, bf16[2,128,512]{2,1,0:T(8,128)(2,1)S(1)}, u32[]{:S(2)}, u32[]{:S(2)}) collective-permute-start(bf16[2,128,512]{2,1,0:T(8,128)(2,1)S(1)} %get-tuple-element.45), channel_id=1, source_target_pairs={{0,8},{8,0},{16,24},{24,16},{1,9},{9,1},{17,25},{25,17},{2,10},{10... | collective-permute-start | bytes 786440 | tf_op jit(solution)/shard_map/ppermute | solution.py:408

commit v4 on v3

--- a/solution.py
+++ b/solution.py
@@ -58,36 +58,36 @@
 def load_tiles(tiles, cols, counts, order):
     snaps, rows, parts, slots, blk, _ = tiles.shape
     half = rows // CORES
+    entries = snaps * rows * parts * slots
     spot = [0] * parts
     for i, d in enumerate(order):
         spot[d] = i
-
-    def kernel(tiles, cols, counts, out, table, sems):
+    slot = lax.broadcasted_iota(jnp.int32, (snaps, rows, slots, parts), 2)
+    live = jnp.where(slot < counts[:, :, None, :], jnp.swapaxes(cols, 2, 3), -1)
+
+    def kernel(tiles, live, out, table, sems):
         core, _ = where_am_i()
+        copies = []
+        for snap in range(snaps):
+            for h in range(CORES):
+                row = lax.rem(core + h, CORES) * half
+                copies.append(
+                    pltpu.make_async_copy(
+                        tiles.at[snap, pl.ds(row, half)], out.at[snap, pl.ds(h * half, half)], sems.at[snap, h]
+                    )
+                )
+                copies[-1].start()
         here = lookup(spot, lax.axis_index("dom"))
         parts_at = [lookup(order, lax.rem(here + step, parts)) for step in range(parts)]
-        copies = []
-        for snap in range(snaps):
-            for step in range(parts):
-                for h in range(CORES):
-                    row = lax.rem(core + h, CORES) * half
-                    copies.append(
-                        pltpu.make_async_copy(
-                            tiles.at[snap, pl.ds(row, half), parts_at[step]],
-                            out.at[snap, pl.ds(h * half, half), step],
-                            sems.at[snap, step, h],
-                        )
-                    )
-                    copies[-1].start()
+        for step in range(parts):
+            table[entries + step] = parts_at[step]
 
         def fill(at, carry):
             snap, rel = at // rows, at % rows
             row = lax.rem(rel + core * half, rows)
             for step in range(parts):
-                count = counts[snap, row, parts_at[step]]
                 for k in range(slots):
-                    col = cols[snap, row, k, parts_at[step]]
-                    table[(at * parts + step) * slots + k] = jnp.where(k < count, col, -1)
+                    table[(at * parts + step) * slots + k] = live[snap, row, k, parts_at[step]]
             return carry
 
         lax.fori_loop(0, snaps * rows, fill, 0)
@@ -98,24 +98,25 @@
         kernel,
         out_shape=(
             jax.ShapeDtypeStruct(tiles.shape, tiles.dtype),
-            jax.ShapeDtypeStruct((snaps * rows * parts * slots,), jnp.int32),
+            jax.ShapeDtypeStruct((entries + parts,), jnp.int32),
         ),
-        in_specs=[whole(pltpu.MemorySpace.HBM), whole(SMEM), whole(SMEM)],
+        in_specs=[whole(pltpu.MemorySpace.HBM), whole(SMEM)],
         out_specs=(whole(), whole(SMEM)),
-        scratch_shapes=[pltpu.SemaphoreType.DMA((snaps, parts, CORES))],
+        scratch_shapes=[pltpu.SemaphoreType.DMA((snaps, CORES))],
         compiler_params=params(44),
         cost_estimate=cost(0, 2**20),
         name="load_tiles",
-    )(tiles, jnp.swapaxes(cols, 2, 3), counts)
+    )(tiles, live)
 
 
 def picked(table, tiles, x_block, snap, rel, step, lhs, rhs):
-    rows, parts, slots, blk = tiles.shape[1:5]
+    snaps, rows, parts, slots, blk, _ = tiles.shape
+    part = table[snaps * rows * parts * slots + step]
     for k in range(slots):
         col = table[((snap * rows + rel) * parts + step) * slots + k]
         block = x_block(pl.ds(pl.multiple_of(jnp.maximum(col, 0) * blk, blk), blk))
         rhs.append(jnp.where(col >= 0, block, jnp.zeros_like(block)))
-        lhs.append(tiles[snap, rel, step, k])
+        lhs.append(tiles[snap, rel, part, k])
 
 
 def product(lhs, rhs):
@@ -363,13 +364,11 @@
                     forward[s] = lax.ppermute(forward[s], "dom", ahead)
                 else:
                     reverse[s] = lax.ppermute(reverse[s], "dom", back)
+        acc = spmm(table, tiles, *waiting.pop(0), acc)
+        for s in range(snaps):
+            passing = forward if s % 2 == 0 else reverse
+            passing[s], acc = lax.optimization_barrier((passing[s], acc))
         waiting.append((forward + reverse, [parts - hop, hop]))
-        if hop > 2:
-            acc = spmm(table, tiles, *waiting.pop(0), acc)
-            first = [forward[s] if s % 2 == 0 else reverse[s] for s in range(snaps)]
-            first, acc = lax.optimization_barrier((first, acc))
-            forward = [first[s] if s % 2 == 0 else forward[s] for s in range(snaps)]
-            reverse = [first[s] if s % 2 == 1 else reverse[s] for s in range(snaps)]
     arriving = [
         lax.ppermute(forward[s], "dom", ahead) if s % 2 == 0 else lax.ppermute(reverse[s], "dom", back)
         for s in range(snaps)

time: 45.4 us -> 44.5 us (0.980)
  local copies, waits for them, and re-layouts: 1.47 us -> 0.07 us
  other arithmetic: 0 us -> 0.73 us
    ppermute x4, starting transfers between devices: 8.51 us -> 6.62 us  [per_device(): forward[s] = lax.ppermute(forward[s], 'dom', ahead)]
    ppermute x4, waiting for transfers between devices: 2.51 us -> 0.74 us  [per_device(): forward[s] = lax.ppermute(forward[s], 'dom', ahead)]
    unnamed x16 -> x12, local copies, waits for them, and re-layouts: 1.44 us -> 0.03 us
    ppermute x4, starting transfers between devices: 0.2 us -> 1.59 us  [per_device(): reverse[s] = lax.ppermute(reverse[s], 'dom', back)]
    ppermute x4, waiting for transfers between devices: 0.86 us -> 1.95 us  [per_device(): reverse[s] = lax.ppermute(reverse[s], 'dom', back)]
    ppermute x1, waiting for transfers between devices: 0.01 us -> 0.77 us  [per_device(): forward = lax.ppermute(features, 'dom', ahead)]
    select_n x0 -> x1, other arithmetic: none -> 0.73 us  [load_tiles(): live = jnp.where(slot < counts[:, :, None, :], jnp.swapaxes(cols, 2, 3), -1)]
    ppermute x1, waiting for transfers between devices: 0.26 us -> 0.87 us  [per_device(): lax.ppermute(reverse[s], 'dom', back)]
  transfers between devices with their start and end apart: 18 -> 18, of which waited for: 8 -> 9; matrix products, arithmetic and copies ran while one was open for 0% -> 2% of each run, Pallas kernels for 34% -> 34%
where the time goes in v4:
time: 44.5 us; the launch traced here: 44.2 us
  Pallas kernels  18 us (40%)
  starting transfers between devices  14.8 us (33%)
  waiting for transfers between devices  10.3 us (23%)
  other arithmetic  0.73 us (2%)
    ppermute x4, starting transfers between devices, per_device(): forward[s] = lax.ppermute(forward[s], 'dom', ahead)  6.62 us
    ppermute x2, waiting for transfers between devices, per_device(): states = [lax.ppermute(state, 'tm', onward) for state in states]  5.37 us
    pallas_call x1, Pallas kernels, load_tiles(): pl.pallas_call(kernel, out_shape=(jax.ShapeDtypeStruct(tiles.shape, tiles...  4.94 us
    pallas_call x2, Pallas kernels, recurrence_first(): pl.pallas_call(kernel, out_shape=(jax.ShapeDtypeStruct((rows, hid), BF16)...  4.28 us
    pallas_call x3, Pallas kernels, spmm(): pl.pallas_call(kernel, out_shape=jax.ShapeDtypeStruct((snaps, rows, blk,...  4.22 us
    ppermute x1, starting transfers between devices, per_device(): forward = lax.ppermute(features, 'dom', ahead)  3.02 us
    ppermute x4, waiting for transfers between devices, per_device(): reverse[s] = lax.ppermute(reverse[s], 'dom', back)  1.95 us
    pallas_call x2, Pallas kernels, spmm_last(): pl.pallas_call(kernel, out_shape=(part, part), in_specs=[whole(SMEM)] + [...  1.74 us
  transfers between devices with their start and end apart: 18, of which 9 were waited for; matrix products, arithmetic and copies ran while one was open for 2% of the time, Pallas kernels for 34%

profile of v4, /device:TPU:0, one launch (start us, length us, event | category | flops | bytes accessed | tf_op | source)
XLA Modules:
  0.0 44.2 jit_solution(690108730974752128)
XLA Ops:
  0.0 3.0 %collective-permute-start = (bf16[2,512,128]{2,1,0:T(8,128)(2,1)}, bf16[2,512,128]{2,1,0:T(8,128)(2,1)S(1)}, u32[]{:S(2)}, u32[]{:S(2)}) collective-permute-start(bf16[2,512,128]{2,1,0:T(8,128)(2,1)} %refs_0_.1), channel_id=1, source_target_pairs={{0,2},{2,4},{4,6},{6,7},{7,5},{5,3},{3,1},{1,0},{8,10},{10,12},{12... | collective-permute-start | bytes 786440 | tf_op jit(solution)/shard_map/ppermute | solution.py:352
  3.0 0.7 %bitcast_select_fusion.live = s32[2,4,4,8]{3,2,1,0:T(4,128)S(1)} fusion(s32[2,4,8,4]{2,3,1,0:T(4,128)} %param.11, s32[2,4,8]{2,1,0:T(4,128)} %param.12), kind=kLoop, calls=%fused_computation.4 | loop fusion | flops 512 | bytes 2304 | tf_op jit(solution)/shard_map/jit(_where)/select_n | solution.py:66
  3.8 4.9 %load_tiles.1 = (bf16[2,4,8,4,128,128]{5,4,3,2,1,0:T(8,128)(2,1)S(1)}, s32[264]{0:T(512)S(1)}) custom-call(bf16[2,4,8,4,128,128]{5,4,3,2,1,0:T(8,128)(2,1)} %tiles.1, s32[2,4,4,8]{3,2,1,0:T(4,128)S(1)} %bitcast_select_fusion.live), custom_call_target="tpu_custom_call" | custom-call | bytes 1048576 | tf_op jit(solution)/shard_map/load_tiles/pallas_call | solution.py:97
  8.7 0.8 %collective-permute-done.refs_1_ = bf16[2,512,128]{2,1,0:T(8,128)(2,1)S(1)} collective-permute-done((bf16[2,512,128]{2,1,0:T(8,128)(2,1)}, bf16[2,512,128]{2,1,0:T(8,128)(2,1)S(1)}, u32[]{:S(2)}, u32[]{:S(2)}) %collective-permute-start) | collective-permute-done | bytes 262176 | tf_op jit(solution)/shard_map/ppermute | solution.py:352
  9.5 1.9 %collective-permute-start.1 = (bf16[512,128]{1,0:T(8,128)(2,1)S(1)}, bf16[512,128]{1,0:T(8,128)(2,1)S(1)}, u32[]{:S(2)}, u32[]{:S(2)}) collective-permute-start(bf16[512,128]{1,0:T(8,128)(2,1)S(1)} %get-tuple-element.66), channel_id=1, source_target_pairs={{0,2},{2,4},{4,6},{6,7},{7,5},{5,3},{3,1},{1,0},{8,10},{10,12},{12... | collective-permute-start | bytes 393224 | tf_op jit(solution)/shard_map/ppermute | solution.py:364
  11.7 1.8 %collective-permute-start.4 = (bf16[512,128]{1,0:T(8,128)(2,1)S(1)}, bf16[512,128]{1,0:T(8,128)(2,1)S(1)}, u32[]{:S(2)}, u32[]{:S(2)}) collective-permute-start(bf16[512,128]{1,0:T(8,128)(2,1)S(1)} %get-tuple-element.65), channel_id=1, source_target_pairs={{0,2},{2,4},{4,6},{6,7},{7,5},{5,3},{3,1},{1,0},{8,10},{10,12},{12... | collective-permute-start | bytes 393224 | tf_op jit(solution)/shard_map/ppermute | solution.py:364
  13.7 1.6 %spmm.3.refs_4_ = f32[2,4,128,128]{3,2,1,0:T(8,128)S(1)} custom-call(s32[264]{0:T(512)S(1)} %get-tuple-element.36.table, bf16[2,4,8,4,128,128]{5,4,3,2,1,0:T(8,128)(2,1)S(1)} %get-tuple-element.37.tiles, bf16[2,512,128]{2,1,0:T(8,128)(2,1)S(1)} %copy-done.3, bf16[2,512,128]{2,1,0:T(8,128)(2,1)S(1)} %collective-permute-done.refs_1_, ...), custom_call_target="tpu_custom_call" | custom-call | flops 1610612736 | bytes 1048576 | tf_op jit(solution)/shard_map/spmm/pallas_call | solution.py:145
  15.4 0.4 collective-permute-done.1.refs_0_
  15.8 1.5 %collective-permute-start.3 = (bf16[512,128]{1,0:T(8,128)(2,1)S(1)}, bf16[512,128]{1,0:T(8,128)(2,1)S(1)}, u32[]{:S(2)}, u32[]{:S(2)}) collective-permute-start(bf16[512,128]{1,0:T(8,128)(2,1)S(1)} %collective-permute-done.1.refs_0_), channel_id=1, source_target_pairs={{0,2},{2,4},{4,6},{6,7},{7,5},{5,3},{3,1},{1,0},{8,10},{10,12},{12... | collective-permute-start | bytes 393224 | tf_op jit(solution)/shard_map/ppermute | solution.py:364
  17.3 0.5 %collective-permute-start.10 = (bf16[512,128]{1,0:T(8,128)(2,1)S(1)}, bf16[512,128]{1,0:T(8,128)(2,1)S(1)}, u32[]{:S(2)}, u32[]{:S(2)}) collective-permute-start(bf16[512,128]{1,0:T(8,128)(2,1)S(1)} %collective-permute-done.6.refs_3_), channel_id=1, source_target_pairs={{2,0},{4,2},{6,4},{7,6},{5,7},{3,5},{1,3},{0,1},{10,8},{12,10},{14... | collective-permute-start | bytes 393224 | tf_op jit(solution)/shard_map/ppermute | solution.py:366
  17.8 0.3 collective-permute-done.4.refs_1_
  18.1 1.5 %collective-permute-start.8 = (bf16[512,128]{1,0:T(8,128)(2,1)S(1)}, bf16[512,128]{1,0:T(8,128)(2,1)S(1)}, u32[]{:S(2)}, u32[]{:S(2)}) collective-permute-start(bf16[512,128]{1,0:T(8,128)(2,1)S(1)} %collective-permute-done.4.refs_1_), channel_id=1, source_target_pairs={{0,2},{2,4},{4,6},{6,7},{7,5},{5,3},{3,1},{1,0},{8,10},{10,12},{12... | collective-permute-start | bytes 393224 | tf_op jit(solution)/shard_map/ppermute | solution.py:364
  19.6 0.5 %collective-permute-start.9 = (bf16[512,128]{1,0:T(8,128)(2,1)S(1)}, bf16[512,128]{1,0:T(8,128)(2,1)S(1)}, u32[]{:S(2)}, u32[]{:S(2)}) collective-permute-start(bf16[512,128]{1,0:T(8,128)(2,1)S(1)} %collective-permute-done.5.refs_2_), channel_id=1, source_target_pairs={{2,0},{4,2},{6,4},{7,6},{5,7},{3,5},{1,3},{0,1},{10,8},{12,10},{14... | collective-permute-start | bytes 393224 | tf_op jit(solution)/shard_map/ppermute | solution.py:366
  20.2 1.3 %spmm.4.refs_4_ = f32[2,4,128,128]{3,2,1,0:T(8,128)S(1)} custom-call(s32[264]{0:T(512)S(1)} %get-tuple-element.36.table, bf16[2,4,8,4,128,128]{5,4,3,2,1,0:T(8,128)(2,1)S(1)} %get-tuple-element.37.tiles, bf16[512,128]{1,0:T(8,128)(2,1)S(1)} %collective-permute-done.1.refs_0_, bf16[512,128]{1,0:T(8,128)(2,1)S(1)} %collective-permute-done.4.refs_1_, ...), custom_call_target="tpu_custom_call" | custom-call | flops 1073741824 | bytes 1048576 | tf_op jit(solution)/shard_map/spmm/pallas_call | solution.py:145
  21.5 1.2 %collective-permute-done.10.refs_3_ = bf16[512,128]{1,0:T(8,128)(2,1)S(1)} collective-permute-done((bf16[512,128]{1,0:T(8,128)(2,1)S(1)}, bf16[512,128]{1,0:T(8,128)(2,1)S(1)}, u32[]{:S(2)}, u32[]{:S(2)}) %collective-permute-start.10) | collective-permute-done | bytes 131104 | tf_op jit(solution)/shard_map/ppermute | solution.py:366
  22.7 0.7 %collective-permute-start.11 = (bf16[512,128]{1,0:T(8,128)(2,1)S(1)}, bf16[512,128]{1,0:T(8,128)(2,1)S(1)}, u32[]{:S(2)}, u32[]{:S(2)}) collective-permute-start(bf16[512,128]{1,0:T(8,128)(2,1)S(1)} %collective-permute-done.10.refs_3_), channel_id=1, source_target_pairs={{2,0},{4,2},{6,4},{7,6},{5,7},{3,5},{1,3},{0,1},{10,8},{12,10},{14... | collective-permute-start | bytes 393224 | tf_op jit(solution)/shard_map/ppermute | solution.py:373
  23.4 1.3 %collective-permute-start.7 = (bf16[512,128]{1,0:T(8,128)(2,1)S(1)}, bf16[512,128]{1,0:T(8,128)(2,1)S(1)}, u32[]{:S(2)}, u32[]{:S(2)}) collective-permute-start(bf16[512,128]{1,0:T(8,128)(2,1)S(1)} %collective-permute-done.3.refs_0_), channel_id=1, source_target_pairs={{0,2},{2,4},{4,6},{6,7},{7,5},{5,3},{3,1},{1,0},{8,10},{10,12},{12... | collective-permute-start | bytes 393224 | tf_op jit(solution)/shard_map/ppermute | solution.py:373
  24.7 0.7 %collective-permute-done.9.refs_2_ = bf16[512,128]{1,0:T(8,128)(2,1)S(1)} collective-permute-done((bf16[512,128]{1,0:T(8,128)(2,1)S(1)}, bf16[512,128]{1,0:T(8,128)(2,1)S(1)}, u32[]{:S(2)}, u32[]{:S(2)}) %collective-permute-start.9) | collective-permute-done | bytes 131104 | tf_op jit(solution)/shard_map/ppermute | solution.py:366
  25.5 1.3 %spmm.5.acc_in = f32[2,4,128,128]{3,2,1,0:T(8,128)S(1)} custom-call(s32[264]{0:T(512)S(1)} %get-tuple-element.36.table, bf16[2,4,8,4,128,128]{5,4,3,2,1,0:T(8,128)(2,1)S(1)} %get-tuple-element.37.tiles, bf16[512,128]{1,0:T(8,128)(2,1)S(1)} %collective-permute-done.3.refs_0_, bf16[512,128]{1,0:T(8,128)(2,1)S(1)} %collective-permute-done.8.refs_1_, ...), custom_call_target="tpu_custom_call" | custom-call | flops 1073741824 | bytes 1048576 | tf_op jit(solution)/shard_map/spmm/pallas_call | solution.py:145
  26.8 0.9 %collective-permute-done.11.x_ref = bf16[512,128]{1,0:T(8,128)(2,1)S(1)} collective-permute-done((bf16[512,128]{1,0:T(8,128)(2,1)S(1)}, bf16[512,128]{1,0:T(8,128)(2,1)S(1)}, u32[]{:S(2)}, u32[]{:S(2)}) %collective-permute-start.11) | collective-permute-done | bytes 131104 | tf_op jit(solution)/shard_map/ppermute | solution.py:373
  27.6 0.9 %spmm_last.3 = (bf16[256,128]{1,0:T(8,128)(2,1)S(1)}, bf16[256,128]{1,0:T(8,128)(2,1)S(1)}) custom-call(s32[264]{0:T(512)S(1)} %get-tuple-element.36.table, bf16[2,4,8,4,128,128]{5,4,3,2,1,0:T(8,128)(2,1)S(1)} %get-tuple-element.37.tiles, bf16[512,128]{1,0:T(8,128)(2,1)S(1)} %collective-permute-done.11.x_ref, f32[2,4,128,128]{3,2,1,0:T(8,128)S(1)} %spmm.5.acc_in), custom_call_target="tpu_custom_call" | custom-call | flops 268435456 | bytes 1048576 | tf_op jit(solution)/shard_map/spmm_last/pallas_call | solution.py:169
  28.6 0.9 %spmm_last.2 = (bf16[256,128]{1,0:T(8,128)(2,1)S(1)}, bf16[256,128]{1,0:T(8,128)(2,1)S(1)}) custom-call(s32[264]{0:T(512)S(1)} %get-tuple-element.36.table, bf16[2,4,8,4,128,128]{5,4,3,2,1,0:T(8,128)(2,1)S(1)} %get-tuple-element.37.tiles, bf16[512,128]{1,0:T(8,128)(2,1)S(1)} %collective-permute-done.7.x_ref, f32[2,4,128,128]{3,2,1,0:T(8,128)S(1)} %spmm.5.acc_in), custom_call_target="tpu_custom_call" | custom-call | flops 268435456 | bytes 1048576 | tf_op jit(solution)/shard_map/spmm_last/pallas_call | solution.py:169
  29.5 0.6 %collective-permute-start.12 = (bf16[256,128]{1,0:T(8,128)(2,1)S(1)}, bf16[256,128]{1,0:T(8,128)(2,1)S(1)}, u32[]{:S(2)}, u32[]{:S(2)}) collective-permute-start(bf16[256,128]{1,0:T(8,128)(2,1)S(1)} %get-tuple-element.49), channel_id=1, source_target_pairs={{0,8},{8,0},{16,24},{24,16},{1,9},{9,1},{17,25},{25,17},{2,10},{10... | collective-permute-start | bytes 196616 | tf_op jit(solution)/shard_map/ppermute | solution.py:384
  30.0 1.1 %gates.1.gx_own = f32[2,256,1536]{2,1,0:T(8,128)S(1)} custom-call(bf16[256,128]{1,0:T(8,128)(2,1)S(1)} %get-tuple-element.47.refs_0_, bf16[256,128]{1,0:T(8,128)(2,1)S(1)} %get-tuple-element.48.refs_1_, bf16[128,512]{1,0:T(8,128)(2,1)S(1)} %copy-done.4, bf16[512,1536]{1,0:T(8,128)(2,1)S(1)} %copy-done), custom_call_target="tpu_custom_call" | custom-call | flops 1610612736 | bytes 1048576 | tf_op jit(solution)/shard_map/gates/pallas_call | solution.py:197
  31.2 2.2 %recurrence_first.3 = (bf16[128,512]{1,0:T(8,128)(2,1)S(1)}, bf16[2,128,512]{2,1,0:T(8,128)(2,1)S(1)}, bf16[2,128,512]{2,1,0:T(8,128)(2,1)S(1)}, f32[2,128,1536]{2,1,0:T(8,128)S(1)}) custom-call(f32[512,512]{1,0:T(8,128)S(1)} %copy-done.2, f32[2,256,1536]{2,1,0:T(8,128)S(1)} %gates.1.gx_own, bf16[128,512]{1,0:T(8,128)(2,1)S(1)} %copy-done.4, ...), custom_call_target="tpu_custom_call" | custom-call | flops 3221225472 | bytes 1048576 | tf_op jit(solution)/shard_map/recurrence_first/pallas_call | solution.py:257
  33.5 2.1 %recurrence_first.2 = (bf16[128,512]{1,0:T(8,128)(2,1)S(1)}, bf16[2,128,512]{2,1,0:T(8,128)(2,1)S(1)}, bf16[2,128,512]{2,1,0:T(8,128)(2,1)S(1)}, f32[2,128,1536]{2,1,0:T(8,128)S(1)}) custom-call(f32[512,512]{1,0:T(8,128)S(1)} %copy-done.2, f32[2,256,1536]{2,1,0:T(8,128)S(1)} %gates.1.gx_own, bf16[128,512]{1,0:T(8,128)(2,1)S(1)} %copy-done.4, ...), custom_call_target="tpu_custom_call" | custom-call | flops 3221225472 | bytes 1048576 | tf_op jit(solution)/shard_map/recurrence_first/pallas_call | solution.py:257
  35.6 0.6 %collective-permute-start.14 = (bf16[128,512]{1,0:T(8,128)(2,1)S(1)}, bf16[128,512]{1,0:T(8,128)(2,1)S(1)}, u32[]{:S(2)}, u32[]{:S(2)}) collective-permute-start(bf16[128,512]{1,0:T(8,128)(2,1)S(1)} %get-tuple-element.51), channel_id=1, source_target_pairs={{0,16},{8,24},{16,0},{24,8},{1,17},{9,25},{17,1},{25,9},{2,18},{10... | collective-permute-start | bytes 393224 | tf_op jit(solution)/shard_map/ppermute | solution.py:398
  36.2 3.2 %collective-permute-done.16.state_in = bf16[128,512]{1,0:T(8,128)(2,1)S(1)} collective-permute-done((bf16[128,512]{1,0:T(8,128)(2,1)S(1)}, bf16[128,512]{1,0:T(8,128)(2,1)S(1)}, u32[]{:S(2)}, u32[]{:S(2)}) %collective-permute-start.16) | collective-permute-done | bytes 131104 | tf_op jit(solution)/shard_map/ppermute | solution.py:398
  39.6 2.1 %collective-permute-done.14.state_in = bf16[128,512]{1,0:T(8,128)(2,1)S(1)} collective-permute-done((bf16[128,512]{1,0:T(8,128)(2,1)S(1)}, bf16[128,512]{1,0:T(8,128)(2,1)S(1)}, u32[]{:S(2)}, u32[]{:S(2)}) %collective-permute-start.14) | collective-permute-done | bytes 131104 | tf_op jit(solution)/shard_map/ppermute | solution.py:398
  41.8 0.9 %write_out.2.refs_1_ = bf16[2,512,512]{2,1,0:T(8,128)(2,1)} custom-call(bf16[2,128,512]{2,1,0:T(8,128)(2,1)S(1)} %get-tuple-element.60.refs_0_, bf16[2,128,512]{2,1,0:T(8,128)(2,1)S(1)} %get-tuple-element.61.refs_1_, bf16[2,128,512]{2,1,0:T(8,128)(2,1)S(1)} %collective-permute-done.17.refs_2_), custom_call_target="tpu_custom_call" | custom-call | bytes 1048576 | tf_op jit(solution)/shard_map/write_out/pallas_call | solution.py:326
  42.8 0.6 %collective-permute-done.15.refs_0_ = bf16[2,128,512]{2,1,0:T(8,128)(2,1)S(1)} collective-permute-done((bf16[2,128,512]{2,1,0:T(8,128)(2,1)S(1)}, bf16[2,128,512]{2,1,0:T(8,128)(2,1)S(1)}, u32[]{:S(2)}, u32[]{:S(2)}) %collective-permute-start.15) | collective-permute-done | bytes 262176 | tf_op jit(solution)/shard_map/ppermute | solution.py:407
  43.3 0.7 %write_out.3 = bf16[2,512,512]{2,1,0:T(8,128)(2,1)} custom-call(bf16[2,128,512]{2,1,0:T(8,128)(2,1)S(1)} %collective-permute-done.15.refs_0_, bf16[2,512,512]{2,1,0:T(8,128)(2,1)} %write_out.2.refs_1_), custom_call_target="tpu_custom_call", output_to_operand_aliasing={{}: (1, {})} | custom-call | bytes 1048576 | tf_op jit(solution)/shard_map/write_out/pallas_call | solution.py:326
  (32 shorter events, 1.0 us)
Async XLA Ops:
  0.0 9.5 %collective-permute-start = (bf16[2,512,128]{2,1,0:T(8,128)(2,1)}, bf16[2,512,128]{2,1,0:T(8,128)(2,1)S(1)}, u32[]{:S(2)}, u32[]{:S(2)}) collective-permute-start(bf16[2,512,128]{2,1,0:T(8,128)(2,1)} %refs_0_.1), channel_id=1, source_target_pairs={{0,2},{2,4},{4,6},{6,7},{7,5},{5,3},{3,1},{1,0},{8,10},{10,12},{12... | collective-permute-start | bytes 786440 | tf_op jit(solution)/shard_map/ppermute | solution.py:352
  3.0 8.3 %collective-permute-start.2 = (bf16[2,512,128]{2,1,0:T(8,128)(2,1)}, bf16[2,512,128]{2,1,0:T(8,128)(2,1)S(1)}, u32[]{:S(2)}, u32[]{:S(2)}) collective-permute-start(bf16[2,512,128]{2,1,0:T(8,128)(2,1)} %refs_0_.1), channel_id=1, source_target_pairs={{2,0},{4,2},{6,4},{7,6},{5,7},{3,5},{1,3},{0,1},{10,8},{12,10},{14... | collective-permute-start | bytes 786440 | tf_op jit(solution)/shard_map/ppermute | solution.py:353
  3.8 9.9 %copy-start.3 = (bf16[2,512,128]{2,1,0:T(8,128)(2,1)S(1)}, bf16[2,512,128]{2,1,0:T(8,128)(2,1)}, u32[]{:S(2)}) copy-start(bf16[2,512,128]{2,1,0:T(8,128)(2,1)} %refs_0_.1) | copy-start | bytes 786436
  9.5 6.3 %collective-permute-start.1 = (bf16[512,128]{1,0:T(8,128)(2,1)S(1)}, bf16[512,128]{1,0:T(8,128)(2,1)S(1)}, u32[]{:S(2)}, u32[]{:S(2)}) collective-permute-start(bf16[512,128]{1,0:T(8,128)(2,1)S(1)} %get-tuple-element.66), channel_id=1, source_target_pairs={{0,2},{2,4},{4,6},{6,7},{7,5},{5,3},{3,1},{1,0},{8,10},{10,12},{12... | collective-permute-start | bytes 393224 | tf_op jit(solution)/shard_map/ppermute | solution.py:364
  11.4 5.9 %collective-permute-start.6 = (bf16[512,128]{1,0:T(8,128)(2,1)S(1)}, bf16[512,128]{1,0:T(8,128)(2,1)S(1)}, u32[]{:S(2)}, u32[]{:S(2)}) collective-permute-start(bf16[512,128]{1,0:T(8,128)(2,1)S(1)} %get-tuple-element.63), channel_id=1, source_target_pairs={{2,0},{4,2},{6,4},{7,6},{5,7},{3,5},{1,3},{0,1},{10,8},{12,10},{14... | collective-permute-start | bytes 393224 | tf_op jit(solution)/shard_map/ppermute | solution.py:366
  11.7 6.5 %collective-permute-start.4 = (bf16[512,128]{1,0:T(8,128)(2,1)S(1)}, bf16[512,128]{1,0:T(8,128)(2,1)S(1)}, u32[]{:S(2)}, u32[]{:S(2)}) collective-permute-start(bf16[512,128]{1,0:T(8,128)(2,1)S(1)} %get-tuple-element.65), channel_id=1, source_target_pairs={{0,2},{2,4},{4,6},{6,7},{7,5},{5,3},{3,1},{1,0},{8,10},{10,12},{12... | collective-permute-start | bytes 393224 | tf_op jit(solution)/shard_map/ppermute | solution.py:364
  13.5 6.2 %collective-permute-start.5 = (bf16[512,128]{1,0:T(8,128)(2,1)S(1)}, bf16[512,128]{1,0:T(8,128)(2,1)S(1)}, u32[]{:S(2)}, u32[]{:S(2)}) collective-permute-start(bf16[512,128]{1,0:T(8,128)(2,1)S(1)} %get-tuple-element.64), channel_id=1, source_target_pairs={{2,0},{4,2},{6,4},{7,6},{5,7},{3,5},{1,3},{0,1},{10,8},{12,10},{14... | collective-permute-start | bytes 393224 | tf_op jit(solution)/shard_map/ppermute | solution.py:366
  15.3 10.1 %copy-start = (bf16[512,1536]{1,0:T(8,128)(2,1)S(1)}, bf16[512,1536]{1,0:T(8,128)(2,1)}, u32[]{:S(2)}) copy-start(bf16[512,1536]{1,0:T(8,128)(2,1)} %w_input.3) | copy-start | bytes 4718596
  15.3 10.1 %copy-start.1 = (bf16[512,1536]{1,0:T(8,128)(2,1)S(1)}, bf16[512,1536]{1,0:T(8,128)(2,1)}, u32[]{:S(2)}) copy-start(bf16[512,1536]{1,0:T(8,128)(2,1)} %w_hidden.7) | copy-start | bytes 4718596
  15.3 10.1 %copy-start.2 = (f32[512,512]{1,0:T(8,128)S(1)}, f32[512,512]{1,0:T(8,128)}, u32[]{:S(2)}) copy-start(f32[512,512]{1,0:T(8,128)} %hidden_start.3) | copy-start | bytes 3145732
  15.4 10.1 %copy-start.4 = (bf16[128,512]{1,0:T(8,128)(2,1)S(1)}, bf16[128,512]{1,0:T(8,128)(2,1)}, u32[]{:S(2)}) copy-start(bf16[128,512]{1,0:T(8,128)(2,1)} %w_graph.3) | copy-start | bytes 393220
  15.8 5.7 %collective-permute-start.3 = (bf16[512,128]{1,0:T(8,128)(2,1)S(1)}, bf16[512,128]{1,0:T(8,128)(2,1)S(1)}, u32[]{:S(2)}, u32[]{:S(2)}) collective-permute-start(bf16[512,128]{1,0:T(8,128)(2,1)S(1)} %collective-permute-done.1.refs_0_), channel_id=1, source_target_pairs={{0,2},{2,4},{4,6},{6,7},{7,5},{5,3},{3,1},{1,0},{8,10},{10,12},{12... | collective-permute-start | bytes 393224 | tf_op jit(solution)/shard_map/ppermute | solution.py:364
  17.3 5.4 %collective-permute-start.10 = (bf16[512,128]{1,0:T(8,128)(2,1)S(1)}, bf16[512,128]{1,0:T(8,128)(2,1)S(1)}, u32[]{:S(2)}, u32[]{:S(2)}) collective-permute-start(bf16[512,128]{1,0:T(8,128)(2,1)S(1)} %collective-permute-done.6.refs_3_), channel_id=1, source_target_pairs={{2,0},{4,2},{6,4},{7,6},{5,7},{3,5},{1,3},{0,1},{10,8},{12,10},{14... | collective-permute-start | bytes 393224 | tf_op jit(solution)/shard_map/ppermute | solution.py:366
  18.1 6.6 %collective-permute-start.8 = (bf16[512,128]{1,0:T(8,128)(2,1)S(1)}, bf16[512,128]{1,0:T(8,128)(2,1)S(1)}, u32[]{:S(2)}, u32[]{:S(2)}) collective-permute-start(bf16[512,128]{1,0:T(8,128)(2,1)S(1)} %collective-permute-done.4.refs_1_), channel_id=1, source_target_pairs={{0,2},{2,4},{4,6},{6,7},{7,5},{5,3},{3,1},{1,0},{8,10},{10,12},{12... | collective-permute-start | bytes 393224 | tf_op jit(solution)/shard_map/ppermute | solution.py:364
  19.6 5.8 %collective-permute-start.9 = (bf16[512,128]{1,0:T(8,128)(2,1)S(1)}, bf16[512,128]{1,0:T(8,128)(2,1)S(1)}, u32[]{:S(2)}, u32[]{:S(2)}) collective-permute-start(bf16[512,128]{1,0:T(8,128)(2,1)S(1)} %collective-permute-done.5.refs_2_), channel_id=1, source_target_pairs={{2,0},{4,2},{6,4},{7,6},{5,7},{3,5},{1,3},{0,1},{10,8},{12,10},{14... | collective-permute-start | bytes 393224 | tf_op jit(solution)/shard_map/ppermute | solution.py:366
  22.7 5.0 %collective-permute-start.11 = (bf16[512,128]{1,0:T(8,128)(2,1)S(1)}, bf16[512,128]{1,0:T(8,128)(2,1)S(1)}, u32[]{:S(2)}, u32[]{:S(2)}) collective-permute-start(bf16[512,128]{1,0:T(8,128)(2,1)S(1)} %collective-permute-done.10.refs_3_), channel_id=1, source_target_pairs={{2,0},{4,2},{6,4},{7,6},{5,7},{3,5},{1,3},{0,1},{10,8},{12,10},{14... | collective-permute-start | bytes 393224 | tf_op jit(solution)/shard_map/ppermute | solution.py:373
  23.4 5.2 %collective-permute-start.7 = (bf16[512,128]{1,0:T(8,128)(2,1)S(1)}, bf16[512,128]{1,0:T(8,128)(2,1)S(1)}, u32[]{:S(2)}, u32[]{:S(2)}) collective-permute-start(bf16[512,128]{1,0:T(8,128)(2,1)S(1)} %collective-permute-done.3.refs_0_), channel_id=1, source_target_pairs={{0,2},{2,4},{4,6},{6,7},{7,5},{5,3},{3,1},{1,0},{8,10},{10,12},{12... | collective-permute-start | bytes 393224 | tf_op jit(solution)/shard_map/ppermute | solution.py:373
  28.5 2.6 %collective-permute-start.13 = (bf16[256,128]{1,0:T(8,128)(2,1)S(1)}, bf16[256,128]{1,0:T(8,128)(2,1)S(1)}, u32[]{:S(2)}, u32[]{:S(2)}) collective-permute-start(bf16[256,128]{1,0:T(8,128)(2,1)S(1)} %get-tuple-element.50), channel_id=1, source_target_pairs={{0,8},{8,0},{16,24},{24,16},{1,9},{9,1},{17,25},{25,17},{2,10},{10... | collective-permute-start | bytes 196616 | tf_op jit(solution)/shard_map/ppermute | solution.py:384
  29.5 1.7 %collective-permute-start.12 = (bf16[256,128]{1,0:T(8,128)(2,1)S(1)}, bf16[256,128]{1,0:T(8,128)(2,1)S(1)}, u32[]{:S(2)}, u32[]{:S(2)}) collective-permute-start(bf16[256,128]{1,0:T(8,128)(2,1)S(1)} %get-tuple-element.49), channel_id=1, source_target_pairs={{0,8},{8,0},{16,24},{24,16},{1,9},{9,1},{17,25},{25,17},{2,10},{10... | collective-permute-start | bytes 196616 | tf_op jit(solution)/shard_map/ppermute | solution.py:384
  30.0 1.1 %copy-start.5 = (f32[512]{0:T(512)S(1)}, f32[512]{0:T(512)}, u32[]{:S(2)}) copy-start(f32[512]{0:T(512)} %param.17) | copy-start | bytes 6148
  33.4 6.1 %collective-permute-start.16 = (bf16[128,512]{1,0:T(8,128)(2,1)S(1)}, bf16[128,512]{1,0:T(8,128)(2,1)S(1)}, u32[]{:S(2)}, u32[]{:S(2)}) collective-permute-start(bf16[128,512]{1,0:T(8,128)(2,1)S(1)} %get-tuple-element.56), channel_id=1, source_target_pairs={{0,16},{8,24},{16,0},{24,8},{1,17},{9,25},{17,1},{25,9},{2,18},{10... | collective-permute-start | bytes 393224 | tf_op jit(solution)/shard_map/ppermute | solution.py:398
  35.6 6.1 %collective-permute-start.14 = (bf16[128,512]{1,0:T(8,128)(2,1)S(1)}, bf16[128,512]{1,0:T(8,128)(2,1)S(1)}, u32[]{:S(2)}, u32[]{:S(2)}) collective-permute-start(bf16[128,512]{1,0:T(8,128)(2,1)S(1)} %get-tuple-element.51), channel_id=1, source_target_pairs={{0,16},{8,24},{16,0},{24,8},{1,17},{9,25},{17,1},{25,9},{2,18},{10... | collective-permute-start | bytes 393224 | tf_op jit(solution)/shard_map/ppermute | solution.py:398
  39.5 2.3 %collective-permute-start.17 = (bf16[2,128,512]{2,1,0:T(8,128)(2,1)S(1)}, bf16[2,128,512]{2,1,0:T(8,128)(2,1)S(1)}, u32[]{:S(2)}, u32[]{:S(2)}) collective-permute-start(bf16[2,128,512]{2,1,0:T(8,128)(2,1)S(1)} %get-tuple-element.62), channel_id=1, source_target_pairs={{0,8},{8,0},{16,24},{24,16},{1,9},{9,1},{17,25},{25,17},{2,10},{10... | collective-permute-start | bytes 786440 | tf_op jit(solution)/shard_map/ppermute | solution.py:407
  41.7 1.6 %collective-permute-start.15 = (bf16[2,128,512]{2,1,0:T(8,128)(2,1)S(1)}, bf16[2,128,512]{2,1,0:T(8,128)(2,1)S(1)}, u32[]{:S(2)}, u32[]{:S(2)}) collective-permute-start(bf16[2,128,512]{2,1,0:T(8,128)(2,1)S(1)} %get-tuple-element.55), channel_id=1, source_target_pairs={{0,8},{8,0},{16,24},{24,16},{1,9},{9,1},{17,25},{25,17},{2,10},{10... | collective-permute-start | bytes 786440 | tf_op jit(solution)/shard_map/ppermute | solution.py:407

commit v5 on v4

--- a/solution.py
+++ b/solution.py
@@ -11,6 +11,7 @@
 F32 = jnp.float32
 CORES = 2
 CHUNKS = 2
+COVER_FLOPS = 3e9
 VMEM = pltpu.MemorySpace.VMEM
 SMEM = pltpu.MemorySpace.SMEM
 
@@ -55,7 +56,7 @@
     return pl.BlockSpec(memory_space=memory)
 
 
-def load_tiles(tiles, cols, counts, order):
+def column_table(tiles, cols, counts, order):
     snaps, rows, parts, slots, blk, _ = tiles.shape
     half = rows // CORES
     entries = snaps * rows * parts * slots
@@ -65,22 +66,14 @@
     slot = lax.broadcasted_iota(jnp.int32, (snaps, rows, slots, parts), 2)
     live = jnp.where(slot < counts[:, :, None, :], jnp.swapaxes(cols, 2, 3), -1)
 
-    def kernel(tiles, live, out, table, sems):
+    def kernel(live, table):
         core, _ = where_am_i()
-        copies = []
-        for snap in range(snaps):
-            for h in range(CORES):
-                row = lax.rem(core + h, CORES) * half
-                copies.append(
-                    pltpu.make_async_copy(
-                        tiles.at[snap, pl.ds(row, half)], out.at[snap, pl.ds(h * half, half)], sems.at[snap, h]
-                    )
-                )
-                copies[-1].start()
         here = lookup(spot, lax.axis_index("dom"))
         parts_at = [lookup(order, lax.rem(here + step, parts)) for step in range(parts)]
         for step in range(parts):
             table[entries + step] = parts_at[step]
+        for rel in range(rows):
+            table[entries + parts + rel] = lax.rem(rel + core * half, rows)
 
         def fill(at, carry):
             snap, rel = at // rows, at % rows
@@ -91,32 +84,27 @@
             return carry
 
         lax.fori_loop(0, snaps * rows, fill, 0)
-        for copy in copies:
-            copy.wait()
-
-    return pl.pallas_call(
-        kernel,
-        out_shape=(
-            jax.ShapeDtypeStruct(tiles.shape, tiles.dtype),
-            jax.ShapeDtypeStruct((entries + parts,), jnp.int32),
-        ),
-        in_specs=[whole(pltpu.MemorySpace.HBM), whole(SMEM)],
-        out_specs=(whole(), whole(SMEM)),
-        scratch_shapes=[pltpu.SemaphoreType.DMA((snaps, CORES))],
-        compiler_params=params(44),
-        cost_estimate=cost(0, 2**20),
-        name="load_tiles",
-    )(tiles, live)
+
+    return pl.pallas_call(
+        kernel,
+        out_shape=jax.ShapeDtypeStruct((entries + parts + rows,), jnp.int32),
+        in_specs=[whole(SMEM)],
+        out_specs=whole(SMEM),
+        compiler_params=params(),
+        cost_estimate=cost(COVER_FLOPS, 2**20),
+        name="column_table",
+    )(live)
 
 
 def picked(table, tiles, x_block, snap, rel, step, lhs, rhs):
     snaps, rows, parts, slots, blk, _ = tiles.shape
     part = table[snaps * rows * parts * slots + step]
+    row = table[snaps * rows * parts * slots + parts + rel]
     for k in range(slots):
         col = table[((snap * rows + rel) * parts + step) * slots + k]
         block = x_block(pl.ds(pl.multiple_of(jnp.maximum(col, 0) * blk, blk), blk))
         rhs.append(jnp.where(col >= 0, block, jnp.zeros_like(block)))
-        lhs.append(tiles[snap, rel, part, k])
+        lhs.append(tiles[snap, row, part, k])
 
 
 def product(lhs, rhs):
@@ -153,28 +141,53 @@
     )(*operands)
 
 
-def spmm_last(table, tiles, x, snap, step, acc):
+def dense_tiles(table, tiles, step):
     snaps, rows, parts, slots, blk, _ = tiles.shape
+
+    def kernel(table, tiles, *outs):
+        entries = snaps * rows * parts * slots
+        part = table[entries + step]
+        for snap in range(snaps):
+            for rel in range(rows):
+                row = table[entries + parts + rel]
+                cols = [table[((snap * rows + rel) * parts + step) * slots + k] for k in range(slots)]
+                found = [tiles[snap, row, part, k] for k in range(slots)]
+                for c in range(rows):
+                    terms = [jnp.where(col == c, tile, jnp.zeros_like(tile)) for col, tile in zip(cols, found)]
+                    outs[snap][rel * blk : (rel + 1) * blk, c * blk : (c + 1) * blk] = functools.reduce(jnp.add, terms)
+
+    out = jax.ShapeDtypeStruct((rows * blk, rows * blk), BF16)
+    return pl.pallas_call(
+        kernel,
+        out_shape=(out,) * snaps,
+        in_specs=[whole(SMEM), whole()],
+        out_specs=(whole(),) * snaps,
+        compiler_params=params(),
+        cost_estimate=cost(0, 2**20),
+        name="dense_tiles",
+    )(table, tiles)
+
+
+def spmm_last(dense, x, snap, acc):
+    total_rows = dense.shape[0]
     feats = x.shape[-1]
-    half = rows // CORES
-
-    def kernel(table, tiles, x_ref, acc_in, *outs):
-        for rel in range(rows):
-            lhs, rhs = [], []
-            picked(table, tiles, lambda at: x_ref[at, :], snap, rel, step, lhs, rhs)
-            total = product(lhs, rhs) + acc_in[snap, rel]
-            outs[rel // half][(rel % half) * blk : (rel % half + 1) * blk, :] = total.astype(BF16)
-
-    part = jax.ShapeDtypeStruct((half * blk, feats), BF16)
+    half = total_rows // CORES
+
+    def kernel(dense, x, acc_in, keep, send):
+        total = jnp.dot(dense[...], x[...], preferred_element_type=F32) + acc_in[snap].reshape(total_rows, feats)
+        keep[...] = total[:half].astype(BF16)
+        send[...] = total[half:].astype(BF16)
+
+    part = jax.ShapeDtypeStruct((half, feats), BF16)
     return pl.pallas_call(
         kernel,
         out_shape=(part, part),
-        in_specs=[whole(SMEM)] + [whole()] * 3,
+        in_specs=[whole()] * 3,
         out_specs=(whole(), whole()),
         compiler_params=params(),
-        cost_estimate=cost(2 * rows * slots * blk * blk * feats * 4, 2**20),
+        cost_estimate=cost(2 * total_rows * dense.shape[1] * feats, 2**20),
         name="spmm_last",
-    )(table, tiles, x, acc)
+    )(dense, x, acc)
 
 
 def write_gates(axs, w_graph, w_input, out):
@@ -348,14 +361,16 @@
     back = [(b, a) for a, b in ahead]
 
     far = parts // 2
-    tiles, table = load_tiles(tile_values, tile_cols, tile_count, order)
+    tiles = tile_values
+    table = column_table(tile_values, tile_cols, tile_count, order)
     forward = lax.ppermute(features, "dom", ahead)
     reverse = lax.ppermute(features, "dom", back)
-    forward, tiles, table = lax.optimization_barrier((forward, tiles, table))
-    waiting = [([features, forward, reverse], [0, parts - 1, 1])]
+    acc = spmm(table, tiles, [features], [0], None)
+    dense = dense_tiles(table, tiles, far)
+    forward, acc, dense = lax.optimization_barrier((forward, acc, dense))
+    waiting = [([forward, reverse], [parts - 1, 1])]
     forward = [forward[s] for s in range(snaps)]
     reverse = [reverse[s] for s in range(snaps)]
-    acc = None
     beside = [w_graph, w_input, w_hidden, hidden_start]
     for hop in range(2, far):
         for turn in range(2):
@@ -379,7 +394,7 @@
     swap = [(t, t ^ 1) for t in range(sections)]
     keep_ax, other_ax = [], []
     for s in range(snaps):
-        keep, send = spmm_last(table, tiles, arriving[s], s, far, acc)
+        keep, send = spmm_last(dense[s], arriving[s], s, acc)
         keep_ax.append(keep)
         other_ax.append(lax.ppermute(send, "tm", swap))
     gx_own = gates(keep_ax, w_graph, w_input)

time: 44.5 us -> 43.9 us (0.987)
  Pallas kernels: 18 us -> 16 us
  local copies, waits for them, and re-layouts: 0.07 us -> 1.3 us
  starting transfers between devices: 14.8 us -> 15.3 us
    pallas_call x3 -> x4, Pallas kernels: 6.68 us -> 3.84 us  [the longest x1 2.14 us: column_table(): pl.pallas_call(kernel, out_shape=jax.ShapeDtypeStruct((entries + parts +...]
    unnamed x12 -> x14, local copies, waits for them, and re-layouts: 0.03 us -> 1.26 us
    pallas_call x3 -> x4, Pallas kernels: 4.22 us -> 4.92 us  [spmm(): pl.pallas_call(kernel, out_shape=jax.ShapeDtypeStruct((snaps, rows, blk,...]
    ppermute x4, starting transfers between devices: 1.59 us -> 2.28 us  [per_device(): reverse[s] = lax.ppermute(reverse[s], 'dom', back)]
    ppermute x4, waiting for transfers between devices: 1.95 us -> 2.57 us  [per_device(): reverse[s] = lax.ppermute(reverse[s], 'dom', back)]
    ppermute x1, waiting for transfers between devices: 0.77 us -> 0.2 us  [per_device(): forward = lax.ppermute(features, 'dom', ahead)]
    ppermute x4, waiting for transfers between devices: 0.74 us -> 0.17 us  [per_device(): forward[s] = lax.ppermute(forward[s], 'dom', ahead)]
    ppermute x1, starting transfers between devices: 1.29 us -> 1.77 us  [per_device(): lax.ppermute(forward[s], 'dom', ahead)]
  transfers between devices with their start and end apart: 18 -> 18, of which waited for: 9 -> 8; matrix products, arithmetic and copies ran while one was open for 2% -> 2% of each run, Pallas kernels for 34% -> 30%
where the time goes in v5:
time: 43.9 us; the launch traced here: 43.7 us
  Pallas kernels  16 us (36%)
  starting transfers between devices  15.3 us (35%)
  waiting for transfers between devices  9.97 us (23%)
  local copies, waits for them, and re-layouts  1.3 us (3%)
  other arithmetic  0.73 us (2%)
    ppermute x4, starting transfers between devices, per_device(): forward[s] = lax.ppermute(forward[s], 'dom', ahead)  6.39 us
    ppermute x2, waiting for transfers between devices, per_device(): states = [lax.ppermute(state, 'tm', onward) for state in states]  5.22 us
    pallas_call x4, Pallas kernels, spmm(): pl.pallas_call(kernel, out_shape=jax.ShapeDtypeStruct((snaps, rows, blk,...  4.92 us
    pallas_call x2, Pallas kernels, recurrence_first(): pl.pallas_call(kernel, out_shape=(jax.ShapeDtypeStruct((rows, hid), BF16)...  4.42 us
    ppermute x1, starting transfers between devices, per_device(): forward = lax.ppermute(features, 'dom', ahead)  3.02 us
    ppermute x4, waiting for transfers between devices, per_device(): reverse[s] = lax.ppermute(reverse[s], 'dom', back)  2.57 us
    ppermute x4, starting transfers between devices, per_device(): reverse[s] = lax.ppermute(reverse[s], 'dom', back)  2.28 us
    pallas_call x1, Pallas kernels, column_table(): pl.pallas_call(kernel, out_shape=jax.ShapeDtypeStruct((entries + parts +...  2.14 us
  transfers between devices with their start and end apart: 18, of which 8 were waited for; matrix products, arithmetic and copies ran while one was open for 2% of the time, Pallas kernels for 30%

profile of v5, /device:TPU:0, one launch (start us, length us, event | category | flops | bytes accessed | tf_op | source)
XLA Modules:
  0.0 43.7 jit_solution(12669787853484644701)
XLA Ops:
  0.0 3.0 %collective-permute-start = (bf16[2,512,128]{2,1,0:T(8,128)(2,1)}, bf16[2,512,128]{2,1,0:T(8,128)(2,1)S(1)}, u32[]{:S(2)}, u32[]{:S(2)}) collective-permute-start(bf16[2,512,128]{2,1,0:T(8,128)(2,1)} %refs_0_.1), channel_id=1, source_target_pairs={{0,2},{2,4},{4,6},{6,7},{7,5},{5,3},{3,1},{1,0},{8,10},{10,12},{12... | collective-permute-start | bytes 786440 | tf_op jit(solution)/shard_map/ppermute | solution.py:366
  3.0 0.7 %bitcast_select_fusion.live = s32[2,4,4,8]{3,2,1,0:T(4,128)S(1)} fusion(s32[2,4,8,4]{2,3,1,0:T(4,128)} %param.11, s32[2,4,8]{2,1,0:T(4,128)} %param.12), kind=kLoop, calls=%fused_computation.4 | loop fusion | flops 512 | bytes 2304 | tf_op jit(solution)/shard_map/jit(_where)/select_n | solution.py:67
  3.8 2.1 %column_table.1.table = s32[268]{0:T(512)S(1)} custom-call(s32[2,4,4,8]{3,2,1,0:T(4,128)S(1)} %bitcast_select_fusion.live), custom_call_target="tpu_custom_call" | custom-call | flops 3000000000 | bytes 1048576 | tf_op jit(solution)/shard_map/column_table/pallas_call | solution.py:88
  5.9 1.2 %copy-done = bf16[2,4,8,4,128,128]{5,4,3,2,1,0:T(8,128)(2,1)S(1)} copy-done((bf16[2,4,8,4,128,128]{5,4,3,2,1,0:T(8,128)(2,1)S(1)}, bf16[2,4,8,4,128,128]{5,4,3,2,1,0:T(8,128)(2,1)}, u32[]{:S(2)}) %copy-start) | copy-done | bytes 8388632
  7.1 1.1 %dense_tiles.1 = (bf16[512,512]{1,0:T(8,128)(2,1)S(1)}, bf16[512,512]{1,0:T(8,128)(2,1)S(1)}) custom-call(s32[268]{0:T(512)S(1)} %column_table.1.table, bf16[2,4,8,4,128,128]{5,4,3,2,1,0:T(8,128)(2,1)S(1)} %copy-done), custom_call_target="tpu_custom_call" | custom-call | bytes 1048576 | tf_op jit(solution)/shard_map/dense_tiles/pallas_call | solution.py:160
  8.3 1.0 %spmm.4.refs_2_ = f32[2,4,128,128]{3,2,1,0:T(8,128)S(1)} custom-call(s32[268]{0:T(512)S(1)} %column_table.1.table, bf16[2,4,8,4,128,128]{5,4,3,2,1,0:T(8,128)(2,1)S(1)} %copy-done, bf16[2,512,128]{2,1,0:T(8,128)(2,1)S(1)} %copy-done.4), custom_call_target="tpu_custom_call" | custom-call | flops 536870912 | bytes 1048576 | tf_op jit(solution)/shard_map/spmm/pallas_call | solution.py:133
  9.5 1.9 %collective-permute-start.1 = (bf16[512,128]{1,0:T(8,128)(2,1)S(1)}, bf16[512,128]{1,0:T(8,128)(2,1)S(1)}, u32[]{:S(2)}, u32[]{:S(2)}) collective-permute-start(bf16[512,128]{1,0:T(8,128)(2,1)S(1)} %get-tuple-element.68), channel_id=1, source_target_pairs={{0,2},{2,4},{4,6},{6,7},{7,5},{5,3},{3,1},{1,0},{8,10},{10,12},{12... | collective-permute-start | bytes 393224 | tf_op jit(solution)/shard_map/ppermute | solution.py:379
  11.7 1.8 %collective-permute-start.5 = (bf16[512,128]{1,0:T(8,128)(2,1)S(1)}, bf16[512,128]{1,0:T(8,128)(2,1)S(1)}, u32[]{:S(2)}, u32[]{:S(2)}) collective-permute-start(bf16[512,128]{1,0:T(8,128)(2,1)S(1)} %get-tuple-element.66), channel_id=1, source_target_pairs={{2,0},{4,2},{6,4},{7,6},{5,7},{3,5},{1,3},{0,1},{10,8},{12,10},{14... | collective-permute-start | bytes 393224 | tf_op jit(solution)/shard_map/ppermute | solution.py:381
  13.4 0.2 collective-permute-start.4
  13.7 1.3 %spmm.5.refs_4_ = f32[2,4,128,128]{3,2,1,0:T(8,128)S(1)} custom-call(s32[268]{0:T(512)S(1)} %column_table.1.table, bf16[2,4,8,4,128,128]{5,4,3,2,1,0:T(8,128)(2,1)S(1)} %copy-done, bf16[2,512,128]{2,1,0:T(8,128)(2,1)S(1)} %collective-permute-done.refs_0_, bf16[2,512,128]{2,1,0:T(8,128)(2,1)S(1)} %collective-permute-done.2.refs_1_, ...), custom_call_target="tpu_custom_call" | custom-call | flops 1073741824 | bytes 1048576 | tf_op jit(solution)/shard_map/spmm/pallas_call | solution.py:133
  15.2 2.5 %collective-permute-start.3 = (bf16[512,128]{1,0:T(8,128)(2,1)S(1)}, bf16[512,128]{1,0:T(8,128)(2,1)S(1)}, u32[]{:S(2)}, u32[]{:S(2)}) collective-permute-start(bf16[512,128]{1,0:T(8,128)(2,1)S(1)} %collective-permute-done.1.refs_0_), channel_id=1, source_target_pairs={{0,2},{2,4},{4,6},{6,7},{7,5},{5,3},{3,1},{1,0},{8,10},{10,12},{12... | collective-permute-start | bytes 393224 | tf_op jit(solution)/shard_map/ppermute | solution.py:379
  17.7 2.2 %collective-permute-done.5.refs_2_ = bf16[512,128]{1,0:T(8,128)(2,1)S(1)} collective-permute-done((bf16[512,128]{1,0:T(8,128)(2,1)S(1)}, bf16[512,128]{1,0:T(8,128)(2,1)S(1)}, u32[]{:S(2)}, u32[]{:S(2)}) %collective-permute-start.5) | collective-permute-done | bytes 131104 | tf_op jit(solution)/shard_map/ppermute | solution.py:381
  19.9 0.3 collective-permute-start.9
  20.1 1.8 %collective-permute-start.8 = (bf16[512,128]{1,0:T(8,128)(2,1)S(1)}, bf16[512,128]{1,0:T(8,128)(2,1)S(1)}, u32[]{:S(2)}, u32[]{:S(2)}) collective-permute-start(bf16[512,128]{1,0:T(8,128)(2,1)S(1)} %collective-permute-done.4.refs_1_), channel_id=1, source_target_pairs={{0,2},{2,4},{4,6},{6,7},{7,5},{5,3},{3,1},{1,0},{8,10},{10,12},{12... | collective-permute-start | bytes 393224 | tf_op jit(solution)/shard_map/ppermute | solution.py:379
  21.9 1.3 %spmm.6.refs_4_ = f32[2,4,128,128]{3,2,1,0:T(8,128)S(1)} custom-call(s32[268]{0:T(512)S(1)} %column_table.1.table, bf16[2,4,8,4,128,128]{5,4,3,2,1,0:T(8,128)(2,1)S(1)} %copy-done, bf16[512,128]{1,0:T(8,128)(2,1)S(1)} %collective-permute-done.1.refs_0_, bf16[512,128]{1,0:T(8,128)(2,1)S(1)} %collective-permute-done.4.refs_1_, ...), custom_call_target="tpu_custom_call" | custom-call | flops 1073741824 | bytes 1048576 | tf_op jit(solution)/shard_map/spmm/pallas_call | solution.py:133
  23.2 0.3 collective-permute-start.11
  23.5 1.8 %collective-permute-start.7 = (bf16[512,128]{1,0:T(8,128)(2,1)S(1)}, bf16[512,128]{1,0:T(8,128)(2,1)S(1)}, u32[]{:S(2)}, u32[]{:S(2)}) collective-permute-start(bf16[512,128]{1,0:T(8,128)(2,1)S(1)} %collective-permute-done.3.refs_0_), channel_id=1, source_target_pairs={{0,2},{2,4},{4,6},{6,7},{7,5},{5,3},{3,1},{1,0},{8,10},{10,12},{12... | collective-permute-start | bytes 393224 | tf_op jit(solution)/shard_map/ppermute | solution.py:388
  25.3 0.4 collective-permute-done.9.refs_2_
  25.7 1.3 %spmm.7.acc_in = f32[2,4,128,128]{3,2,1,0:T(8,128)S(1)} custom-call(s32[268]{0:T(512)S(1)} %column_table.1.table, bf16[2,4,8,4,128,128]{5,4,3,2,1,0:T(8,128)(2,1)S(1)} %copy-done, bf16[512,128]{1,0:T(8,128)(2,1)S(1)} %collective-permute-done.3.refs_0_, bf16[512,128]{1,0:T(8,128)(2,1)S(1)} %collective-permute-done.8.refs_1_, ...), custom_call_target="tpu_custom_call" | custom-call | flops 1073741824 | bytes 1048576 | tf_op jit(solution)/shard_map/spmm/pallas_call | solution.py:133
  27.0 1.2 %collective-permute-done.11.x = bf16[512,128]{1,0:T(8,128)(2,1)S(1)} collective-permute-done((bf16[512,128]{1,0:T(8,128)(2,1)S(1)}, bf16[512,128]{1,0:T(8,128)(2,1)S(1)}, u32[]{:S(2)}, u32[]{:S(2)}) %collective-permute-start.11) | collective-permute-done | bytes 131104 | tf_op jit(solution)/shard_map/ppermute | solution.py:388
  28.3 0.3 spmm_last.3
  28.6 0.3 spmm_last.2
  28.9 0.6 %collective-permute-start.12 = (bf16[256,128]{1,0:T(8,128)(2,1)S(1)}, bf16[256,128]{1,0:T(8,128)(2,1)S(1)}, u32[]{:S(2)}, u32[]{:S(2)}) collective-permute-start(bf16[256,128]{1,0:T(8,128)(2,1)S(1)} %get-tuple-element.51), channel_id=1, source_target_pairs={{0,8},{8,0},{16,24},{24,16},{1,9},{9,1},{17,25},{25,17},{2,10},{10... | collective-permute-start | bytes 196616 | tf_op jit(solution)/shard_map/ppermute | solution.py:399
  29.5 1.1 %gates.1.gx_own = f32[2,256,1536]{2,1,0:T(8,128)S(1)} custom-call(bf16[256,128]{1,0:T(8,128)(2,1)S(1)} %get-tuple-element.48.refs_0_, bf16[256,128]{1,0:T(8,128)(2,1)S(1)} %get-tuple-element.50.refs_1_, bf16[128,512]{1,0:T(8,128)(2,1)S(1)} %copy-done.5, bf16[512,1536]{1,0:T(8,128)(2,1)S(1)} %copy-done.1), custom_call_target="tpu_custom_call" | custom-call | flops 1610612736 | bytes 1048576 | tf_op jit(solution)/shard_map/gates/pallas_call | solution.py:210
  30.6 2.1 %recurrence_first.3 = (bf16[128,512]{1,0:T(8,128)(2,1)S(1)}, bf16[2,128,512]{2,1,0:T(8,128)(2,1)S(1)}, bf16[2,128,512]{2,1,0:T(8,128)(2,1)S(1)}, f32[2,128,1536]{2,1,0:T(8,128)S(1)}) custom-call(f32[512,512]{1,0:T(8,128)S(1)} %copy-done.3, f32[2,256,1536]{2,1,0:T(8,128)S(1)} %gates.1.gx_own, bf16[128,512]{1,0:T(8,128)(2,1)S(1)} %copy-done.5, ...), custom_call_target="tpu_custom_call" | custom-call | flops 3221225472 | bytes 1048576 | tf_op jit(solution)/shard_map/recurrence_first/pallas_call | solution.py:270
  32.9 2.3 %recurrence_first.2 = (bf16[128,512]{1,0:T(8,128)(2,1)S(1)}, bf16[2,128,512]{2,1,0:T(8,128)(2,1)S(1)}, bf16[2,128,512]{2,1,0:T(8,128)(2,1)S(1)}, f32[2,128,1536]{2,1,0:T(8,128)S(1)}) custom-call(f32[512,512]{1,0:T(8,128)S(1)} %copy-done.3, f32[2,256,1536]{2,1,0:T(8,128)S(1)} %gates.1.gx_own, bf16[128,512]{1,0:T(8,128)(2,1)S(1)} %copy-done.5, ...), custom_call_target="tpu_custom_call" | custom-call | flops 3221225472 | bytes 1048576 | tf_op jit(solution)/shard_map/recurrence_first/pallas_call | solution.py:270
  35.2 0.6 %collective-permute-start.14 = (bf16[128,512]{1,0:T(8,128)(2,1)S(1)}, bf16[128,512]{1,0:T(8,128)(2,1)S(1)}, u32[]{:S(2)}, u32[]{:S(2)}) collective-permute-start(bf16[128,512]{1,0:T(8,128)(2,1)S(1)} %get-tuple-element.53), channel_id=1, source_target_pairs={{0,16},{8,24},{16,0},{24,8},{1,17},{9,25},{17,1},{25,9},{2,18},{10... | collective-permute-start | bytes 393224 | tf_op jit(solution)/shard_map/ppermute | solution.py:413
  35.8 2.9 %collective-permute-done.16.state_in = bf16[128,512]{1,0:T(8,128)(2,1)S(1)} collective-permute-done((bf16[128,512]{1,0:T(8,128)(2,1)S(1)}, bf16[128,512]{1,0:T(8,128)(2,1)S(1)}, u32[]{:S(2)}, u32[]{:S(2)}) %collective-permute-start.16) | collective-permute-done | bytes 131104 | tf_op jit(solution)/shard_map/ppermute | solution.py:413
  38.8 2.3 %collective-permute-done.14.state_in = bf16[128,512]{1,0:T(8,128)(2,1)S(1)} collective-permute-done((bf16[128,512]{1,0:T(8,128)(2,1)S(1)}, bf16[128,512]{1,0:T(8,128)(2,1)S(1)}, u32[]{:S(2)}, u32[]{:S(2)}) %collective-permute-start.14) | collective-permute-done | bytes 131104 | tf_op jit(solution)/shard_map/ppermute | solution.py:413
  41.3 0.9 %write_out.2.refs_1_ = bf16[2,512,512]{2,1,0:T(8,128)(2,1)} custom-call(bf16[2,128,512]{2,1,0:T(8,128)(2,1)S(1)} %get-tuple-element.62.refs_0_, bf16[2,128,512]{2,1,0:T(8,128)(2,1)S(1)} %get-tuple-element.63.refs_1_, bf16[2,128,512]{2,1,0:T(8,128)(2,1)S(1)} %collective-permute-done.17.refs_2_), custom_call_target="tpu_custom_call" | custom-call | bytes 1048576 | tf_op jit(solution)/shard_map/write_out/pallas_call | solution.py:339
  42.2 0.6 %collective-permute-done.15.refs_0_ = bf16[2,128,512]{2,1,0:T(8,128)(2,1)S(1)} collective-permute-done((bf16[2,128,512]{2,1,0:T(8,128)(2,1)S(1)}, bf16[2,128,512]{2,1,0:T(8,128)(2,1)S(1)}, u32[]{:S(2)}, u32[]{:S(2)}) %collective-permute-start.15) | collective-permute-done | bytes 262176 | tf_op jit(solution)/shard_map/ppermute | solution.py:422
  42.8 0.7 %write_out.3 = bf16[2,512,512]{2,1,0:T(8,128)(2,1)} custom-call(bf16[2,128,512]{2,1,0:T(8,128)(2,1)S(1)} %collective-permute-done.15.refs_0_, bf16[2,512,512]{2,1,0:T(8,128)(2,1)} %write_out.2.refs_1_), custom_call_target="tpu_custom_call", output_to_operand_aliasing={{}: (1, {})} | custom-call | bytes 1048576 | tf_op jit(solution)/shard_map/write_out/pallas_call | solution.py:339
  (36 shorter events, 1.1 us)
Async XLA Ops:
  0.0 9.5 %collective-permute-start = (bf16[2,512,128]{2,1,0:T(8,128)(2,1)}, bf16[2,512,128]{2,1,0:T(8,128)(2,1)S(1)}, u32[]{:S(2)}, u32[]{:S(2)}) collective-permute-start(bf16[2,512,128]{2,1,0:T(8,128)(2,1)} %refs_0_.1), channel_id=1, source_target_pairs={{0,2},{2,4},{4,6},{6,7},{7,5},{5,3},{3,1},{1,0},{8,10},{10,12},{12... | collective-permute-start | bytes 786440 | tf_op jit(solution)/shard_map/ppermute | solution.py:366
  3.0 8.4 %collective-permute-start.2 = (bf16[2,512,128]{2,1,0:T(8,128)(2,1)}, bf16[2,512,128]{2,1,0:T(8,128)(2,1)S(1)}, u32[]{:S(2)}, u32[]{:S(2)}) collective-permute-start(bf16[2,512,128]{2,1,0:T(8,128)(2,1)} %refs_0_.1), channel_id=1, source_target_pairs={{2,0},{4,2},{6,4},{7,6},{5,7},{3,5},{1,3},{0,1},{10,8},{12,10},{14... | collective-permute-start | bytes 786440 | tf_op jit(solution)/shard_map/ppermute | solution.py:367
  3.8 3.4 %copy-start = (bf16[2,4,8,4,128,128]{5,4,3,2,1,0:T(8,128)(2,1)S(1)}, bf16[2,4,8,4,128,128]{5,4,3,2,1,0:T(8,128)(2,1)}, u32[]{:S(2)}) copy-start(bf16[2,4,8,4,128,128]{5,4,3,2,1,0:T(8,128)(2,1)} %tiles.9) | copy-start | bytes 25165828
  7.1 1.1 %copy-start.4 = (bf16[2,512,128]{2,1,0:T(8,128)(2,1)S(1)}, bf16[2,512,128]{2,1,0:T(8,128)(2,1)}, u32[]{:S(2)}) copy-start(bf16[2,512,128]{2,1,0:T(8,128)(2,1)} %refs_0_.1) | copy-start | bytes 786436
  9.5 5.7 %collective-permute-start.1 = (bf16[512,128]{1,0:T(8,128)(2,1)S(1)}, bf16[512,128]{1,0:T(8,128)(2,1)S(1)}, u32[]{:S(2)}, u32[]{:S(2)}) collective-permute-start(bf16[512,128]{1,0:T(8,128)(2,1)S(1)} %get-tuple-element.68), channel_id=1, source_target_pairs={{0,2},{2,4},{4,6},{6,7},{7,5},{5,3},{3,1},{1,0},{8,10},{10,12},{12... | collective-permute-start | bytes 393224 | tf_op jit(solution)/shard_map/ppermute | solution.py:379
  11.4 6.3 %collective-permute-start.6 = (bf16[512,128]{1,0:T(8,128)(2,1)S(1)}, bf16[512,128]{1,0:T(8,128)(2,1)S(1)}, u32[]{:S(2)}, u32[]{:S(2)}) collective-permute-start(bf16[512,128]{1,0:T(8,128)(2,1)S(1)} %get-tuple-element.65), channel_id=1, source_target_pairs={{2,0},{4,2},{6,4},{7,6},{5,7},{3,5},{1,3},{0,1},{10,8},{12,10},{14... | collective-permute-start | bytes 393224 | tf_op jit(solution)/shard_map/ppermute | solution.py:381
  11.7 8.2 %collective-permute-start.5 = (bf16[512,128]{1,0:T(8,128)(2,1)S(1)}, bf16[512,128]{1,0:T(8,128)(2,1)S(1)}, u32[]{:S(2)}, u32[]{:S(2)}) collective-permute-start(bf16[512,128]{1,0:T(8,128)(2,1)S(1)} %get-tuple-element.66), channel_id=1, source_target_pairs={{2,0},{4,2},{6,4},{7,6},{5,7},{3,5},{1,3},{0,1},{10,8},{12,10},{14... | collective-permute-start | bytes 393224 | tf_op jit(solution)/shard_map/ppermute | solution.py:381
  13.4 6.7 %collective-permute-start.4 = (bf16[512,128]{1,0:T(8,128)(2,1)S(1)}, bf16[512,128]{1,0:T(8,128)(2,1)S(1)}, u32[]{:S(2)}, u32[]{:S(2)}) collective-permute-start(bf16[512,128]{1,0:T(8,128)(2,1)S(1)} %get-tuple-element.67), channel_id=1, source_target_pairs={{0,2},{2,4},{4,6},{6,7},{7,5},{5,3},{3,1},{1,0},{8,10},{10,12},{12... | collective-permute-start | bytes 393224 | tf_op jit(solution)/shard_map/ppermute | solution.py:379
  15.0 10.7 %copy-start.1 = (bf16[512,1536]{1,0:T(8,128)(2,1)S(1)}, bf16[512,1536]{1,0:T(8,128)(2,1)}, u32[]{:S(2)}) copy-start(bf16[512,1536]{1,0:T(8,128)(2,1)} %w_input.3) | copy-start | bytes 4718596
  15.0 10.7 %copy-start.2 = (bf16[512,1536]{1,0:T(8,128)(2,1)S(1)}, bf16[512,1536]{1,0:T(8,128)(2,1)}, u32[]{:S(2)}) copy-start(bf16[512,1536]{1,0:T(8,128)(2,1)} %w_hidden.7) | copy-start | bytes 4718596
  15.0 10.7 %copy-start.3 = (f32[512,512]{1,0:T(8,128)S(1)}, f32[512,512]{1,0:T(8,128)}, u32[]{:S(2)}) copy-start(f32[512,512]{1,0:T(8,128)} %hidden_start.3) | copy-start | bytes 3145732
  15.0 10.7 %copy-start.5 = (bf16[128,512]{1,0:T(8,128)(2,1)S(1)}, bf16[128,512]{1,0:T(8,128)(2,1)}, u32[]{:S(2)}) copy-start(bf16[128,512]{1,0:T(8,128)(2,1)} %w_graph.3) | copy-start | bytes 393220
  15.2 8.0 %collective-permute-start.3 = (bf16[512,128]{1,0:T(8,128)(2,1)S(1)}, bf16[512,128]{1,0:T(8,128)(2,1)S(1)}, u32[]{:S(2)}, u32[]{:S(2)}) collective-permute-start(bf16[512,128]{1,0:T(8,128)(2,1)S(1)} %collective-permute-done.1.refs_0_), channel_id=1, source_target_pairs={{0,2},{2,4},{4,6},{6,7},{7,5},{5,3},{3,1},{1,0},{8,10},{10,12},{12... | collective-permute-start | bytes 393224 | tf_op jit(solution)/shard_map/ppermute | solution.py:379
  17.7 5.5 %collective-permute-start.10 = (bf16[512,128]{1,0:T(8,128)(2,1)S(1)}, bf16[512,128]{1,0:T(8,128)(2,1)S(1)}, u32[]{:S(2)}, u32[]{:S(2)}) collective-permute-start(bf16[512,128]{1,0:T(8,128)(2,1)S(1)} %collective-permute-done.6.refs_3_), channel_id=1, source_target_pairs={{2,0},{4,2},{6,4},{7,6},{5,7},{3,5},{1,3},{0,1},{10,8},{12,10},{14... | collective-permute-start | bytes 393224 | tf_op jit(solution)/shard_map/ppermute | solution.py:381
  19.9 5.8 %collective-permute-start.9 = (bf16[512,128]{1,0:T(8,128)(2,1)S(1)}, bf16[512,128]{1,0:T(8,128)(2,1)S(1)}, u32[]{:S(2)}, u32[]{:S(2)}) collective-permute-start(bf16[512,128]{1,0:T(8,128)(2,1)S(1)} %collective-permute-done.5.refs_2_), channel_id=1, source_target_pairs={{2,0},{4,2},{6,4},{7,6},{5,7},{3,5},{1,3},{0,1},{10,8},{12,10},{14... | collective-permute-start | bytes 393224 | tf_op jit(solution)/shard_map/ppermute | solution.py:381
  20.1 5.6 %collective-permute-start.8 = (bf16[512,128]{1,0:T(8,128)(2,1)S(1)}, bf16[512,128]{1,0:T(8,128)(2,1)S(1)}, u32[]{:S(2)}, u32[]{:S(2)}) collective-permute-start(bf16[512,128]{1,0:T(8,128)(2,1)S(1)} %collective-permute-done.4.refs_1_), channel_id=1, source_target_pairs={{0,2},{2,4},{4,6},{6,7},{7,5},{5,3},{3,1},{1,0},{8,10},{10,12},{12... | collective-permute-start | bytes 393224 | tf_op jit(solution)/shard_map/ppermute | solution.py:379
  23.2 5.0 %collective-permute-start.11 = (bf16[512,128]{1,0:T(8,128)(2,1)S(1)}, bf16[512,128]{1,0:T(8,128)(2,1)S(1)}, u32[]{:S(2)}, u32[]{:S(2)}) collective-permute-start(bf16[512,128]{1,0:T(8,128)(2,1)S(1)} %collective-permute-done.10.refs_3_), channel_id=1, source_target_pairs={{2,0},{4,2},{6,4},{7,6},{5,7},{3,5},{1,3},{0,1},{10,8},{12,10},{14... | collective-permute-start | bytes 393224 | tf_op jit(solution)/shard_map/ppermute | solution.py:388
  23.5 5.1 %collective-permute-start.7 = (bf16[512,128]{1,0:T(8,128)(2,1)S(1)}, bf16[512,128]{1,0:T(8,128)(2,1)S(1)}, u32[]{:S(2)}, u32[]{:S(2)}) collective-permute-start(bf16[512,128]{1,0:T(8,128)(2,1)S(1)} %collective-permute-done.3.refs_0_), channel_id=1, source_target_pairs={{0,2},{2,4},{4,6},{6,7},{7,5},{5,3},{3,1},{1,0},{8,10},{10,12},{12... | collective-permute-start | bytes 393224 | tf_op jit(solution)/shard_map/ppermute | solution.py:388
  28.6 2.1 %collective-permute-start.13 = (bf16[256,128]{1,0:T(8,128)(2,1)S(1)}, bf16[256,128]{1,0:T(8,128)(2,1)S(1)}, u32[]{:S(2)}, u32[]{:S(2)}) collective-permute-start(bf16[256,128]{1,0:T(8,128)(2,1)S(1)} %get-tuple-element.52), channel_id=1, source_target_pairs={{0,8},{8,0},{16,24},{24,16},{1,9},{9,1},{17,25},{25,17},{2,10},{10... | collective-permute-start | bytes 196616 | tf_op jit(solution)/shard_map/ppermute | solution.py:399
  28.9 1.7 %collective-permute-start.12 = (bf16[256,128]{1,0:T(8,128)(2,1)S(1)}, bf16[256,128]{1,0:T(8,128)(2,1)S(1)}, u32[]{:S(2)}, u32[]{:S(2)}) collective-permute-start(bf16[256,128]{1,0:T(8,128)(2,1)S(1)} %get-tuple-element.51), channel_id=1, source_target_pairs={{0,8},{8,0},{16,24},{24,16},{1,9},{9,1},{17,25},{25,17},{2,10},{10... | collective-permute-start | bytes 196616 | tf_op jit(solution)/shard_map/ppermute | solution.py:399
  29.5 1.1 %copy-start.6 = (f32[512]{0:T(512)S(1)}, f32[512]{0:T(512)}, u32[]{:S(2)}) copy-start(f32[512]{0:T(512)} %param.17) | copy-start | bytes 6148
  32.8 5.9 %collective-permute-start.16 = (bf16[128,512]{1,0:T(8,128)(2,1)S(1)}, bf16[128,512]{1,0:T(8,128)(2,1)S(1)}, u32[]{:S(2)}, u32[]{:S(2)}) collective-permute-start(bf16[128,512]{1,0:T(8,128)(2,1)S(1)} %get-tuple-element.58), channel_id=1, source_target_pairs={{0,16},{8,24},{16,0},{24,8},{1,17},{9,25},{17,1},{25,9},{2,18},{10... | collective-permute-start | bytes 393224 | tf_op jit(solution)/shard_map/ppermute | solution.py:413
  35.2 5.9 %collective-permute-start.14 = (bf16[128,512]{1,0:T(8,128)(2,1)S(1)}, bf16[128,512]{1,0:T(8,128)(2,1)S(1)}, u32[]{:S(2)}, u32[]{:S(2)}) collective-permute-start(bf16[128,512]{1,0:T(8,128)(2,1)S(1)} %get-tuple-element.53), channel_id=1, source_target_pairs={{0,16},{8,24},{16,0},{24,8},{1,17},{9,25},{17,1},{25,9},{2,18},{10... | collective-permute-start | bytes 393224 | tf_op jit(solution)/shard_map/ppermute | solution.py:413
  38.7 2.5 %collective-permute-start.17 = (bf16[2,128,512]{2,1,0:T(8,128)(2,1)S(1)}, bf16[2,128,512]{2,1,0:T(8,128)(2,1)S(1)}, u32[]{:S(2)}, u32[]{:S(2)}) collective-permute-start(bf16[2,128,512]{2,1,0:T(8,128)(2,1)S(1)} %get-tuple-element.64), channel_id=1, source_target_pairs={{0,8},{8,0},{16,24},{24,16},{1,9},{9,1},{17,25},{25,17},{2,10},{10... | collective-permute-start | bytes 786440 | tf_op jit(solution)/shard_map/ppermute | solution.py:422
  41.2 1.6 %collective-permute-start.15 = (bf16[2,128,512]{2,1,0:T(8,128)(2,1)S(1)}, bf16[2,128,512]{2,1,0:T(8,128)(2,1)S(1)}, u32[]{:S(2)}, u32[]{:S(2)}) collective-permute-start(bf16[2,128,512]{2,1,0:T(8,128)(2,1)S(1)} %get-tuple-element.57), channel_id=1, source_target_pairs={{0,8},{8,0},{16,24},{24,16},{1,9},{9,1},{17,25},{25,17},{2,10},{10... | collective-permute-start | bytes 786440 | tf_op jit(solution)/shard_map/ppermute | solution.py:422

commit v6 on v5

--- a/solution.py
+++ b/solution.py
@@ -168,54 +168,58 @@
     )(table, tiles)
 
 
-def spmm_last(dense, x, snap, acc):
-    total_rows = dense.shape[0]
-    feats = x.shape[-1]
+def spmm_last(dense, xs, acc):
+    snaps = len(dense)
+    total_rows = dense[0].shape[0]
+    feats = xs[0].shape[-1]
     half = total_rows // CORES
 
-    def kernel(dense, x, acc_in, keep, send):
-        total = jnp.dot(dense[...], x[...], preferred_element_type=F32) + acc_in[snap].reshape(total_rows, feats)
-        keep[...] = total[:half].astype(BF16)
-        send[...] = total[half:].astype(BF16)
-
-    part = jax.ShapeDtypeStruct((half, feats), BF16)
+    def kernel(*refs):
+        mats, x_refs, (acc_in, keep, send) = refs[:snaps], refs[snaps : 2 * snaps], refs[2 * snaps :]
+        for snap in range(snaps):
+            total = jnp.dot(mats[snap][...], x_refs[snap][...], preferred_element_type=F32)
+            total = total + acc_in[snap].reshape(total_rows, feats)
+            keep[snap] = total[:half].astype(BF16)
+            send[snap] = total[half:].astype(BF16)
+
+    part = jax.ShapeDtypeStruct((snaps, half, feats), BF16)
     return pl.pallas_call(
         kernel,
         out_shape=(part, part),
-        in_specs=[whole()] * 3,
+        in_specs=[whole()] * (2 * snaps + 1),
         out_specs=(whole(), whole()),
         compiler_params=params(),
-        cost_estimate=cost(2 * total_rows * dense.shape[1] * feats, 2**20),
+        cost_estimate=cost(2 * snaps * total_rows * dense[0].shape[1] * feats, 2**20),
         name="spmm_last",
-    )(dense, x, acc)
-
-
-def write_gates(axs, w_graph, w_input, out):
-    snaps, rows = len(axs), axs[0].shape[0]
+    )(*dense, *xs, acc)
+
+
+def write_gates(ax, w_graph, w_input, out):
+    snaps, rows, feats = ax.shape
     hid, width = w_input.shape
-    graph = jnp.dot(jnp.concatenate(axs, axis=0), w_graph[...], preferred_element_type=F32)
+    graph = jnp.dot(ax.reshape(snaps * rows, feats), w_graph[...], preferred_element_type=F32)
     graph = jnp.maximum(graph, 0.0).astype(BF16)
     for j in range(0, width, hid):
         part = jnp.dot(graph, w_input[:, j : j + hid], preferred_element_type=F32)
         out[:, :, j : j + hid] = part.reshape(snaps, rows, hid)
 
 
-def gates(axs, w_graph, w_input):
-    snaps, rows = len(axs), axs[0].shape[0]
+def gates(ax, w_graph, w_input):
+    snaps, rows, _ = ax.shape
     hid, width = w_input.shape
 
-    def kernel(*refs):
-        write_gates([ref[...] for ref in refs[:snaps]], *refs[snaps:])
+    def kernel(ax, *refs):
+        write_gates(ax[...], *refs)
 
     return pl.pallas_call(
         kernel,
         out_shape=jax.ShapeDtypeStruct((snaps, rows, width), F32),
-        in_specs=[whole()] * (snaps + 2),
+        in_specs=[whole()] * 3,
         out_specs=whole(),
         compiler_params=params(),
         cost_estimate=cost(2 * snaps * rows * hid * width * 2, 2**20),
         name="gates",
-    )(*axs, w_graph, w_input)
+    )(ax, w_graph, w_input)
 
 
 def run_steps(state, given_first, given_second, outs_first, outs_second, w_hidden, bias, state_out):
@@ -243,16 +247,15 @@
         state_out[...] = state.astype(BF16)
 
 
-def recurrence_first(hidden_start, gx_own, axs_other, w_graph, w_input, w_hidden, bias, chunk):
+def recurrence_first(hidden_start, gx_own, ax_other, w_graph, w_input, w_hidden, bias, chunk):
     snaps, mine, width = gx_own.shape
     feats, hid = w_graph.shape
     rows = mine // CHUNKS
 
-    def kernel(hidden_start, gx_own, w_graph, w_input, w_hidden, bias, *refs):
-        axs, (state_out, keep, send, gx_other) = refs[:snaps], refs[snaps:]
+    def kernel(hidden_start, gx_own, ax_other, w_graph, w_input, w_hidden, bias, state_out, keep, send, gx_other):
         core, place = where_am_i()
         at = slice(chunk * rows, (chunk + 1) * rows)
-        write_gates([ref[at, :] for ref in axs], w_graph, w_input, gx_other)
+        write_gates(ax_other[:, at, :], w_graph, w_input, gx_other)
         own = lambda s, columns: gx_own[s, at, columns]
         other = lambda s, columns: gx_other[s, :, columns]
 
@@ -275,12 +278,12 @@
             part,
             jax.ShapeDtypeStruct((snaps, rows, width), F32),
         ),
-        in_specs=[whole()] * (6 + snaps),
+        in_specs=[whole()] * 7,
         out_specs=(whole(),) * 4,
         compiler_params=params(),
         cost_estimate=cost(2 * CORES * snaps * rows * hid * 3 * hid * 4, 2**20),
         name="recurrence_first",
-    )(hidden_start, gx_own, w_graph, w_input, w_hidden, bias, *axs_other)
+    )(hidden_start, gx_own, ax_other, w_graph, w_input, w_hidden, bias)
 
 
 def recurrence_later(state, gx_own, gx_other, w_hidden, bias, before, phase, chunk, last):
@@ -392,11 +395,8 @@
         xs, steps = waiting.pop(0)
         acc = spmm(table, tiles, xs, steps, acc, [] if waiting else beside)
     swap = [(t, t ^ 1) for t in range(sections)]
-    keep_ax, other_ax = [], []
-    for s in range(snaps):
-        keep, send = spmm_last(dense[s], arriving[s], s, acc)
-        keep_ax.append(keep)
-        other_ax.append(lax.ppermute(send, "tm", swap))
+    keep_ax, send_ax = spmm_last(dense, arriving, acc)
+    other_ax = lax.ppermute(send_ax, "tm", swap)
     gx_own = gates(keep_ax, w_graph, w_input)
 
     bias = update_bias.reshape(1, -1)

time: 43.9 us -> 43.9 us (level)
  waiting for transfers between devices: 9.97 us -> 10.6 us
  starting transfers between devices: 15.3 us -> 14.7 us
    ppermute x2 -> x1, starting transfers between devices: 0.63 us -> 0.07 us  [per_device(): other_ax = lax.ppermute(send_ax, 'tm', swap)]
  transfers between devices with their start and end apart: 18 -> 17, of which waited for: 8 -> 10; matrix products, arithmetic and copies ran while one was open for 2% -> 2% of each run, Pallas kernels for 30% -> 29%
where the time goes in v6:
time: 43.9 us; the launch traced here: 43.6 us
  Pallas kernels  15.9 us (36%)
  starting transfers between devices  14.7 us (33%)
  waiting for transfers between devices  10.6 us (24%)
  local copies, waits for them, and re-layouts  1.3 us (3%)
  other arithmetic  0.73 us (2%)
    ppermute x4, starting transfers between devices, per_device(): forward[s] = lax.ppermute(forward[s], 'dom', ahead)  6.39 us
    ppermute x2, waiting for transfers between devices, per_device(): states = [lax.ppermute(state, 'tm', onward) for state in states]  5.41 us
    pallas_call x4, Pallas kernels, spmm(): pl.pallas_call(kernel, out_shape=jax.ShapeDtypeStruct((snaps, rows, blk,...  4.94 us
    pallas_call x2, Pallas kernels, recurrence_first(): pl.pallas_call(kernel, out_shape=(jax.ShapeDtypeStruct((rows, hid), BF16)...  4.43 us
    ppermute x1, starting transfers between devices, per_device(): forward = lax.ppermute(features, 'dom', ahead)  3.02 us
    ppermute x4, waiting for transfers between devices, per_device(): reverse[s] = lax.ppermute(reverse[s], 'dom', back)  2.57 us
    ppermute x4, starting transfers between devices, per_device(): reverse[s] = lax.ppermute(reverse[s], 'dom', back)  2.28 us
    pallas_call x1, Pallas kernels, column_table(): pl.pallas_call(kernel, out_shape=jax.ShapeDtypeStruct((entries + parts +...  2.14 us
  transfers between devices with their start and end apart: 17, of which 10 were waited for; matrix products, arithmetic and copies ran while one was open for 2% of the time, Pallas kernels for 29%

profile of v6, /device:TPU:0, one launch (start us, length us, event | category | flops | bytes accessed | tf_op | source)
XLA Modules:
  0.0 43.6 jit_solution(15140150723226004901)
XLA Ops:
  0.0 3.0 %collective-permute-start = (bf16[2,512,128]{2,1,0:T(8,128)(2,1)}, bf16[2,512,128]{2,1,0:T(8,128)(2,1)S(1)}, u32[]{:S(2)}, u32[]{:S(2)}) collective-permute-start(bf16[2,512,128]{2,1,0:T(8,128)(2,1)} %refs_0_.2), channel_id=1, source_target_pairs={{0,2},{2,4},{4,6},{6,7},{7,5},{5,3},{3,1},{1,0},{8,10},{10,12},{12... | collective-permute-start | bytes 786440 | tf_op jit(solution)/shard_map/ppermute | solution.py:369
  3.0 0.7 %bitcast_select_fusion.live = s32[2,4,4,8]{3,2,1,0:T(4,128)S(1)} fusion(s32[2,4,8,4]{2,3,1,0:T(4,128)} %param.11, s32[2,4,8]{2,1,0:T(4,128)} %param.12), kind=kLoop, calls=%fused_computation.4 | loop fusion | flops 512 | bytes 2304 | tf_op jit(solution)/shard_map/jit(_where)/select_n | solution.py:67
  3.8 2.1 %column_table.1.table = s32[268]{0:T(512)S(1)} custom-call(s32[2,4,4,8]{3,2,1,0:T(4,128)S(1)} %bitcast_select_fusion.live), custom_call_target="tpu_custom_call" | custom-call | flops 3000000000 | bytes 1048576 | tf_op jit(solution)/shard_map/column_table/pallas_call | solution.py:88
  5.9 1.2 %copy-done = bf16[2,4,8,4,128,128]{5,4,3,2,1,0:T(8,128)(2,1)S(1)} copy-done((bf16[2,4,8,4,128,128]{5,4,3,2,1,0:T(8,128)(2,1)S(1)}, bf16[2,4,8,4,128,128]{5,4,3,2,1,0:T(8,128)(2,1)}, u32[]{:S(2)}) %copy-start) | copy-done | bytes 8388632
  7.1 1.1 %dense_tiles.1 = (bf16[512,512]{1,0:T(8,128)(2,1)S(1)}, bf16[512,512]{1,0:T(8,128)(2,1)S(1)}) custom-call(s32[268]{0:T(512)S(1)} %column_table.1.table, bf16[2,4,8,4,128,128]{5,4,3,2,1,0:T(8,128)(2,1)S(1)} %copy-done), custom_call_target="tpu_custom_call" | custom-call | bytes 1048576 | tf_op jit(solution)/shard_map/dense_tiles/pallas_call | solution.py:160
  8.3 1.0 %spmm.4.refs_2_ = f32[2,4,128,128]{3,2,1,0:T(8,128)S(1)} custom-call(s32[268]{0:T(512)S(1)} %column_table.1.table, bf16[2,4,8,4,128,128]{5,4,3,2,1,0:T(8,128)(2,1)S(1)} %copy-done, bf16[2,512,128]{2,1,0:T(8,128)(2,1)S(1)} %copy-done.4), custom_call_target="tpu_custom_call" | custom-call | flops 536870912 | bytes 1048576 | tf_op jit(solution)/shard_map/spmm/pallas_call | solution.py:133
  9.5 1.9 %collective-permute-start.1 = (bf16[512,128]{1,0:T(8,128)(2,1)S(1)}, bf16[512,128]{1,0:T(8,128)(2,1)S(1)}, u32[]{:S(2)}, u32[]{:S(2)}) collective-permute-start(bf16[512,128]{1,0:T(8,128)(2,1)S(1)} %get-tuple-element.64), channel_id=1, source_target_pairs={{0,2},{2,4},{4,6},{6,7},{7,5},{5,3},{3,1},{1,0},{8,10},{10,12},{12... | collective-permute-start | bytes 393224 | tf_op jit(solution)/shard_map/ppermute | solution.py:382
  11.7 1.8 %collective-permute-start.5 = (bf16[512,128]{1,0:T(8,128)(2,1)S(1)}, bf16[512,128]{1,0:T(8,128)(2,1)S(1)}, u32[]{:S(2)}, u32[]{:S(2)}) collective-permute-start(bf16[512,128]{1,0:T(8,128)(2,1)S(1)} %get-tuple-element.62), channel_id=1, source_target_pairs={{2,0},{4,2},{6,4},{7,6},{5,7},{3,5},{1,3},{0,1},{10,8},{12,10},{14... | collective-permute-start | bytes 393224 | tf_op jit(solution)/shard_map/ppermute | solution.py:384
  13.4 0.2 collective-permute-start.4
  13.7 1.3 %spmm.5.refs_4_ = f32[2,4,128,128]{3,2,1,0:T(8,128)S(1)} custom-call(s32[268]{0:T(512)S(1)} %column_table.1.table, bf16[2,4,8,4,128,128]{5,4,3,2,1,0:T(8,128)(2,1)S(1)} %copy-done, bf16[2,512,128]{2,1,0:T(8,128)(2,1)S(1)} %collective-permute-done.refs_0_, bf16[2,512,128]{2,1,0:T(8,128)(2,1)S(1)} %collective-permute-done.2.refs_1_, ...), custom_call_target="tpu_custom_call" | custom-call | flops 1073741824 | bytes 1048576 | tf_op jit(solution)/shard_map/spmm/pallas_call | solution.py:133
  15.2 2.5 %collective-permute-start.3 = (bf16[512,128]{1,0:T(8,128)(2,1)S(1)}, bf16[512,128]{1,0:T(8,128)(2,1)S(1)}, u32[]{:S(2)}, u32[]{:S(2)}) collective-permute-start(bf16[512,128]{1,0:T(8,128)(2,1)S(1)} %collective-permute-done.1.refs_0_), channel_id=1, source_target_pairs={{0,2},{2,4},{4,6},{6,7},{7,5},{5,3},{3,1},{1,0},{8,10},{10,12},{12... | collective-permute-start | bytes 393224 | tf_op jit(solution)/shard_map/ppermute | solution.py:382
  17.7 2.2 %collective-permute-done.5.refs_2_ = bf16[512,128]{1,0:T(8,128)(2,1)S(1)} collective-permute-done((bf16[512,128]{1,0:T(8,128)(2,1)S(1)}, bf16[512,128]{1,0:T(8,128)(2,1)S(1)}, u32[]{:S(2)}, u32[]{:S(2)}) %collective-permute-start.5) | collective-permute-done | bytes 131104 | tf_op jit(solution)/shard_map/ppermute | solution.py:384
  19.9 0.3 collective-permute-start.11
  20.1 1.8 %collective-permute-start.10 = (bf16[512,128]{1,0:T(8,128)(2,1)S(1)}, bf16[512,128]{1,0:T(8,128)(2,1)S(1)}, u32[]{:S(2)}, u32[]{:S(2)}) collective-permute-start(bf16[512,128]{1,0:T(8,128)(2,1)S(1)} %collective-permute-done.4.refs_1_), channel_id=1, source_target_pairs={{0,2},{2,4},{4,6},{6,7},{7,5},{5,3},{3,1},{1,0},{8,10},{10,12},{12... | collective-permute-start | bytes 393224 | tf_op jit(solution)/shard_map/ppermute | solution.py:382
  21.9 1.3 %spmm.6.refs_4_ = f32[2,4,128,128]{3,2,1,0:T(8,128)S(1)} custom-call(s32[268]{0:T(512)S(1)} %column_table.1.table, bf16[2,4,8,4,128,128]{5,4,3,2,1,0:T(8,128)(2,1)S(1)} %copy-done, bf16[512,128]{1,0:T(8,128)(2,1)S(1)} %collective-permute-done.1.refs_0_, bf16[512,128]{1,0:T(8,128)(2,1)S(1)} %collective-permute-done.4.refs_1_, ...), custom_call_target="tpu_custom_call" | custom-call | flops 1073741824 | bytes 1048576 | tf_op jit(solution)/shard_map/spmm/pallas_call | solution.py:133
  23.2 0.3 collective-permute-start.9
  23.5 1.8 %collective-permute-start.7 = (bf16[512,128]{1,0:T(8,128)(2,1)S(1)}, bf16[512,128]{1,0:T(8,128)(2,1)S(1)}, u32[]{:S(2)}, u32[]{:S(2)}) collective-permute-start(bf16[512,128]{1,0:T(8,128)(2,1)S(1)} %collective-permute-done.3.refs_0_), channel_id=1, source_target_pairs={{0,2},{2,4},{4,6},{6,7},{7,5},{5,3},{3,1},{1,0},{8,10},{10,12},{12... | collective-permute-start | bytes 393224 | tf_op jit(solution)/shard_map/ppermute | solution.py:391
  25.3 0.4 collective-permute-done.11.refs_2_
  25.7 1.3 %spmm.7.refs_4_ = f32[2,4,128,128]{3,2,1,0:T(8,128)S(1)} custom-call(s32[268]{0:T(512)S(1)} %column_table.1.table, bf16[2,4,8,4,128,128]{5,4,3,2,1,0:T(8,128)(2,1)S(1)} %copy-done, bf16[512,128]{1,0:T(8,128)(2,1)S(1)} %collective-permute-done.3.refs_0_, bf16[512,128]{1,0:T(8,128)(2,1)S(1)} %collective-permute-done.10.refs_1_, ...), custom_call_target="tpu_custom_call" | custom-call | flops 1073741824 | bytes 1048576 | tf_op jit(solution)/shard_map/spmm/pallas_call | solution.py:133
  27.1 1.2 %collective-permute-done.9.refs_3_ = bf16[512,128]{1,0:T(8,128)(2,1)S(1)} collective-permute-done((bf16[512,128]{1,0:T(8,128)(2,1)S(1)}, bf16[512,128]{1,0:T(8,128)(2,1)S(1)}, u32[]{:S(2)}, u32[]{:S(2)}) %collective-permute-start.9) | collective-permute-done | bytes 131104 | tf_op jit(solution)/shard_map/ppermute | solution.py:391
  28.3 0.3 collective-permute-done.7.refs_2_
  28.5 0.4 %spmm_last.1 = (bf16[2,256,128]{2,1,0:T(8,128)(2,1)S(1)}, bf16[2,256,128]{2,1,0:T(8,128)(2,1)S(1)}) custom-call(bf16[512,512]{1,0:T(8,128)(2,1)S(1)} %get-tuple-element.35.refs_0_, bf16[512,512]{1,0:T(8,128)(2,1)S(1)} %get-tuple-element.36.refs_1_, bf16[512,128]{1,0:T(8,128)(2,1)S(1)} %collective-permute-done.7.refs_2_, ...), custom_call_target="tpu_custom_call" | custom-call | flops 134217728 | bytes 1048576 | tf_op jit(solution)/shard_map/spmm_last/pallas_call | solution.py:186
  29.0 1.1 %gates.1.gx_own = f32[2,256,1536]{2,1,0:T(8,128)S(1)} custom-call(bf16[2,256,128]{2,1,0:T(8,128)(2,1)S(1)} %get-tuple-element.47.ax, bf16[128,512]{1,0:T(8,128)(2,1)S(1)} %copy-done.5, bf16[512,1536]{1,0:T(8,128)(2,1)S(1)} %copy-done.1), custom_call_target="tpu_custom_call" | custom-call | flops 1610612736 | bytes 1048576 | tf_op jit(solution)/shard_map/gates/pallas_call | solution.py:214
  30.4 2.1 %recurrence_first.3 = (bf16[128,512]{1,0:T(8,128)(2,1)S(1)}, bf16[2,128,512]{2,1,0:T(8,128)(2,1)S(1)}, bf16[2,128,512]{2,1,0:T(8,128)(2,1)S(1)}, f32[2,128,1536]{2,1,0:T(8,128)S(1)}) custom-call(f32[512,512]{1,0:T(8,128)S(1)} %copy-done.3, f32[2,256,1536]{2,1,0:T(8,128)S(1)} %gates.1.gx_own, bf16[2,256,128]{2,1,0:T(8,128)(2,1)S(1)} %collective-permute-done.12.ax_other, ...), custom_call_target="tpu_custom_call" | custom-call | flops 3221225472 | bytes 1048576 | tf_op jit(solution)/shard_map/recurrence_first/pallas_call | solution.py:273
  32.5 0.3 collective-permute-start.15
  32.8 2.3 %recurrence_first.2 = (bf16[128,512]{1,0:T(8,128)(2,1)S(1)}, bf16[2,128,512]{2,1,0:T(8,128)(2,1)S(1)}, bf16[2,128,512]{2,1,0:T(8,128)(2,1)S(1)}, f32[2,128,1536]{2,1,0:T(8,128)S(1)}) custom-call(f32[512,512]{1,0:T(8,128)S(1)} %copy-done.3, f32[2,256,1536]{2,1,0:T(8,128)S(1)} %gates.1.gx_own, bf16[2,256,128]{2,1,0:T(8,128)(2,1)S(1)} %collective-permute-done.12.ax_other, ...), custom_call_target="tpu_custom_call" | custom-call | flops 3221225472 | bytes 1048576 | tf_op jit(solution)/shard_map/recurrence_first/pallas_call | solution.py:273
  35.1 0.4 collective-permute-start.13
  35.6 3.1 %collective-permute-done.15.state_in = bf16[128,512]{1,0:T(8,128)(2,1)S(1)} collective-permute-done((bf16[128,512]{1,0:T(8,128)(2,1)S(1)}, bf16[128,512]{1,0:T(8,128)(2,1)S(1)}, u32[]{:S(2)}, u32[]{:S(2)}) %collective-permute-start.15) | collective-permute-done | bytes 131104 | tf_op jit(solution)/shard_map/ppermute | solution.py:413
  38.7 2.3 %collective-permute-done.13.state_in = bf16[128,512]{1,0:T(8,128)(2,1)S(1)} collective-permute-done((bf16[128,512]{1,0:T(8,128)(2,1)S(1)}, bf16[128,512]{1,0:T(8,128)(2,1)S(1)}, u32[]{:S(2)}, u32[]{:S(2)}) %collective-permute-start.13) | collective-permute-done | bytes 131104 | tf_op jit(solution)/shard_map/ppermute | solution.py:413
  41.2 0.9 %write_out.2.refs_1_ = bf16[2,512,512]{2,1,0:T(8,128)(2,1)} custom-call(bf16[2,128,512]{2,1,0:T(8,128)(2,1)S(1)} %get-tuple-element.58.refs_0_, bf16[2,128,512]{2,1,0:T(8,128)(2,1)S(1)} %get-tuple-element.59.refs_1_, bf16[2,128,512]{2,1,0:T(8,128)(2,1)S(1)} %collective-permute-done.16.refs_2_), custom_call_target="tpu_custom_call" | custom-call | bytes 1048576 | tf_op jit(solution)/shard_map/write_out/pallas_call | solution.py:342
  42.1 0.6 %collective-permute-done.14.refs_0_ = bf16[2,128,512]{2,1,0:T(8,128)(2,1)S(1)} collective-permute-done((bf16[2,128,512]{2,1,0:T(8,128)(2,1)S(1)}, bf16[2,128,512]{2,1,0:T(8,128)(2,1)S(1)}, u32[]{:S(2)}, u32[]{:S(2)}) %collective-permute-start.14) | collective-permute-done | bytes 262176 | tf_op jit(solution)/shard_map/ppermute | solution.py:422
  42.7 0.7 %write_out.3 = bf16[2,512,512]{2,1,0:T(8,128)(2,1)} custom-call(bf16[2,128,512]{2,1,0:T(8,128)(2,1)S(1)} %collective-permute-done.14.refs_0_, bf16[2,512,512]{2,1,0:T(8,128)(2,1)} %write_out.2.refs_1_), custom_call_target="tpu_custom_call", output_to_operand_aliasing={{}: (1, {})} | custom-call | bytes 1048576 | tf_op jit(solution)/shard_map/write_out/pallas_call | solution.py:342
  (33 shorter events, 1.2 us)
Async XLA Ops:
  0.0 9.5 %collective-permute-start = (bf16[2,512,128]{2,1,0:T(8,128)(2,1)}, bf16[2,512,128]{2,1,0:T(8,128)(2,1)S(1)}, u32[]{:S(2)}, u32[]{:S(2)}) collective-permute-start(bf16[2,512,128]{2,1,0:T(8,128)(2,1)} %refs_0_.2), channel_id=1, source_target_pairs={{0,2},{2,4},{4,6},{6,7},{7,5},{5,3},{3,1},{1,0},{8,10},{10,12},{12... | collective-permute-start | bytes 786440 | tf_op jit(solution)/shard_map/ppermute | solution.py:369
  3.0 8.4 %collective-permute-start.2 = (bf16[2,512,128]{2,1,0:T(8,128)(2,1)}, bf16[2,512,128]{2,1,0:T(8,128)(2,1)S(1)}, u32[]{:S(2)}, u32[]{:S(2)}) collective-permute-start(bf16[2,512,128]{2,1,0:T(8,128)(2,1)} %refs_0_.2), channel_id=1, source_target_pairs={{2,0},{4,2},{6,4},{7,6},{5,7},{3,5},{1,3},{0,1},{10,8},{12,10},{14... | collective-permute-start | bytes 786440 | tf_op jit(solution)/shard_map/ppermute | solution.py:370
  3.8 3.4 %copy-start = (bf16[2,4,8,4,128,128]{5,4,3,2,1,0:T(8,128)(2,1)S(1)}, bf16[2,4,8,4,128,128]{5,4,3,2,1,0:T(8,128)(2,1)}, u32[]{:S(2)}) copy-start(bf16[2,4,8,4,128,128]{5,4,3,2,1,0:T(8,128)(2,1)} %tiles.9) | copy-start | bytes 25165828
  7.1 1.1 %copy-start.4 = (bf16[2,512,128]{2,1,0:T(8,128)(2,1)S(1)}, bf16[2,512,128]{2,1,0:T(8,128)(2,1)}, u32[]{:S(2)}) copy-start(bf16[2,512,128]{2,1,0:T(8,128)(2,1)} %refs_0_.2) | copy-start | bytes 786436
  9.5 5.7 %collective-permute-start.1 = (bf16[512,128]{1,0:T(8,128)(2,1)S(1)}, bf16[512,128]{1,0:T(8,128)(2,1)S(1)}, u32[]{:S(2)}, u32[]{:S(2)}) collective-permute-start(bf16[512,128]{1,0:T(8,128)(2,1)S(1)} %get-tuple-element.64), channel_id=1, source_target_pairs={{0,2},{2,4},{4,6},{6,7},{7,5},{5,3},{3,1},{1,0},{8,10},{10,12},{12... | collective-permute-start | bytes 393224 | tf_op jit(solution)/shard_map/ppermute | solution.py:382
  11.4 6.3 %collective-permute-start.6 = (bf16[512,128]{1,0:T(8,128)(2,1)S(1)}, bf16[512,128]{1,0:T(8,128)(2,1)S(1)}, u32[]{:S(2)}, u32[]{:S(2)}) collective-permute-start(bf16[512,128]{1,0:T(8,128)(2,1)S(1)} %get-tuple-element.61), channel_id=1, source_target_pairs={{2,0},{4,2},{6,4},{7,6},{5,7},{3,5},{1,3},{0,1},{10,8},{12,10},{14... | collective-permute-start | bytes 393224 | tf_op jit(solution)/shard_map/ppermute | solution.py:384
  11.7 8.2 %collective-permute-start.5 = (bf16[512,128]{1,0:T(8,128)(2,1)S(1)}, bf16[512,128]{1,0:T(8,128)(2,1)S(1)}, u32[]{:S(2)}, u32[]{:S(2)}) collective-permute-start(bf16[512,128]{1,0:T(8,128)(2,1)S(1)} %get-tuple-element.62), channel_id=1, source_target_pairs={{2,0},{4,2},{6,4},{7,6},{5,7},{3,5},{1,3},{0,1},{10,8},{12,10},{14... | collective-permute-start | bytes 393224 | tf_op jit(solution)/shard_map/ppermute | solution.py:384
  13.4 6.7 %collective-permute-start.4 = (bf16[512,128]{1,0:T(8,128)(2,1)S(1)}, bf16[512,128]{1,0:T(8,128)(2,1)S(1)}, u32[]{:S(2)}, u32[]{:S(2)}) collective-permute-start(bf16[512,128]{1,0:T(8,128)(2,1)S(1)} %get-tuple-element.63), channel_id=1, source_target_pairs={{0,2},{2,4},{4,6},{6,7},{7,5},{5,3},{3,1},{1,0},{8,10},{10,12},{12... | collective-permute-start | bytes 393224 | tf_op jit(solution)/shard_map/ppermute | solution.py:382
  15.0 10.7 %copy-start.1 = (bf16[512,1536]{1,0:T(8,128)(2,1)S(1)}, bf16[512,1536]{1,0:T(8,128)(2,1)}, u32[]{:S(2)}) copy-start(bf16[512,1536]{1,0:T(8,128)(2,1)} %w_input.3) | copy-start | bytes 4718596
  15.0 10.7 %copy-start.2 = (bf16[512,1536]{1,0:T(8,128)(2,1)S(1)}, bf16[512,1536]{1,0:T(8,128)(2,1)}, u32[]{:S(2)}) copy-start(bf16[512,1536]{1,0:T(8,128)(2,1)} %w_hidden.7) | copy-start | bytes 4718596
  15.0 10.7 %copy-start.3 = (f32[512,512]{1,0:T(8,128)S(1)}, f32[512,512]{1,0:T(8,128)}, u32[]{:S(2)}) copy-start(f32[512,512]{1,0:T(8,128)} %hidden_start.3) | copy-start | bytes 3145732
  15.0 10.7 %copy-start.5 = (bf16[128,512]{1,0:T(8,128)(2,1)S(1)}, bf16[128,512]{1,0:T(8,128)(2,1)}, u32[]{:S(2)}) copy-start(bf16[128,512]{1,0:T(8,128)(2,1)} %w_graph.3) | copy-start | bytes 393220
  15.2 8.0 %collective-permute-start.3 = (bf16[512,128]{1,0:T(8,128)(2,1)S(1)}, bf16[512,128]{1,0:T(8,128)(2,1)S(1)}, u32[]{:S(2)}, u32[]{:S(2)}) collective-permute-start(bf16[512,128]{1,0:T(8,128)(2,1)S(1)} %collective-permute-done.1.refs_0_), channel_id=1, source_target_pairs={{0,2},{2,4},{4,6},{6,7},{7,5},{5,3},{3,1},{1,0},{8,10},{10,12},{12... | collective-permute-start | bytes 393224 | tf_op jit(solution)/shard_map/ppermute | solution.py:382
  17.7 5.5 %collective-permute-start.8 = (bf16[512,128]{1,0:T(8,128)(2,1)S(1)}, bf16[512,128]{1,0:T(8,128)(2,1)S(1)}, u32[]{:S(2)}, u32[]{:S(2)}) collective-permute-start(bf16[512,128]{1,0:T(8,128)(2,1)S(1)} %collective-permute-done.6.refs_3_), channel_id=1, source_target_pairs={{2,0},{4,2},{6,4},{7,6},{5,7},{3,5},{1,3},{0,1},{10,8},{12,10},{14... | collective-permute-start | bytes 393224 | tf_op jit(solution)/shard_map/ppermute | solution.py:384
  19.9 5.8 %collective-permute-start.11 = (bf16[512,128]{1,0:T(8,128)(2,1)S(1)}, bf16[512,128]{1,0:T(8,128)(2,1)S(1)}, u32[]{:S(2)}, u32[]{:S(2)}) collective-permute-start(bf16[512,128]{1,0:T(8,128)(2,1)S(1)} %collective-permute-done.5.refs_2_), channel_id=1, source_target_pairs={{2,0},{4,2},{6,4},{7,6},{5,7},{3,5},{1,3},{0,1},{10,8},{12,10},{14... | collective-permute-start | bytes 393224 | tf_op jit(solution)/shard_map/ppermute | solution.py:384
  20.1 5.6 %collective-permute-start.10 = (bf16[512,128]{1,0:T(8,128)(2,1)S(1)}, bf16[512,128]{1,0:T(8,128)(2,1)S(1)}, u32[]{:S(2)}, u32[]{:S(2)}) collective-permute-start(bf16[512,128]{1,0:T(8,128)(2,1)S(1)} %collective-permute-done.4.refs_1_), channel_id=1, source_target_pairs={{0,2},{2,4},{4,6},{6,7},{7,5},{5,3},{3,1},{1,0},{8,10},{10,12},{12... | collective-permute-start | bytes 393224 | tf_op jit(solution)/shard_map/ppermute | solution.py:382
  23.2 5.0 %collective-permute-start.9 = (bf16[512,128]{1,0:T(8,128)(2,1)S(1)}, bf16[512,128]{1,0:T(8,128)(2,1)S(1)}, u32[]{:S(2)}, u32[]{:S(2)}) collective-permute-start(bf16[512,128]{1,0:T(8,128)(2,1)S(1)} %collective-permute-done.8.refs_3_), channel_id=1, source_target_pairs={{2,0},{4,2},{6,4},{7,6},{5,7},{3,5},{1,3},{0,1},{10,8},{12,10},{14... | collective-permute-start | bytes 393224 | tf_op jit(solution)/shard_map/ppermute | solution.py:391
  23.5 5.0 %collective-permute-start.7 = (bf16[512,128]{1,0:T(8,128)(2,1)S(1)}, bf16[512,128]{1,0:T(8,128)(2,1)S(1)}, u32[]{:S(2)}, u32[]{:S(2)}) collective-permute-start(bf16[512,128]{1,0:T(8,128)(2,1)S(1)} %collective-permute-done.3.refs_0_), channel_id=1, source_target_pairs={{0,2},{2,4},{4,6},{6,7},{7,5},{5,3},{3,1},{1,0},{8,10},{10,12},{12... | collective-permute-start | bytes 393224 | tf_op jit(solution)/shard_map/ppermute | solution.py:391
  29.0 1.4 %collective-permute-start.12 = (bf16[2,256,128]{2,1,0:T(8,128)(2,1)S(1)}, bf16[2,256,128]{2,1,0:T(8,128)(2,1)S(1)}, u32[]{:S(2)}, u32[]{:S(2)}) collective-permute-start(bf16[2,256,128]{2,1,0:T(8,128)(2,1)S(1)} %get-tuple-element.48), channel_id=1, source_target_pairs={{0,8},{8,0},{16,24},{24,16},{1,9},{9,1},{17,25},{25,17},{2,10},{10... | collective-permute-start | bytes 393224 | tf_op jit(solution)/shard_map/ppermute | solution.py:399
  29.0 1.3 %copy-start.6 = (f32[512]{0:T(512)S(1)}, f32[512]{0:T(512)}, u32[]{:S(2)}) copy-start(f32[512]{0:T(512)} %param.17) | copy-start | bytes 6148
  32.5 6.1 %collective-permute-start.15 = (bf16[128,512]{1,0:T(8,128)(2,1)S(1)}, bf16[128,512]{1,0:T(8,128)(2,1)S(1)}, u32[]{:S(2)}, u32[]{:S(2)}) collective-permute-start(bf16[128,512]{1,0:T(8,128)(2,1)S(1)} %get-tuple-element.54), channel_id=1, source_target_pairs={{0,16},{8,24},{16,0},{24,8},{1,17},{9,25},{17,1},{25,9},{2,18},{10... | collective-permute-start | bytes 393224 | tf_op jit(solution)/shard_map/ppermute | solution.py:413
  35.1 5.9 %collective-permute-start.13 = (bf16[128,512]{1,0:T(8,128)(2,1)S(1)}, bf16[128,512]{1,0:T(8,128)(2,1)S(1)}, u32[]{:S(2)}, u32[]{:S(2)}) collective-permute-start(bf16[128,512]{1,0:T(8,128)(2,1)S(1)} %get-tuple-element.49), channel_id=1, source_target_pairs={{0,16},{8,24},{16,0},{24,8},{1,17},{9,25},{17,1},{25,9},{2,18},{10... | collective-permute-start | bytes 393224 | tf_op jit(solution)/shard_map/ppermute | solution.py:413
  38.7 2.5 %collective-permute-start.16 = (bf16[2,128,512]{2,1,0:T(8,128)(2,1)S(1)}, bf16[2,128,512]{2,1,0:T(8,128)(2,1)S(1)}, u32[]{:S(2)}, u32[]{:S(2)}) collective-permute-start(bf16[2,128,512]{2,1,0:T(8,128)(2,1)S(1)} %get-tuple-element.60), channel_id=1, source_target_pairs={{0,8},{8,0},{16,24},{24,16},{1,9},{9,1},{17,25},{25,17},{2,10},{10... | collective-permute-start | bytes 786440 | tf_op jit(solution)/shard_map/ppermute | solution.py:422
  41.1 1.6 %collective-permute-start.14 = (bf16[2,128,512]{2,1,0:T(8,128)(2,1)S(1)}, bf16[2,128,512]{2,1,0:T(8,128)(2,1)S(1)}, u32[]{:S(2)}, u32[]{:S(2)}) collective-permute-start(bf16[2,128,512]{2,1,0:T(8,128)(2,1)S(1)} %get-tuple-element.53), channel_id=1, source_target_pairs={{0,8},{8,0},{16,24},{24,16},{1,9},{9,1},{17,25},{25,17},{2,10},{10... | collective-permute-start | bytes 786440 | tf_op jit(solution)/shard_map/ppermute | solution.py:422

commit v7 on v6

--- a/solution.py
+++ b/solution.py
@@ -382,10 +382,11 @@
                     forward[s] = lax.ppermute(forward[s], "dom", ahead)
                 else:
                     reverse[s] = lax.ppermute(reverse[s], "dom", back)
-        acc = spmm(table, tiles, *waiting.pop(0), acc)
-        for s in range(snaps):
-            passing = forward if s % 2 == 0 else reverse
-            passing[s], acc = lax.optimization_barrier((passing[s], acc))
+        if hop < far - 1:
+            acc = spmm(table, tiles, *waiting.pop(0), acc)
+            for s in range(snaps):
+                passing = forward if s % 2 == 0 else reverse
+                passing[s], acc = lax.optimization_barrier((passing[s], acc))
         waiting.append((forward + reverse, [parts - hop, hop]))
     arriving = [
         lax.ppermute(forward[s], "dom", ahead) if s % 2 == 0 else lax.ppermute(reverse[s], "dom", back)

time: 43.9 us -> 43.5 us (level)
  starting transfers between devices: 14.7 us -> 14.2 us
    ppermute x4, waiting for transfers between devices: 2.57 us -> 3.71 us  [per_device(): reverse[s] = lax.ppermute(reverse[s], 'dom', back)]
    ppermute x1, waiting for transfers between devices: 1.18 us -> 0.22 us  [per_device(): lax.ppermute(reverse[s], 'dom', back)]
    ppermute x4, starting transfers between devices: 6.39 us -> 5.84 us  [per_device(): forward[s] = lax.ppermute(forward[s], 'dom', ahead)]
  transfers between devices with their start and end apart: 17 -> 17, of which waited for: 10 -> 11; matrix products, arithmetic and copies ran while one was open for 2% -> 2% of each run, Pallas kernels for 29% -> 29%
where the time goes in v7:
time: 43.5 us; the launch traced here: 43.3 us
  Pallas kernels  15.9 us (37%)
  starting transfers between devices  14.2 us (33%)
  waiting for transfers between devices  10.8 us (25%)
  local copies, waits for them, and re-layouts  1.3 us (3%)
  other arithmetic  0.73 us (2%)
    ppermute x4, starting transfers between devices, per_device(): forward[s] = lax.ppermute(forward[s], 'dom', ahead)  5.84 us
    ppermute x2, waiting for transfers between devices, per_device(): states = [lax.ppermute(state, 'tm', onward) for state in states]  5.41 us
    pallas_call x4, Pallas kernels, spmm(): pl.pallas_call(kernel, out_shape=jax.ShapeDtypeStruct((snaps, rows, blk,...  4.95 us
    pallas_call x2, Pallas kernels, recurrence_first(): pl.pallas_call(kernel, out_shape=(jax.ShapeDtypeStruct((rows, hid), BF16)...  4.42 us
    ppermute x4, waiting for transfers between devices, per_device(): reverse[s] = lax.ppermute(reverse[s], 'dom', back)  3.71 us
    ppermute x1, starting transfers between devices, per_device(): forward = lax.ppermute(features, 'dom', ahead)  3.02 us
    ppermute x4, starting transfers between devices, per_device(): reverse[s] = lax.ppermute(reverse[s], 'dom', back)  2.37 us
    pallas_call x1, Pallas kernels, column_table(): pl.pallas_call(kernel, out_shape=jax.ShapeDtypeStruct((entries + parts +...  2.14 us
  transfers between devices with their start and end apart: 17, of which 11 were waited for; matrix products, arithmetic and copies ran while one was open for 2% of the time, Pallas kernels for 29%

profile of v7, /device:TPU:0, one launch (start us, length us, event | category | flops | bytes accessed | tf_op | source)
XLA Modules:
  0.0 43.3 jit_solution(11112132281328490662)
XLA Ops:
  0.0 3.0 %collective-permute-start = (bf16[2,512,128]{2,1,0:T(8,128)(2,1)}, bf16[2,512,128]{2,1,0:T(8,128)(2,1)S(1)}, u32[]{:S(2)}, u32[]{:S(2)}) collective-permute-start(bf16[2,512,128]{2,1,0:T(8,128)(2,1)} %refs_0_.2), channel_id=1, source_target_pairs={{0,2},{2,4},{4,6},{6,7},{7,5},{5,3},{3,1},{1,0},{8,10},{10,12},{12... | collective-permute-start | bytes 786440 | tf_op jit(solution)/shard_map/ppermute | solution.py:369
  3.0 0.7 %bitcast_select_fusion.live = s32[2,4,4,8]{3,2,1,0:T(4,128)S(1)} fusion(s32[2,4,8,4]{2,3,1,0:T(4,128)} %param.11, s32[2,4,8]{2,1,0:T(4,128)} %param.12), kind=kLoop, calls=%fused_computation.4 | loop fusion | flops 512 | bytes 2304 | tf_op jit(solution)/shard_map/jit(_where)/select_n | solution.py:67
  3.8 2.1 %column_table.1.table = s32[268]{0:T(512)S(1)} custom-call(s32[2,4,4,8]{3,2,1,0:T(4,128)S(1)} %bitcast_select_fusion.live), custom_call_target="tpu_custom_call" | custom-call | flops 3000000000 | bytes 1048576 | tf_op jit(solution)/shard_map/column_table/pallas_call | solution.py:88
  5.9 1.2 %copy-done = bf16[2,4,8,4,128,128]{5,4,3,2,1,0:T(8,128)(2,1)S(1)} copy-done((bf16[2,4,8,4,128,128]{5,4,3,2,1,0:T(8,128)(2,1)S(1)}, bf16[2,4,8,4,128,128]{5,4,3,2,1,0:T(8,128)(2,1)}, u32[]{:S(2)}) %copy-start) | copy-done | bytes 8388632
  7.1 1.1 %dense_tiles.1 = (bf16[512,512]{1,0:T(8,128)(2,1)S(1)}, bf16[512,512]{1,0:T(8,128)(2,1)S(1)}) custom-call(s32[268]{0:T(512)S(1)} %column_table.1.table, bf16[2,4,8,4,128,128]{5,4,3,2,1,0:T(8,128)(2,1)S(1)} %copy-done), custom_call_target="tpu_custom_call" | custom-call | bytes 1048576 | tf_op jit(solution)/shard_map/dense_tiles/pallas_call | solution.py:160
  8.3 1.0 %spmm.4.refs_2_ = f32[2,4,128,128]{3,2,1,0:T(8,128)S(1)} custom-call(s32[268]{0:T(512)S(1)} %column_table.1.table, bf16[2,4,8,4,128,128]{5,4,3,2,1,0:T(8,128)(2,1)S(1)} %copy-done, bf16[2,512,128]{2,1,0:T(8,128)(2,1)S(1)} %copy-done.4), custom_call_target="tpu_custom_call" | custom-call | flops 536870912 | bytes 1048576 | tf_op jit(solution)/shard_map/spmm/pallas_call | solution.py:133
  9.5 1.9 %collective-permute-start.1 = (bf16[512,128]{1,0:T(8,128)(2,1)S(1)}, bf16[512,128]{1,0:T(8,128)(2,1)S(1)}, u32[]{:S(2)}, u32[]{:S(2)}) collective-permute-start(bf16[512,128]{1,0:T(8,128)(2,1)S(1)} %get-tuple-element.56), channel_id=1, source_target_pairs={{0,2},{2,4},{4,6},{6,7},{7,5},{5,3},{3,1},{1,0},{8,10},{10,12},{12... | collective-permute-start | bytes 393224 | tf_op jit(solution)/shard_map/ppermute | solution.py:382
  11.7 1.8 %collective-permute-start.10 = (bf16[512,128]{1,0:T(8,128)(2,1)S(1)}, bf16[512,128]{1,0:T(8,128)(2,1)S(1)}, u32[]{:S(2)}, u32[]{:S(2)}) collective-permute-start(bf16[512,128]{1,0:T(8,128)(2,1)S(1)} %get-tuple-element.53), channel_id=1, source_target_pairs={{2,0},{4,2},{6,4},{7,6},{5,7},{3,5},{1,3},{0,1},{10,8},{12,10},{14... | collective-permute-start | bytes 393224 | tf_op jit(solution)/shard_map/ppermute | solution.py:384
  13.4 0.2 collective-permute-start.8
  13.7 1.3 %spmm.5.refs_4_ = f32[2,4,128,128]{3,2,1,0:T(8,128)S(1)} custom-call(s32[268]{0:T(512)S(1)} %column_table.1.table, bf16[2,4,8,4,128,128]{5,4,3,2,1,0:T(8,128)(2,1)S(1)} %copy-done, bf16[2,512,128]{2,1,0:T(8,128)(2,1)S(1)} %collective-permute-done.refs_0_, bf16[2,512,128]{2,1,0:T(8,128)(2,1)S(1)} %collective-permute-done.2.refs_1_, ...), custom_call_target="tpu_custom_call" | custom-call | flops 1073741824 | bytes 1048576 | tf_op jit(solution)/shard_map/spmm/pallas_call | solution.py:133
  15.2 2.1 %collective-permute-done.5.refs_3_ = bf16[512,128]{1,0:T(8,128)(2,1)S(1)} collective-permute-done((bf16[512,128]{1,0:T(8,128)(2,1)S(1)}, bf16[512,128]{1,0:T(8,128)(2,1)S(1)}, u32[]{:S(2)}, u32[]{:S(2)}) %collective-permute-start.5) | collective-permute-done | bytes 131104 | tf_op jit(solution)/shard_map/ppermute | solution.py:384
  17.3 0.3 collective-permute-start.6
  17.6 1.8 %collective-permute-start.3 = (bf16[512,128]{1,0:T(8,128)(2,1)S(1)}, bf16[512,128]{1,0:T(8,128)(2,1)S(1)}, u32[]{:S(2)}, u32[]{:S(2)}) collective-permute-start(bf16[512,128]{1,0:T(8,128)(2,1)S(1)} %collective-permute-done.1.refs_0_), channel_id=1, source_target_pairs={{0,2},{2,4},{4,6},{6,7},{7,5},{5,3},{3,1},{1,0},{8,10},{10,12},{12... | collective-permute-start | bytes 393224 | tf_op jit(solution)/shard_map/ppermute | solution.py:382
  19.3 0.8 %collective-permute-done.10.refs_2_ = bf16[512,128]{1,0:T(8,128)(2,1)S(1)} collective-permute-done((bf16[512,128]{1,0:T(8,128)(2,1)S(1)}, bf16[512,128]{1,0:T(8,128)(2,1)S(1)}, u32[]{:S(2)}, u32[]{:S(2)}) %collective-permute-start.10) | collective-permute-done | bytes 131104 | tf_op jit(solution)/shard_map/ppermute | solution.py:384
  20.2 1.9 %collective-permute-start.9 = (bf16[512,128]{1,0:T(8,128)(2,1)S(1)}, bf16[512,128]{1,0:T(8,128)(2,1)S(1)}, u32[]{:S(2)}, u32[]{:S(2)}) collective-permute-start(bf16[512,128]{1,0:T(8,128)(2,1)S(1)} %collective-permute-done.8.refs_1_), channel_id=1, source_target_pairs={{0,2},{2,4},{4,6},{6,7},{7,5},{5,3},{3,1},{1,0},{8,10},{10,12},{12... | collective-permute-start | bytes 393224 | tf_op jit(solution)/shard_map/ppermute | solution.py:382
  22.1 0.8 %collective-permute-done.6.refs_3_ = bf16[512,128]{1,0:T(8,128)(2,1)S(1)} collective-permute-done((bf16[512,128]{1,0:T(8,128)(2,1)S(1)}, bf16[512,128]{1,0:T(8,128)(2,1)S(1)}, u32[]{:S(2)}, u32[]{:S(2)}) %collective-permute-start.6) | collective-permute-done | bytes 131104 | tf_op jit(solution)/shard_map/ppermute | solution.py:384
  23.0 0.2 collective-permute-start.7
  23.2 1.8 %collective-permute-start.4 = (bf16[512,128]{1,0:T(8,128)(2,1)S(1)}, bf16[512,128]{1,0:T(8,128)(2,1)S(1)}, u32[]{:S(2)}, u32[]{:S(2)}) collective-permute-start(bf16[512,128]{1,0:T(8,128)(2,1)S(1)} %collective-permute-done.3.refs_0_), channel_id=1, source_target_pairs={{0,2},{2,4},{4,6},{6,7},{7,5},{5,3},{3,1},{1,0},{8,10},{10,12},{12... | collective-permute-start | bytes 393224 | tf_op jit(solution)/shard_map/ppermute | solution.py:392
  25.0 1.3 %spmm.6.refs_4_ = f32[2,4,128,128]{3,2,1,0:T(8,128)S(1)} custom-call(s32[268]{0:T(512)S(1)} %column_table.1.table, bf16[2,4,8,4,128,128]{5,4,3,2,1,0:T(8,128)(2,1)S(1)} %copy-done, bf16[512,128]{1,0:T(8,128)(2,1)S(1)} %collective-permute-done.1.refs_0_, bf16[512,128]{1,0:T(8,128)(2,1)S(1)} %collective-permute-done.8.refs_1_, ...), custom_call_target="tpu_custom_call" | custom-call | flops 1073741824 | bytes 1048576 | tf_op jit(solution)/shard_map/spmm/pallas_call | solution.py:133
  26.4 1.3 %spmm.7.refs_4_ = f32[2,4,128,128]{3,2,1,0:T(8,128)S(1)} custom-call(s32[268]{0:T(512)S(1)} %column_table.1.table, bf16[2,4,8,4,128,128]{5,4,3,2,1,0:T(8,128)(2,1)S(1)} %copy-done, bf16[512,128]{1,0:T(8,128)(2,1)S(1)} %collective-permute-done.3.refs_0_, bf16[512,128]{1,0:T(8,128)(2,1)S(1)} %collective-permute-done.9.refs_1_, ...), custom_call_target="tpu_custom_call" | custom-call | flops 1073741824 | bytes 1048576 | tf_op jit(solution)/shard_map/spmm/pallas_call | solution.py:133
  27.9 0.3 collective-permute-done.4.refs_2_
  28.2 0.4 %spmm_last.1 = (bf16[2,256,128]{2,1,0:T(8,128)(2,1)S(1)}, bf16[2,256,128]{2,1,0:T(8,128)(2,1)S(1)}) custom-call(bf16[512,512]{1,0:T(8,128)(2,1)S(1)} %get-tuple-element.31.refs_0_, bf16[512,512]{1,0:T(8,128)(2,1)S(1)} %get-tuple-element.32.refs_1_, bf16[512,128]{1,0:T(8,128)(2,1)S(1)} %collective-permute-done.4.refs_2_, ...), custom_call_target="tpu_custom_call" | custom-call | flops 134217728 | bytes 1048576 | tf_op jit(solution)/shard_map/spmm_last/pallas_call | solution.py:186
  28.7 1.1 %gates.1.gx_own = f32[2,256,1536]{2,1,0:T(8,128)S(1)} custom-call(bf16[2,256,128]{2,1,0:T(8,128)(2,1)S(1)} %get-tuple-element.39.ax, bf16[128,512]{1,0:T(8,128)(2,1)S(1)} %copy-done.5, bf16[512,1536]{1,0:T(8,128)(2,1)S(1)} %copy-done.1), custom_call_target="tpu_custom_call" | custom-call | flops 1610612736 | bytes 1048576 | tf_op jit(solution)/shard_map/gates/pallas_call | solution.py:214
  30.1 2.1 %recurrence_first.3 = (bf16[128,512]{1,0:T(8,128)(2,1)S(1)}, bf16[2,128,512]{2,1,0:T(8,128)(2,1)S(1)}, bf16[2,128,512]{2,1,0:T(8,128)(2,1)S(1)}, f32[2,128,1536]{2,1,0:T(8,128)S(1)}) custom-call(f32[512,512]{1,0:T(8,128)S(1)} %copy-done.3, f32[2,256,1536]{2,1,0:T(8,128)S(1)} %gates.1.gx_own, bf16[2,256,128]{2,1,0:T(8,128)(2,1)S(1)} %collective-permute-done.12.ax_other, ...), custom_call_target="tpu_custom_call" | custom-call | flops 3221225472 | bytes 1048576 | tf_op jit(solution)/shard_map/recurrence_first/pallas_call | solution.py:273
  32.2 0.3 collective-permute-start.15
  32.5 2.3 %recurrence_first.2 = (bf16[128,512]{1,0:T(8,128)(2,1)S(1)}, bf16[2,128,512]{2,1,0:T(8,128)(2,1)S(1)}, bf16[2,128,512]{2,1,0:T(8,128)(2,1)S(1)}, f32[2,128,1536]{2,1,0:T(8,128)S(1)}) custom-call(f32[512,512]{1,0:T(8,128)S(1)} %copy-done.3, f32[2,256,1536]{2,1,0:T(8,128)S(1)} %gates.1.gx_own, bf16[2,256,128]{2,1,0:T(8,128)(2,1)S(1)} %collective-permute-done.12.ax_other, ...), custom_call_target="tpu_custom_call" | custom-call | flops 3221225472 | bytes 1048576 | tf_op jit(solution)/shard_map/recurrence_first/pallas_call | solution.py:273
  34.8 0.4 collective-permute-start.13
  35.2 3.1 %collective-permute-done.15.state_in = bf16[128,512]{1,0:T(8,128)(2,1)S(1)} collective-permute-done((bf16[128,512]{1,0:T(8,128)(2,1)S(1)}, bf16[128,512]{1,0:T(8,128)(2,1)S(1)}, u32[]{:S(2)}, u32[]{:S(2)}) %collective-permute-start.15) | collective-permute-done | bytes 131104 | tf_op jit(solution)/shard_map/ppermute | solution.py:414
  38.4 2.3 %collective-permute-done.13.state_in = bf16[128,512]{1,0:T(8,128)(2,1)S(1)} collective-permute-done((bf16[128,512]{1,0:T(8,128)(2,1)S(1)}, bf16[128,512]{1,0:T(8,128)(2,1)S(1)}, u32[]{:S(2)}, u32[]{:S(2)}) %collective-permute-start.13) | collective-permute-done | bytes 131104 | tf_op jit(solution)/shard_map/ppermute | solution.py:414
  40.9 0.9 %write_out.2.refs_1_ = bf16[2,512,512]{2,1,0:T(8,128)(2,1)} custom-call(bf16[2,128,512]{2,1,0:T(8,128)(2,1)S(1)} %get-tuple-element.50.refs_0_, bf16[2,128,512]{2,1,0:T(8,128)(2,1)S(1)} %get-tuple-element.51.refs_1_, bf16[2,128,512]{2,1,0:T(8,128)(2,1)S(1)} %collective-permute-done.16.refs_2_), custom_call_target="tpu_custom_call" | custom-call | bytes 1048576 | tf_op jit(solution)/shard_map/write_out/pallas_call | solution.py:342
  41.8 0.6 %collective-permute-done.14.refs_0_ = bf16[2,128,512]{2,1,0:T(8,128)(2,1)S(1)} collective-permute-done((bf16[2,128,512]{2,1,0:T(8,128)(2,1)S(1)}, bf16[2,128,512]{2,1,0:T(8,128)(2,1)S(1)}, u32[]{:S(2)}, u32[]{:S(2)}) %collective-permute-start.14) | collective-permute-done | bytes 262176 | tf_op jit(solution)/shard_map/ppermute | solution.py:423
  42.4 0.7 %write_out.3 = bf16[2,512,512]{2,1,0:T(8,128)(2,1)} custom-call(bf16[2,128,512]{2,1,0:T(8,128)(2,1)S(1)} %collective-permute-done.14.refs_0_, bf16[2,512,512]{2,1,0:T(8,128)(2,1)} %write_out.2.refs_1_), custom_call_target="tpu_custom_call", output_to_operand_aliasing={{}: (1, {})} | custom-call | bytes 1048576 | tf_op jit(solution)/shard_map/write_out/pallas_call | solution.py:342
  (33 shorter events, 1.5 us)
Async XLA Ops:
  0.0 9.5 %collective-permute-start = (bf16[2,512,128]{2,1,0:T(8,128)(2,1)}, bf16[2,512,128]{2,1,0:T(8,128)(2,1)S(1)}, u32[]{:S(2)}, u32[]{:S(2)}) collective-permute-start(bf16[2,512,128]{2,1,0:T(8,128)(2,1)} %refs_0_.2), channel_id=1, source_target_pairs={{0,2},{2,4},{4,6},{6,7},{7,5},{5,3},{3,1},{1,0},{8,10},{10,12},{12... | collective-permute-start | bytes 786440 | tf_op jit(solution)/shard_map/ppermute | solution.py:369
  3.0 8.4 %collective-permute-start.2 = (bf16[2,512,128]{2,1,0:T(8,128)(2,1)}, bf16[2,512,128]{2,1,0:T(8,128)(2,1)S(1)}, u32[]{:S(2)}, u32[]{:S(2)}) collective-permute-start(bf16[2,512,128]{2,1,0:T(8,128)(2,1)} %refs_0_.2), channel_id=1, source_target_pairs={{2,0},{4,2},{6,4},{7,6},{5,7},{3,5},{1,3},{0,1},{10,8},{12,10},{14... | collective-permute-start | bytes 786440 | tf_op jit(solution)/shard_map/ppermute | solution.py:370
  3.8 3.4 %copy-start = (bf16[2,4,8,4,128,128]{5,4,3,2,1,0:T(8,128)(2,1)S(1)}, bf16[2,4,8,4,128,128]{5,4,3,2,1,0:T(8,128)(2,1)}, u32[]{:S(2)}) copy-start(bf16[2,4,8,4,128,128]{5,4,3,2,1,0:T(8,128)(2,1)} %tiles.9) | copy-start | bytes 25165828
  7.1 1.1 %copy-start.4 = (bf16[2,512,128]{2,1,0:T(8,128)(2,1)S(1)}, bf16[2,512,128]{2,1,0:T(8,128)(2,1)}, u32[]{:S(2)}) copy-start(bf16[2,512,128]{2,1,0:T(8,128)(2,1)} %refs_0_.2) | copy-start | bytes 786436
  9.5 5.7 %collective-permute-start.1 = (bf16[512,128]{1,0:T(8,128)(2,1)S(1)}, bf16[512,128]{1,0:T(8,128)(2,1)S(1)}, u32[]{:S(2)}, u32[]{:S(2)}) collective-permute-start(bf16[512,128]{1,0:T(8,128)(2,1)S(1)} %get-tuple-element.56), channel_id=1, source_target_pairs={{0,2},{2,4},{4,6},{6,7},{7,5},{5,3},{3,1},{1,0},{8,10},{10,12},{12... | collective-permute-start | bytes 393224 | tf_op jit(solution)/shard_map/ppermute | solution.py:382
  11.4 5.9 %collective-permute-start.5 = (bf16[512,128]{1,0:T(8,128)(2,1)S(1)}, bf16[512,128]{1,0:T(8,128)(2,1)S(1)}, u32[]{:S(2)}, u32[]{:S(2)}) collective-permute-start(bf16[512,128]{1,0:T(8,128)(2,1)S(1)} %get-tuple-element.54), channel_id=1, source_target_pairs={{2,0},{4,2},{6,4},{7,6},{5,7},{3,5},{1,3},{0,1},{10,8},{12,10},{14... | collective-permute-start | bytes 393224 | tf_op jit(solution)/shard_map/ppermute | solution.py:384
  11.7 8.5 %collective-permute-start.10 = (bf16[512,128]{1,0:T(8,128)(2,1)S(1)}, bf16[512,128]{1,0:T(8,128)(2,1)S(1)}, u32[]{:S(2)}, u32[]{:S(2)}) collective-permute-start(bf16[512,128]{1,0:T(8,128)(2,1)S(1)} %get-tuple-element.53), channel_id=1, source_target_pairs={{2,0},{4,2},{6,4},{7,6},{5,7},{3,5},{1,3},{0,1},{10,8},{12,10},{14... | collective-permute-start | bytes 393224 | tf_op jit(solution)/shard_map/ppermute | solution.py:384
  13.4 6.8 %collective-permute-start.8 = (bf16[512,128]{1,0:T(8,128)(2,1)S(1)}, bf16[512,128]{1,0:T(8,128)(2,1)S(1)}, u32[]{:S(2)}, u32[]{:S(2)}) collective-permute-start(bf16[512,128]{1,0:T(8,128)(2,1)S(1)} %get-tuple-element.55), channel_id=1, source_target_pairs={{0,2},{2,4},{4,6},{6,7},{7,5},{5,3},{3,1},{1,0},{8,10},{10,12},{12... | collective-permute-start | bytes 393224 | tf_op jit(solution)/shard_map/ppermute | solution.py:382
  15.0 11.3 %copy-start.1 = (bf16[512,1536]{1,0:T(8,128)(2,1)S(1)}, bf16[512,1536]{1,0:T(8,128)(2,1)}, u32[]{:S(2)}) copy-start(bf16[512,1536]{1,0:T(8,128)(2,1)} %w_input.3) | copy-start | bytes 4718596
  15.0 11.3 %copy-start.2 = (bf16[512,1536]{1,0:T(8,128)(2,1)S(1)}, bf16[512,1536]{1,0:T(8,128)(2,1)}, u32[]{:S(2)}) copy-start(bf16[512,1536]{1,0:T(8,128)(2,1)} %w_hidden.7) | copy-start | bytes 4718596
  15.0 11.3 %copy-start.3 = (f32[512,512]{1,0:T(8,128)S(1)}, f32[512,512]{1,0:T(8,128)}, u32[]{:S(2)}) copy-start(f32[512,512]{1,0:T(8,128)} %hidden_start.3) | copy-start | bytes 3145732
  15.0 11.3 %copy-start.5 = (bf16[128,512]{1,0:T(8,128)(2,1)S(1)}, bf16[128,512]{1,0:T(8,128)(2,1)}, u32[]{:S(2)}) copy-start(bf16[128,512]{1,0:T(8,128)(2,1)} %w_graph.3) | copy-start | bytes 393220
  17.3 5.7 %collective-permute-start.6 = (bf16[512,128]{1,0:T(8,128)(2,1)S(1)}, bf16[512,128]{1,0:T(8,128)(2,1)S(1)}, u32[]{:S(2)}, u32[]{:S(2)}) collective-permute-start(bf16[512,128]{1,0:T(8,128)(2,1)S(1)} %collective-permute-done.5.refs_3_), channel_id=1, source_target_pairs={{2,0},{4,2},{6,4},{7,6},{5,7},{3,5},{1,3},{0,1},{10,8},{12,10},{14... | collective-permute-start | bytes 393224 | tf_op jit(solution)/shard_map/ppermute | solution.py:384
  17.6 5.7 %collective-permute-start.3 = (bf16[512,128]{1,0:T(8,128)(2,1)S(1)}, bf16[512,128]{1,0:T(8,128)(2,1)S(1)}, u32[]{:S(2)}, u32[]{:S(2)}) collective-permute-start(bf16[512,128]{1,0:T(8,128)(2,1)S(1)} %collective-permute-done.1.refs_0_), channel_id=1, source_target_pairs={{0,2},{2,4},{4,6},{6,7},{7,5},{5,3},{3,1},{1,0},{8,10},{10,12},{12... | collective-permute-start | bytes 393224 | tf_op jit(solution)/shard_map/ppermute | solution.py:382
  20.1 6.2 %collective-permute-start.11 = (bf16[512,128]{1,0:T(8,128)(2,1)S(1)}, bf16[512,128]{1,0:T(8,128)(2,1)S(1)}, u32[]{:S(2)}, u32[]{:S(2)}) collective-permute-start(bf16[512,128]{1,0:T(8,128)(2,1)S(1)} %collective-permute-done.10.refs_2_), channel_id=1, source_target_pairs={{2,0},{4,2},{6,4},{7,6},{5,7},{3,5},{1,3},{0,1},{10,8},{12,10},{14... | collective-permute-start | bytes 393224 | tf_op jit(solution)/shard_map/ppermute | solution.py:384
  20.2 6.1 %collective-permute-start.9 = (bf16[512,128]{1,0:T(8,128)(2,1)S(1)}, bf16[512,128]{1,0:T(8,128)(2,1)S(1)}, u32[]{:S(2)}, u32[]{:S(2)}) collective-permute-start(bf16[512,128]{1,0:T(8,128)(2,1)S(1)} %collective-permute-done.8.refs_1_), channel_id=1, source_target_pairs={{0,2},{2,4},{4,6},{6,7},{7,5},{5,3},{3,1},{1,0},{8,10},{10,12},{12... | collective-permute-start | bytes 393224 | tf_op jit(solution)/shard_map/ppermute | solution.py:382
  23.0 5.0 %collective-permute-start.7 = (bf16[512,128]{1,0:T(8,128)(2,1)S(1)}, bf16[512,128]{1,0:T(8,128)(2,1)S(1)}, u32[]{:S(2)}, u32[]{:S(2)}) collective-permute-start(bf16[512,128]{1,0:T(8,128)(2,1)S(1)} %collective-permute-done.6.refs_3_), channel_id=1, source_target_pairs={{2,0},{4,2},{6,4},{7,6},{5,7},{3,5},{1,3},{0,1},{10,8},{12,10},{14... | collective-permute-start | bytes 393224 | tf_op jit(solution)/shard_map/ppermute | solution.py:392
  23.2 5.0 %collective-permute-start.4 = (bf16[512,128]{1,0:T(8,128)(2,1)S(1)}, bf16[512,128]{1,0:T(8,128)(2,1)S(1)}, u32[]{:S(2)}, u32[]{:S(2)}) collective-permute-start(bf16[512,128]{1,0:T(8,128)(2,1)S(1)} %collective-permute-done.3.refs_0_), channel_id=1, source_target_pairs={{0,2},{2,4},{4,6},{6,7},{7,5},{5,3},{3,1},{1,0},{8,10},{10,12},{12... | collective-permute-start | bytes 393224 | tf_op jit(solution)/shard_map/ppermute | solution.py:392
  28.6 1.4 %collective-permute-start.12 = (bf16[2,256,128]{2,1,0:T(8,128)(2,1)S(1)}, bf16[2,256,128]{2,1,0:T(8,128)(2,1)S(1)}, u32[]{:S(2)}, u32[]{:S(2)}) collective-permute-start(bf16[2,256,128]{2,1,0:T(8,128)(2,1)S(1)} %get-tuple-element.40), channel_id=1, source_target_pairs={{0,8},{8,0},{16,24},{24,16},{1,9},{9,1},{17,25},{25,17},{2,10},{10... | collective-permute-start | bytes 393224 | tf_op jit(solution)/shard_map/ppermute | solution.py:400
  28.7 1.3 %copy-start.6 = (f32[512]{0:T(512)S(1)}, f32[512]{0:T(512)}, u32[]{:S(2)}) copy-start(f32[512]{0:T(512)} %param.17) | copy-start | bytes 6148
  32.2 6.1 %collective-permute-start.15 = (bf16[128,512]{1,0:T(8,128)(2,1)S(1)}, bf16[128,512]{1,0:T(8,128)(2,1)S(1)}, u32[]{:S(2)}, u32[]{:S(2)}) collective-permute-start(bf16[128,512]{1,0:T(8,128)(2,1)S(1)} %get-tuple-element.46), channel_id=1, source_target_pairs={{0,16},{8,24},{16,0},{24,8},{1,17},{9,25},{17,1},{25,9},{2,18},{10... | collective-permute-start | bytes 393224 | tf_op jit(solution)/shard_map/ppermute | solution.py:414
  34.8 6.0 %collective-permute-start.13 = (bf16[128,512]{1,0:T(8,128)(2,1)S(1)}, bf16[128,512]{1,0:T(8,128)(2,1)S(1)}, u32[]{:S(2)}, u32[]{:S(2)}) collective-permute-start(bf16[128,512]{1,0:T(8,128)(2,1)S(1)} %get-tuple-element.41), channel_id=1, source_target_pairs={{0,16},{8,24},{16,0},{24,8},{1,17},{9,25},{17,1},{25,9},{2,18},{10... | collective-permute-start | bytes 393224 | tf_op jit(solution)/shard_map/ppermute | solution.py:414
  38.3 2.5 %collective-permute-start.16 = (bf16[2,128,512]{2,1,0:T(8,128)(2,1)S(1)}, bf16[2,128,512]{2,1,0:T(8,128)(2,1)S(1)}, u32[]{:S(2)}, u32[]{:S(2)}) collective-permute-start(bf16[2,128,512]{2,1,0:T(8,128)(2,1)S(1)} %get-tuple-element.52), channel_id=1, source_target_pairs={{0,8},{8,0},{16,24},{24,16},{1,9},{9,1},{17,25},{25,17},{2,10},{10... | collective-permute-start | bytes 786440 | tf_op jit(solution)/shard_map/ppermute | solution.py:423
  40.8 1.6 %collective-permute-start.14 = (bf16[2,128,512]{2,1,0:T(8,128)(2,1)S(1)}, bf16[2,128,512]{2,1,0:T(8,128)(2,1)S(1)}, u32[]{:S(2)}, u32[]{:S(2)}) collective-permute-start(bf16[2,128,512]{2,1,0:T(8,128)(2,1)S(1)} %get-tuple-element.45), channel_id=1, source_target_pairs={{0,8},{8,0},{16,24},{24,16},{1,9},{9,1},{17,25},{25,17},{2,10},{10... | collective-permute-start | bytes 786440 | tf_op jit(solution)/shard_map/ppermute | solution.py:423

commit v8 on v7

--- a/solution.py
+++ b/solution.py
@@ -384,7 +384,7 @@
                     reverse[s] = lax.ppermute(reverse[s], "dom", back)
         if hop < far - 1:
             acc = spmm(table, tiles, *waiting.pop(0), acc)
-            for s in range(snaps):
+            for s in range(1):
                 passing = forward if s % 2 == 0 else reverse
                 passing[s], acc = lax.optimization_barrier((passing[s], acc))
         waiting.append((forward + reverse, [parts - hop, hop]))

time: 43.5 us -> 43.5 us (level)
  no operation moved by 1% of the time
where the time goes in v8:
time: 43.5 us; the launch traced here: 43.3 us
  Pallas kernels  15.9 us (37%)
  starting transfers between devices  14.2 us (33%)
  waiting for transfers between devices  10.8 us (25%)
  local copies, waits for them, and re-layouts  1.3 us (3%)
  other arithmetic  0.73 us (2%)
    ppermute x4, starting transfers between devices, per_device(): forward[s] = lax.ppermute(forward[s], 'dom', ahead)  5.84 us
    ppermute x2, waiting for transfers between devices, per_device(): states = [lax.ppermute(state, 'tm', onward) for state in states]  5.41 us
    pallas_call x4, Pallas kernels, spmm(): pl.pallas_call(kernel, out_shape=jax.ShapeDtypeStruct((snaps, rows, blk,...  4.95 us
    pallas_call x2, Pallas kernels, recurrence_first(): pl.pallas_call(kernel, out_shape=(jax.ShapeDtypeStruct((rows, hid), BF16)...  4.42 us
    ppermute x4, waiting for transfers between devices, per_device(): reverse[s] = lax.ppermute(reverse[s], 'dom', back)  3.71 us
    ppermute x1, starting transfers between devices, per_device(): forward = lax.ppermute(features, 'dom', ahead)  3.02 us
    ppermute x4, starting transfers between devices, per_device(): reverse[s] = lax.ppermute(reverse[s], 'dom', back)  2.37 us
    pallas_call x1, Pallas kernels, column_table(): pl.pallas_call(kernel, out_shape=jax.ShapeDtypeStruct((entries + parts +...  2.14 us
  transfers between devices with their start and end apart: 17, of which 11 were waited for; matrix products, arithmetic and copies ran while one was open for 2% of the time, Pallas kernels for 29%

profile of v8, /device:TPU:0, one launch (start us, length us, event | category | flops | bytes accessed | tf_op | source)
XLA Modules:
  0.0 43.3 jit_solution(11112132281328490662)
XLA Ops:
  0.0 3.0 %collective-permute-start = (bf16[2,512,128]{2,1,0:T(8,128)(2,1)}, bf16[2,512,128]{2,1,0:T(8,128)(2,1)S(1)}, u32[]{:S(2)}, u32[]{:S(2)}) collective-permute-start(bf16[2,512,128]{2,1,0:T(8,128)(2,1)} %refs_0_.2), channel_id=1, source_target_pairs={{0,2},{2,4},{4,6},{6,7},{7,5},{5,3},{3,1},{1,0},{8,10},{10,12},{12... | collective-permute-start | bytes 786440 | tf_op jit(solution)/shard_map/ppermute | solution.py:369
  3.0 0.7 %bitcast_select_fusion.live = s32[2,4,4,8]{3,2,1,0:T(4,128)S(1)} fusion(s32[2,4,8,4]{2,3,1,0:T(4,128)} %param.11, s32[2,4,8]{2,1,0:T(4,128)} %param.12), kind=kLoop, calls=%fused_computation.4 | loop fusion | flops 512 | bytes 2304 | tf_op jit(solution)/shard_map/jit(_where)/select_n | solution.py:67
  3.8 2.1 %column_table.1.table = s32[268]{0:T(512)S(1)} custom-call(s32[2,4,4,8]{3,2,1,0:T(4,128)S(1)} %bitcast_select_fusion.live), custom_call_target="tpu_custom_call" | custom-call | flops 3000000000 | bytes 1048576 | tf_op jit(solution)/shard_map/column_table/pallas_call | solution.py:88
  5.9 1.2 %copy-done = bf16[2,4,8,4,128,128]{5,4,3,2,1,0:T(8,128)(2,1)S(1)} copy-done((bf16[2,4,8,4,128,128]{5,4,3,2,1,0:T(8,128)(2,1)S(1)}, bf16[2,4,8,4,128,128]{5,4,3,2,1,0:T(8,128)(2,1)}, u32[]{:S(2)}) %copy-start) | copy-done | bytes 8388632
  7.1 1.1 %dense_tiles.1 = (bf16[512,512]{1,0:T(8,128)(2,1)S(1)}, bf16[512,512]{1,0:T(8,128)(2,1)S(1)}) custom-call(s32[268]{0:T(512)S(1)} %column_table.1.table, bf16[2,4,8,4,128,128]{5,4,3,2,1,0:T(8,128)(2,1)S(1)} %copy-done), custom_call_target="tpu_custom_call" | custom-call | bytes 1048576 | tf_op jit(solution)/shard_map/dense_tiles/pallas_call | solution.py:160
  8.3 1.0 %spmm.4.refs_2_ = f32[2,4,128,128]{3,2,1,0:T(8,128)S(1)} custom-call(s32[268]{0:T(512)S(1)} %column_table.1.table, bf16[2,4,8,4,128,128]{5,4,3,2,1,0:T(8,128)(2,1)S(1)} %copy-done, bf16[2,512,128]{2,1,0:T(8,128)(2,1)S(1)} %copy-done.4), custom_call_target="tpu_custom_call" | custom-call | flops 536870912 | bytes 1048576 | tf_op jit(solution)/shard_map/spmm/pallas_call | solution.py:133
  9.5 1.9 %collective-permute-start.1 = (bf16[512,128]{1,0:T(8,128)(2,1)S(1)}, bf16[512,128]{1,0:T(8,128)(2,1)S(1)}, u32[]{:S(2)}, u32[]{:S(2)}) collective-permute-start(bf16[512,128]{1,0:T(8,128)(2,1)S(1)} %get-tuple-element.52), channel_id=1, source_target_pairs={{0,2},{2,4},{4,6},{6,7},{7,5},{5,3},{3,1},{1,0},{8,10},{10,12},{12... | collective-permute-start | bytes 393224 | tf_op jit(solution)/shard_map/ppermute | solution.py:382
  11.7 1.8 %collective-permute-start.10 = (bf16[512,128]{1,0:T(8,128)(2,1)S(1)}, bf16[512,128]{1,0:T(8,128)(2,1)S(1)}, u32[]{:S(2)}, u32[]{:S(2)}) collective-permute-start(bf16[512,128]{1,0:T(8,128)(2,1)S(1)} %get-tuple-element.49), channel_id=1, source_target_pairs={{2,0},{4,2},{6,4},{7,6},{5,7},{3,5},{1,3},{0,1},{10,8},{12,10},{14... | collective-permute-start | bytes 393224 | tf_op jit(solution)/shard_map/ppermute | solution.py:384
  13.4 0.2 collective-permute-start.8
  13.7 1.3 %spmm.5.refs_4_ = f32[2,4,128,128]{3,2,1,0:T(8,128)S(1)} custom-call(s32[268]{0:T(512)S(1)} %column_table.1.table, bf16[2,4,8,4,128,128]{5,4,3,2,1,0:T(8,128)(2,1)S(1)} %copy-done, bf16[2,512,128]{2,1,0:T(8,128)(2,1)S(1)} %collective-permute-done.refs_0_, bf16[2,512,128]{2,1,0:T(8,128)(2,1)S(1)} %collective-permute-done.2.refs_1_, ...), custom_call_target="tpu_custom_call" | custom-call | flops 1073741824 | bytes 1048576 | tf_op jit(solution)/shard_map/spmm/pallas_call | solution.py:133
  15.2 2.1 %collective-permute-done.5.refs_3_ = bf16[512,128]{1,0:T(8,128)(2,1)S(1)} collective-permute-done((bf16[512,128]{1,0:T(8,128)(2,1)S(1)}, bf16[512,128]{1,0:T(8,128)(2,1)S(1)}, u32[]{:S(2)}, u32[]{:S(2)}) %collective-permute-start.5) | collective-permute-done | bytes 131104 | tf_op jit(solution)/shard_map/ppermute | solution.py:384
  17.3 0.3 collective-permute-start.6
  17.6 1.8 %collective-permute-start.3 = (bf16[512,128]{1,0:T(8,128)(2,1)S(1)}, bf16[512,128]{1,0:T(8,128)(2,1)S(1)}, u32[]{:S(2)}, u32[]{:S(2)}) collective-permute-start(bf16[512,128]{1,0:T(8,128)(2,1)S(1)} %collective-permute-done.1.refs_0_), channel_id=1, source_target_pairs={{0,2},{2,4},{4,6},{6,7},{7,5},{5,3},{3,1},{1,0},{8,10},{10,12},{12... | collective-permute-start | bytes 393224 | tf_op jit(solution)/shard_map/ppermute | solution.py:382
  19.3 0.8 %collective-permute-done.10.refs_2_ = bf16[512,128]{1,0:T(8,128)(2,1)S(1)} collective-permute-done((bf16[512,128]{1,0:T(8,128)(2,1)S(1)}, bf16[512,128]{1,0:T(8,128)(2,1)S(1)}, u32[]{:S(2)}, u32[]{:S(2)}) %collective-permute-start.10) | collective-permute-done | bytes 131104 | tf_op jit(solution)/shard_map/ppermute | solution.py:384
  20.2 1.9 %collective-permute-start.9 = (bf16[512,128]{1,0:T(8,128)(2,1)S(1)}, bf16[512,128]{1,0:T(8,128)(2,1)S(1)}, u32[]{:S(2)}, u32[]{:S(2)}) collective-permute-start(bf16[512,128]{1,0:T(8,128)(2,1)S(1)} %collective-permute-done.8.refs_1_), channel_id=1, source_target_pairs={{0,2},{2,4},{4,6},{6,7},{7,5},{5,3},{3,1},{1,0},{8,10},{10,12},{12... | collective-permute-start | bytes 393224 | tf_op jit(solution)/shard_map/ppermute | solution.py:382
  22.1 0.8 %collective-permute-done.6.refs_3_ = bf16[512,128]{1,0:T(8,128)(2,1)S(1)} collective-permute-done((bf16[512,128]{1,0:T(8,128)(2,1)S(1)}, bf16[512,128]{1,0:T(8,128)(2,1)S(1)}, u32[]{:S(2)}, u32[]{:S(2)}) %collective-permute-start.6) | collective-permute-done | bytes 131104 | tf_op jit(solution)/shard_map/ppermute | solution.py:384
  23.0 0.2 collective-permute-start.7
  23.2 1.8 %collective-permute-start.4 = (bf16[512,128]{1,0:T(8,128)(2,1)S(1)}, bf16[512,128]{1,0:T(8,128)(2,1)S(1)}, u32[]{:S(2)}, u32[]{:S(2)}) collective-permute-start(bf16[512,128]{1,0:T(8,128)(2,1)S(1)} %collective-permute-done.3.refs_0_), channel_id=1, source_target_pairs={{0,2},{2,4},{4,6},{6,7},{7,5},{5,3},{3,1},{1,0},{8,10},{10,12},{12... | collective-permute-start | bytes 393224 | tf_op jit(solution)/shard_map/ppermute | solution.py:392
  25.0 1.3 %spmm.6.refs_4_ = f32[2,4,128,128]{3,2,1,0:T(8,128)S(1)} custom-call(s32[268]{0:T(512)S(1)} %column_table.1.table, bf16[2,4,8,4,128,128]{5,4,3,2,1,0:T(8,128)(2,1)S(1)} %copy-done, bf16[512,128]{1,0:T(8,128)(2,1)S(1)} %collective-permute-done.1.refs_0_, bf16[512,128]{1,0:T(8,128)(2,1)S(1)} %collective-permute-done.8.refs_1_, ...), custom_call_target="tpu_custom_call" | custom-call | flops 1073741824 | bytes 1048576 | tf_op jit(solution)/shard_map/spmm/pallas_call | solution.py:133
  26.4 1.3 %spmm.7.refs_4_ = f32[2,4,128,128]{3,2,1,0:T(8,128)S(1)} custom-call(s32[268]{0:T(512)S(1)} %column_table.1.table, bf16[2,4,8,4,128,128]{5,4,3,2,1,0:T(8,128)(2,1)S(1)} %copy-done, bf16[512,128]{1,0:T(8,128)(2,1)S(1)} %collective-permute-done.3.refs_0_, bf16[512,128]{1,0:T(8,128)(2,1)S(1)} %collective-permute-done.9.refs_1_, ...), custom_call_target="tpu_custom_call" | custom-call | flops 1073741824 | bytes 1048576 | tf_op jit(solution)/shard_map/spmm/pallas_call | solution.py:133
  27.9 0.3 collective-permute-done.4.refs_2_
  28.2 0.4 %spmm_last.1 = (bf16[2,256,128]{2,1,0:T(8,128)(2,1)S(1)}, bf16[2,256,128]{2,1,0:T(8,128)(2,1)S(1)}) custom-call(bf16[512,512]{1,0:T(8,128)(2,1)S(1)} %get-tuple-element.29.refs_0_, bf16[512,512]{1,0:T(8,128)(2,1)S(1)} %get-tuple-element.30.refs_1_, bf16[512,128]{1,0:T(8,128)(2,1)S(1)} %collective-permute-done.4.refs_2_, ...), custom_call_target="tpu_custom_call" | custom-call | flops 134217728 | bytes 1048576 | tf_op jit(solution)/shard_map/spmm_last/pallas_call | solution.py:186
  28.7 1.1 %gates.1.gx_own = f32[2,256,1536]{2,1,0:T(8,128)S(1)} custom-call(bf16[2,256,128]{2,1,0:T(8,128)(2,1)S(1)} %get-tuple-element.35.ax, bf16[128,512]{1,0:T(8,128)(2,1)S(1)} %copy-done.5, bf16[512,1536]{1,0:T(8,128)(2,1)S(1)} %copy-done.1), custom_call_target="tpu_custom_call" | custom-call | flops 1610612736 | bytes 1048576 | tf_op jit(solution)/shard_map/gates/pallas_call | solution.py:214
  30.1 2.1 %recurrence_first.3 = (bf16[128,512]{1,0:T(8,128)(2,1)S(1)}, bf16[2,128,512]{2,1,0:T(8,128)(2,1)S(1)}, bf16[2,128,512]{2,1,0:T(8,128)(2,1)S(1)}, f32[2,128,1536]{2,1,0:T(8,128)S(1)}) custom-call(f32[512,512]{1,0:T(8,128)S(1)} %copy-done.3, f32[2,256,1536]{2,1,0:T(8,128)S(1)} %gates.1.gx_own, bf16[2,256,128]{2,1,0:T(8,128)(2,1)S(1)} %collective-permute-done.12.ax_other, ...), custom_call_target="tpu_custom_call" | custom-call | flops 3221225472 | bytes 1048576 | tf_op jit(solution)/shard_map/recurrence_first/pallas_call | solution.py:273
  32.2 0.3 collective-permute-start.15
  32.5 2.3 %recurrence_first.2 = (bf16[128,512]{1,0:T(8,128)(2,1)S(1)}, bf16[2,128,512]{2,1,0:T(8,128)(2,1)S(1)}, bf16[2,128,512]{2,1,0:T(8,128)(2,1)S(1)}, f32[2,128,1536]{2,1,0:T(8,128)S(1)}) custom-call(f32[512,512]{1,0:T(8,128)S(1)} %copy-done.3, f32[2,256,1536]{2,1,0:T(8,128)S(1)} %gates.1.gx_own, bf16[2,256,128]{2,1,0:T(8,128)(2,1)S(1)} %collective-permute-done.12.ax_other, ...), custom_call_target="tpu_custom_call" | custom-call | flops 3221225472 | bytes 1048576 | tf_op jit(solution)/shard_map/recurrence_first/pallas_call | solution.py:273
  34.8 0.4 collective-permute-start.13
  35.2 3.1 %collective-permute-done.15.state_in = bf16[128,512]{1,0:T(8,128)(2,1)S(1)} collective-permute-done((bf16[128,512]{1,0:T(8,128)(2,1)S(1)}, bf16[128,512]{1,0:T(8,128)(2,1)S(1)}, u32[]{:S(2)}, u32[]{:S(2)}) %collective-permute-start.15) | collective-permute-done | bytes 131104 | tf_op jit(solution)/shard_map/ppermute | solution.py:414
  38.4 2.3 %collective-permute-done.13.state_in = bf16[128,512]{1,0:T(8,128)(2,1)S(1)} collective-permute-done((bf16[128,512]{1,0:T(8,128)(2,1)S(1)}, bf16[128,512]{1,0:T(8,128)(2,1)S(1)}, u32[]{:S(2)}, u32[]{:S(2)}) %collective-permute-start.13) | collective-permute-done | bytes 131104 | tf_op jit(solution)/shard_map/ppermute | solution.py:414
  40.9 0.9 %write_out.2.refs_1_ = bf16[2,512,512]{2,1,0:T(8,128)(2,1)} custom-call(bf16[2,128,512]{2,1,0:T(8,128)(2,1)S(1)} %get-tuple-element.46.refs_0_, bf16[2,128,512]{2,1,0:T(8,128)(2,1)S(1)} %get-tuple-element.47.refs_1_, bf16[2,128,512]{2,1,0:T(8,128)(2,1)S(1)} %collective-permute-done.16.refs_2_), custom_call_target="tpu_custom_call" | custom-call | bytes 1048576 | tf_op jit(solution)/shard_map/write_out/pallas_call | solution.py:342
  41.8 0.6 %collective-permute-done.14.refs_0_ = bf16[2,128,512]{2,1,0:T(8,128)(2,1)S(1)} collective-permute-done((bf16[2,128,512]{2,1,0:T(8,128)(2,1)S(1)}, bf16[2,128,512]{2,1,0:T(8,128)(2,1)S(1)}, u32[]{:S(2)}, u32[]{:S(2)}) %collective-permute-start.14) | collective-permute-done | bytes 262176 | tf_op jit(solution)/shard_map/ppermute | solution.py:423
  42.4 0.7 %write_out.3 = bf16[2,512,512]{2,1,0:T(8,128)(2,1)} custom-call(bf16[2,128,512]{2,1,0:T(8,128)(2,1)S(1)} %collective-permute-done.14.refs_0_, bf16[2,512,512]{2,1,0:T(8,128)(2,1)} %write_out.2.refs_1_), custom_call_target="tpu_custom_call", output_to_operand_aliasing={{}: (1, {})} | custom-call | bytes 1048576 | tf_op jit(solution)/shard_map/write_out/pallas_call | solution.py:342
  (33 shorter events, 1.5 us)
Async XLA Ops:
  0.0 9.5 %collective-permute-start = (bf16[2,512,128]{2,1,0:T(8,128)(2,1)}, bf16[2,512,128]{2,1,0:T(8,128)(2,1)S(1)}, u32[]{:S(2)}, u32[]{:S(2)}) collective-permute-start(bf16[2,512,128]{2,1,0:T(8,128)(2,1)} %refs_0_.2), channel_id=1, source_target_pairs={{0,2},{2,4},{4,6},{6,7},{7,5},{5,3},{3,1},{1,0},{8,10},{10,12},{12... | collective-permute-start | bytes 786440 | tf_op jit(solution)/shard_map/ppermute | solution.py:369
  3.0 8.4 %collective-permute-start.2 = (bf16[2,512,128]{2,1,0:T(8,128)(2,1)}, bf16[2,512,128]{2,1,0:T(8,128)(2,1)S(1)}, u32[]{:S(2)}, u32[]{:S(2)}) collective-permute-start(bf16[2,512,128]{2,1,0:T(8,128)(2,1)} %refs_0_.2), channel_id=1, source_target_pairs={{2,0},{4,2},{6,4},{7,6},{5,7},{3,5},{1,3},{0,1},{10,8},{12,10},{14... | collective-permute-start | bytes 786440 | tf_op jit(solution)/shard_map/ppermute | solution.py:370
  3.8 3.4 %copy-start = (bf16[2,4,8,4,128,128]{5,4,3,2,1,0:T(8,128)(2,1)S(1)}, bf16[2,4,8,4,128,128]{5,4,3,2,1,0:T(8,128)(2,1)}, u32[]{:S(2)}) copy-start(bf16[2,4,8,4,128,128]{5,4,3,2,1,0:T(8,128)(2,1)} %tiles.9) | copy-start | bytes 25165828
  7.1 1.1 %copy-start.4 = (bf16[2,512,128]{2,1,0:T(8,128)(2,1)S(1)}, bf16[2,512,128]{2,1,0:T(8,128)(2,1)}, u32[]{:S(2)}) copy-start(bf16[2,512,128]{2,1,0:T(8,128)(2,1)} %refs_0_.2) | copy-start | bytes 786436
  9.5 5.7 %collective-permute-start.1 = (bf16[512,128]{1,0:T(8,128)(2,1)S(1)}, bf16[512,128]{1,0:T(8,128)(2,1)S(1)}, u32[]{:S(2)}, u32[]{:S(2)}) collective-permute-start(bf16[512,128]{1,0:T(8,128)(2,1)S(1)} %get-tuple-element.52), channel_id=1, source_target_pairs={{0,2},{2,4},{4,6},{6,7},{7,5},{5,3},{3,1},{1,0},{8,10},{10,12},{12... | collective-permute-start | bytes 393224 | tf_op jit(solution)/shard_map/ppermute | solution.py:382
  11.4 5.9 %collective-permute-start.5 = (bf16[512,128]{1,0:T(8,128)(2,1)S(1)}, bf16[512,128]{1,0:T(8,128)(2,1)S(1)}, u32[]{:S(2)}, u32[]{:S(2)}) collective-permute-start(bf16[512,128]{1,0:T(8,128)(2,1)S(1)} %get-tuple-element.50), channel_id=1, source_target_pairs={{2,0},{4,2},{6,4},{7,6},{5,7},{3,5},{1,3},{0,1},{10,8},{12,10},{14... | collective-permute-start | bytes 393224 | tf_op jit(solution)/shard_map/ppermute | solution.py:384
  11.7 8.5 %collective-permute-start.10 = (bf16[512,128]{1,0:T(8,128)(2,1)S(1)}, bf16[512,128]{1,0:T(8,128)(2,1)S(1)}, u32[]{:S(2)}, u32[]{:S(2)}) collective-permute-start(bf16[512,128]{1,0:T(8,128)(2,1)S(1)} %get-tuple-element.49), channel_id=1, source_target_pairs={{2,0},{4,2},{6,4},{7,6},{5,7},{3,5},{1,3},{0,1},{10,8},{12,10},{14... | collective-permute-start | bytes 393224 | tf_op jit(solution)/shard_map/ppermute | solution.py:384
  13.4 6.8 %collective-permute-start.8 = (bf16[512,128]{1,0:T(8,128)(2,1)S(1)}, bf16[512,128]{1,0:T(8,128)(2,1)S(1)}, u32[]{:S(2)}, u32[]{:S(2)}) collective-permute-start(bf16[512,128]{1,0:T(8,128)(2,1)S(1)} %get-tuple-element.51), channel_id=1, source_target_pairs={{0,2},{2,4},{4,6},{6,7},{7,5},{5,3},{3,1},{1,0},{8,10},{10,12},{12... | collective-permute-start | bytes 393224 | tf_op jit(solution)/shard_map/ppermute | solution.py:382
  15.0 11.3 %copy-start.1 = (bf16[512,1536]{1,0:T(8,128)(2,1)S(1)}, bf16[512,1536]{1,0:T(8,128)(2,1)}, u32[]{:S(2)}) copy-start(bf16[512,1536]{1,0:T(8,128)(2,1)} %w_input.3) | copy-start | bytes 4718596
  15.0 11.3 %copy-start.2 = (bf16[512,1536]{1,0:T(8,128)(2,1)S(1)}, bf16[512,1536]{1,0:T(8,128)(2,1)}, u32[]{:S(2)}) copy-start(bf16[512,1536]{1,0:T(8,128)(2,1)} %w_hidden.7) | copy-start | bytes 4718596
  15.0 11.3 %copy-start.3 = (f32[512,512]{1,0:T(8,128)S(1)}, f32[512,512]{1,0:T(8,128)}, u32[]{:S(2)}) copy-start(f32[512,512]{1,0:T(8,128)} %hidden_start.3) | copy-start | bytes 3145732
  15.0 11.3 %copy-start.5 = (bf16[128,512]{1,0:T(8,128)(2,1)S(1)}, bf16[128,512]{1,0:T(8,128)(2,1)}, u32[]{:S(2)}) copy-start(bf16[128,512]{1,0:T(8,128)(2,1)} %w_graph.3) | copy-start | bytes 393220
  17.3 5.7 %collective-permute-start.6 = (bf16[512,128]{1,0:T(8,128)(2,1)S(1)}, bf16[512,128]{1,0:T(8,128)(2,1)S(1)}, u32[]{:S(2)}, u32[]{:S(2)}) collective-permute-start(bf16[512,128]{1,0:T(8,128)(2,1)S(1)} %collective-permute-done.5.refs_3_), channel_id=1, source_target_pairs={{2,0},{4,2},{6,4},{7,6},{5,7},{3,5},{1,3},{0,1},{10,8},{12,10},{14... | collective-permute-start | bytes 393224 | tf_op jit(solution)/shard_map/ppermute | solution.py:384
  17.6 5.7 %collective-permute-start.3 = (bf16[512,128]{1,0:T(8,128)(2,1)S(1)}, bf16[512,128]{1,0:T(8,128)(2,1)S(1)}, u32[]{:S(2)}, u32[]{:S(2)}) collective-permute-start(bf16[512,128]{1,0:T(8,128)(2,1)S(1)} %collective-permute-done.1.refs_0_), channel_id=1, source_target_pairs={{0,2},{2,4},{4,6},{6,7},{7,5},{5,3},{3,1},{1,0},{8,10},{10,12},{12... | collective-permute-start | bytes 393224 | tf_op jit(solution)/shard_map/ppermute | solution.py:382
  20.1 6.2 %collective-permute-start.11 = (bf16[512,128]{1,0:T(8,128)(2,1)S(1)}, bf16[512,128]{1,0:T(8,128)(2,1)S(1)}, u32[]{:S(2)}, u32[]{:S(2)}) collective-permute-start(bf16[512,128]{1,0:T(8,128)(2,1)S(1)} %collective-permute-done.10.refs_2_), channel_id=1, source_target_pairs={{2,0},{4,2},{6,4},{7,6},{5,7},{3,5},{1,3},{0,1},{10,8},{12,10},{14... | collective-permute-start | bytes 393224 | tf_op jit(solution)/shard_map/ppermute | solution.py:384
  20.2 6.1 %collective-permute-start.9 = (bf16[512,128]{1,0:T(8,128)(2,1)S(1)}, bf16[512,128]{1,0:T(8,128)(2,1)S(1)}, u32[]{:S(2)}, u32[]{:S(2)}) collective-permute-start(bf16[512,128]{1,0:T(8,128)(2,1)S(1)} %collective-permute-done.8.refs_1_), channel_id=1, source_target_pairs={{0,2},{2,4},{4,6},{6,7},{7,5},{5,3},{3,1},{1,0},{8,10},{10,12},{12... | collective-permute-start | bytes 393224 | tf_op jit(solution)/shard_map/ppermute | solution.py:382
  23.0 5.0 %collective-permute-start.7 = (bf16[512,128]{1,0:T(8,128)(2,1)S(1)}, bf16[512,128]{1,0:T(8,128)(2,1)S(1)}, u32[]{:S(2)}, u32[]{:S(2)}) collective-permute-start(bf16[512,128]{1,0:T(8,128)(2,1)S(1)} %collective-permute-done.6.refs_3_), channel_id=1, source_target_pairs={{2,0},{4,2},{6,4},{7,6},{5,7},{3,5},{1,3},{0,1},{10,8},{12,10},{14... | collective-permute-start | bytes 393224 | tf_op jit(solution)/shard_map/ppermute | solution.py:392
  23.2 5.0 %collective-permute-start.4 = (bf16[512,128]{1,0:T(8,128)(2,1)S(1)}, bf16[512,128]{1,0:T(8,128)(2,1)S(1)}, u32[]{:S(2)}, u32[]{:S(2)}) collective-permute-start(bf16[512,128]{1,0:T(8,128)(2,1)S(1)} %collective-permute-done.3.refs_0_), channel_id=1, source_target_pairs={{0,2},{2,4},{4,6},{6,7},{7,5},{5,3},{3,1},{1,0},{8,10},{10,12},{12... | collective-permute-start | bytes 393224 | tf_op jit(solution)/shard_map/ppermute | solution.py:392
  28.6 1.4 %collective-permute-start.12 = (bf16[2,256,128]{2,1,0:T(8,128)(2,1)S(1)}, bf16[2,256,128]{2,1,0:T(8,128)(2,1)S(1)}, u32[]{:S(2)}, u32[]{:S(2)}) collective-permute-start(bf16[2,256,128]{2,1,0:T(8,128)(2,1)S(1)} %get-tuple-element.36), channel_id=1, source_target_pairs={{0,8},{8,0},{16,24},{24,16},{1,9},{9,1},{17,25},{25,17},{2,10},{10... | collective-permute-start | bytes 393224 | tf_op jit(solution)/shard_map/ppermute | solution.py:400
  28.7 1.3 %copy-start.6 = (f32[512]{0:T(512)S(1)}, f32[512]{0:T(512)}, u32[]{:S(2)}) copy-start(f32[512]{0:T(512)} %param.17) | copy-start | bytes 6148
  32.2 6.1 %collective-permute-start.15 = (bf16[128,512]{1,0:T(8,128)(2,1)S(1)}, bf16[128,512]{1,0:T(8,128)(2,1)S(1)}, u32[]{:S(2)}, u32[]{:S(2)}) collective-permute-start(bf16[128,512]{1,0:T(8,128)(2,1)S(1)} %get-tuple-element.42), channel_id=1, source_target_pairs={{0,16},{8,24},{16,0},{24,8},{1,17},{9,25},{17,1},{25,9},{2,18},{10... | collective-permute-start | bytes 393224 | tf_op jit(solution)/shard_map/ppermute | solution.py:414
  34.8 6.0 %collective-permute-start.13 = (bf16[128,512]{1,0:T(8,128)(2,1)S(1)}, bf16[128,512]{1,0:T(8,128)(2,1)S(1)}, u32[]{:S(2)}, u32[]{:S(2)}) collective-permute-start(bf16[128,512]{1,0:T(8,128)(2,1)S(1)} %get-tuple-element.37), channel_id=1, source_target_pairs={{0,16},{8,24},{16,0},{24,8},{1,17},{9,25},{17,1},{25,9},{2,18},{10... | collective-permute-start | bytes 393224 | tf_op jit(solution)/shard_map/ppermute | solution.py:414
  38.3 2.5 %collective-permute-start.16 = (bf16[2,128,512]{2,1,0:T(8,128)(2,1)S(1)}, bf16[2,128,512]{2,1,0:T(8,128)(2,1)S(1)}, u32[]{:S(2)}, u32[]{:S(2)}) collective-permute-start(bf16[2,128,512]{2,1,0:T(8,128)(2,1)S(1)} %get-tuple-element.48), channel_id=1, source_target_pairs={{0,8},{8,0},{16,24},{24,16},{1,9},{9,1},{17,25},{25,17},{2,10},{10... | collective-permute-start | bytes 786440 | tf_op jit(solution)/shard_map/ppermute | solution.py:423
  40.8 1.6 %collective-permute-start.14 = (bf16[2,128,512]{2,1,0:T(8,128)(2,1)S(1)}, bf16[2,128,512]{2,1,0:T(8,128)(2,1)S(1)}, u32[]{:S(2)}, u32[]{:S(2)}) collective-permute-start(bf16[2,128,512]{2,1,0:T(8,128)(2,1)S(1)} %get-tuple-element.41), channel_id=1, source_target_pairs={{0,8},{8,0},{16,24},{24,16},{1,9},{9,1},{17,25},{25,17},{2,10},{10... | collective-permute-start | bytes 786440 | tf_op jit(solution)/shard_map/ppermute | solution.py:423
